TPU v7x, 512 devices: a whole 4x4x16 slice. The times are simulated.
512 devices in a mesh: section: 64 (over y, z_hi, x), dp: 8 (over z_lo, core).
Axes of the slice: x: 4, y: 4, z: 16 (z_hi: 4, z_lo: 4; z = z_hi * 4 + z_lo), core: 2. Of those that a mesh axis runs over, the one named last changes fastest.
Arguments:
- x_saved: bfloat16 [4, 256, 16384], P(None, 'dp', 'section'), may hold values from -6 to 6
- side_grad: bfloat16 [4, 256, 16384], P(None, 'dp', 'section'), may hold values from -4 to 4
- plan: int32 [4], replicated, may hold values from 0 to 3, each once
- w_low: bfloat16 [16384, 512], P('section'), may hold values from -0.0625 to 0.0625
- w_delta: bfloat16 [512, 16384], P(None, 'section'), may hold values from -0.25 to 0.25
- w_select: bfloat16 [32, 16384], P(None, 'section'), may hold values from -0.015625 to 0.015625
- decay_rate: float32 [16, 16384], P(None, 'section'), may hold values from 0.1 to 16
- delta_bias: float32 [16384], P('section'), may hold values from -4 to -1
- skip_gain: float32 [16384], P('section'), may hold values from -0.25 to 0.25
Outputs:
- grad_inputs: bfloat16 [4, 256, 16384], P(None, 'dp', 'section')
- grad_low: float32 [16384, 512], P(('section', 'dp'))
- grad_delta: float32 [512, 16384], P('dp', 'section')
- grad_select: float32 [32, 16384], P('dp', 'section')
- grad_rate: float32 [16, 16384], P('dp', 'section')
- grad_bias: float32 [16384], P(('section', 'dp'))
- grad_skip: float32 [16384], P(('section', 'dp'))
Inputs may be any that keep to these rules, and one draw needn't show every extreme that they name: `plan`: each micro-batch appears exactly once.
All inputs are finite; a program needn't handle non-finite values.
Results may differ from a plain program's by a relative error of at most 0.03.
Values may be sent and summed in bfloat16 or wider, within the bound.
No kernel may reach another device: no remote copies, remote signals or barrier semaphores. Data moves between devices by JAX's collectives and lax.ppermute only.
A program may use at most 64 MiB of HBM per device.

v0:
```python
import jax
import jax.numpy as jnp
from jax import lax
from jax.sharding import PartitionSpec as P

LAYERS = 2


def swapped(block, axis, apart):
    count = lax.axis_size(axis)
    route = []
    for low in range(count):
        high = low | 1 << apart
        if high != low and high < count:
            route += [(low, high), (high, low)]
    return lax.ppermute(block, axis, route)


def shifted(block, axis, distance):
    devices = range(lax.axis_size(axis))
    route = [(i - distance, i) for i in devices if i - distance in devices]
    return lax.ppermute(block, axis, route)


def combine(earlier, later_pair):
    return (earlier[0] * later_pair[0], later_pair[0] * earlier[1] + later_pair[1])


def scan_core(x_float, step_size, b_proj, c_proj, rate_table, gain_vector):
    decays = jnp.exp(-step_size[:, None, :] * rate_table[None, :, :])
    driven = b_proj[:, :, None] * (step_size * x_float)[:, None, :]
    _, states = lax.associative_scan(combine, (decays, driven), axis=0)
    return jnp.einsum("lnc,ln->lc", states, c_proj) + gain_vector * x_float


def group_sum(values, members):
    for bit in range(members.bit_length() - 1):
        partner = swapped((values[0], values[1]), "section", bit)
        values = (values[0] + partner[0], values[1] + partner[1])
    return values


def forward_parts(x_rows, w_lowrank, w_proj):
    low_part = jnp.dot(x_rows, w_lowrank, preferred_element_type=jnp.float32)
    sel_part = lax.dot_general(
        x_rows, w_proj, (((1,), (1,)), ((), ())), preferred_element_type=jnp.float32
    )
    return (low_part, sel_part)


def scan_pullback(x_rows, lowrank, selected, grad_out, w_step, rate_table, biases, gain_vector):
    state_count = selected.shape[1] // 2
    pre_act = jnp.dot(lowrank, w_step, preferred_element_type=jnp.float32) + biases
    step_size = jax.nn.softplus(pre_act)
    x_float = x_rows.astype(jnp.float32)
    _, pullback = jax.vjp(
        scan_core,
        x_float,
        step_size,
        selected[:, :state_count],
        selected[:, state_count:],
        rate_table,
        gain_vector,
    )
    grad_core, grad_step, grad_bsel, grad_csel, rate_part, skip_part = pullback(grad_out)
    dpre = grad_step * jax.nn.sigmoid(pre_act)
    dpre_half = dpre.astype(jnp.bfloat16)
    dsel_part = jnp.concatenate([grad_bsel, grad_csel], axis=1)
    dlow_part = lax.dot_general(
        dpre_half, w_step, (((1,), (1,)), ((), ())), preferred_element_type=jnp.float32
    )
    return (grad_core, dpre_half, dlow_part, dsel_part, rate_part, jnp.sum(dpre, axis=0), skip_part)


def weight_terms(x_rows, lowrank, dpre_half, dlow_half, dsel_half):
    contract = (((0,), (0,)), ((), ()))
    low_term = lax.dot_general(x_rows, dlow_half, contract, preferred_element_type=jnp.float32)
    step_term = lax.dot_general(lowrank, dpre_half, contract, preferred_element_type=jnp.float32)
    proj_term = lax.dot_general(dsel_half, x_rows, contract, preferred_element_type=jnp.float32)
    return (low_term, step_term, proj_term)


def per_device(
    x_saved, side_grad, plan, w_low, w_delta, w_select, decay_rate, delta_bias, skip_gain
):
    micro_count, length, channels = x_saved.shape
    rank_count = w_low.shape[1]
    doubled = w_select.shape[0]
    state_count = decay_rate.shape[0]
    layers = LAYERS
    members = lax.axis_size("section") // layers
    layer_index = lax.axis_index("section") // members
    ordered = jnp.take(x_saved, plan, axis=0).reshape(micro_count * length, channels)
    low_all, sel_all = forward_parts(ordered, w_low, w_select)
    low_all, sel_all = group_sum((low_all, sel_all), members)
    lowrank_all = low_all.astype(jnp.bfloat16).reshape(micro_count, length, rank_count)
    selected_all = sel_all.reshape(micro_count, length, doubled)
    results = jnp.zeros((micro_count, length, channels), jnp.bfloat16)
    small_sums = (
        jnp.zeros((state_count, channels), jnp.float32),
        jnp.zeros((channels,), jnp.float32),
        jnp.zeros((channels,), jnp.float32),
    )
    stashed = (
        jnp.zeros((channels, rank_count), jnp.float32),
        jnp.zeros((rank_count, channels), jnp.float32),
        jnp.zeros((doubled, channels), jnp.float32),
    )

    def one_tick(tick_index, carry):
        incoming, results, small_sums, stashed = carry
        slot_index = tick_index - (layers - 1 - layer_index)
        active = jnp.logical_and(slot_index >= 0, slot_index < micro_count)
        safe_slot = jnp.clip(slot_index, 0, micro_count - 1)
        picked = plan[safe_slot]
        x_now = lax.dynamic_index_in_dim(x_saved, picked, 0, keepdims=False)
        side_now = lax.dynamic_index_in_dim(side_grad, picked, 0, keepdims=False)
        grad_out = side_now.astype(jnp.float32) + incoming.astype(jnp.float32)
        lowrank = lax.dynamic_index_in_dim(lowrank_all, safe_slot, 0, keepdims=False)
        selected = lax.dynamic_index_in_dim(selected_all, safe_slot, 0, keepdims=False)

        def pull_active(unused):
            return scan_pullback(
                x_now, lowrank, selected, grad_out, w_delta, decay_rate, delta_bias, skip_gain
            )

        def pull_spare(unused):
            return (
                jnp.zeros((length, channels), jnp.float32),
                jnp.zeros((length, channels), jnp.bfloat16),
                jnp.zeros((length, rank_count), jnp.float32),
                jnp.zeros((length, doubled), jnp.float32),
                jnp.zeros((state_count, channels), jnp.float32),
                jnp.zeros((channels,), jnp.float32),
                jnp.zeros((channels,), jnp.float32),
            )

        pulled = lax.cond(active, pull_active, pull_spare, 0)
        grad_core, dpre_half, dlow_part, dsel_part, rate_part, bias_part, skip_part = pulled
        dlow_sum, dsel_sum = group_sum((dlow_part, dsel_part), members)
        dlow_half = dlow_sum.astype(jnp.bfloat16)
        dsel_half = dsel_sum.astype(jnp.bfloat16)

        def finish_active(carried):
            results, small_sums, stashed = carried
            summed_grad = grad_out + grad_core
            summed_grad = summed_grad + lax.dot_general(
                dlow_half, w_low, (((1,), (1,)), ((), ())), preferred_element_type=jnp.float32
            )
            summed_grad = summed_grad + jnp.dot(
                dsel_half, w_select, preferred_element_type=jnp.float32
            )
            grad_in = summed_grad.astype(jnp.bfloat16)
            results = lax.dynamic_update_index_in_dim(results, grad_in, safe_slot, 0)
            small_sums = (
                small_sums[0] + rate_part,
                small_sums[1] + bias_part,
                small_sums[2] + skip_part,
            )
            terms = weight_terms(x_now, lowrank, dpre_half, dlow_half, dsel_half)
            stashed = tuple((old + new for old, new in zip(stashed, terms)))
            return (grad_in, (results, small_sums, stashed))

        def finish_spare(carried):
            return (jnp.zeros((length, channels), jnp.bfloat16), carried)

        grad_in, carried = lax.cond(
            active, finish_active, finish_spare, (results, small_sums, stashed)
        )
        outgoing = shifted(grad_in, "section", -members)
        return (outgoing,) + carried

    start = (jnp.zeros((length, channels), jnp.bfloat16), results, small_sums, stashed)
    finished = lax.fori_loop(0, layers + micro_count - 1, one_tick, start)
    _, results, small_sums, stashed = finished
    reduced = (
        lax.psum_scatter(
            stashed[0].astype(jnp.bfloat16), "dp", scatter_dimension=0, tiled=True
        ).astype(jnp.float32),
        lax.psum_scatter(
            stashed[1].astype(jnp.bfloat16), "dp", scatter_dimension=0, tiled=True
        ).astype(jnp.float32),
        lax.psum_scatter(
            stashed[2].astype(jnp.bfloat16), "dp", scatter_dimension=0, tiled=True
        ).astype(jnp.float32),
        lax.psum_scatter(
            small_sums[0].astype(jnp.bfloat16), "dp", scatter_dimension=0, tiled=True
        ).astype(jnp.float32),
        lax.psum_scatter(
            small_sums[1].astype(jnp.bfloat16), "dp", scatter_dimension=0, tiled=True
        ).astype(jnp.float32),
        lax.psum_scatter(
            small_sums[2].astype(jnp.bfloat16), "dp", scatter_dimension=0, tiled=True
        ).astype(jnp.float32),
    )
    return (results, reduced[0], reduced[1], reduced[2], reduced[3], reduced[4], reduced[5])


def solution(mesh):
    in_specs = (
        P(None, "dp", "section"),
        P(None, "dp", "section"),
        P(),
        P("section", None),
        P(None, "section"),
        P(None, "section"),
        P(None, "section"),
        P("section"),
        P("section"),
    )
    out_specs = (
        P(None, "dp", "section"),
        P(("section", "dp"), None),
        P("dp", "section"),
        P("dp", "section"),
        P("dp", "section"),
        P(("section", "dp")),
        P(("section", "dp")),
    )
    return jax.shard_map(
        per_device, mesh=mesh, in_specs=in_specs, out_specs=out_specs, check_vma=False
    )
```

profile of v0, /device:TPU:1, one launch (start us, length us, event | category | flops | bytes accessed | tf_op | source)
XLA Modules:
  0.0 890.3 jit_solution(1973928513267787726)
XLA Ops:
  11.3 4.0 collective-permute-start.11
  15.3 3.7 collective-permute-done.11
  19.1 6.8 collective-permute-start.12
  25.9 3.7 collective-permute-done.12
  29.7 10.1 %collective-permute-start.13 = (f32[128,512]{1,0:T(8,128)S(1)}, f32[128,512]{1,0:T(8,128)S(1)}, u32[]{:S(2)}, u32[]{:S(2)}) collective-permute-start(f32[128,512]{1,0:T(8,128)S(1)} %add.381), channel_id=1, source_target_pairs={{0,32},{32,0},{8,40},{40,8},{16,48},{48,16},{24,56},{56,24},{64,96... | collective-permute-start | bytes 786440 | tf_op jit(solution)/shard_map/ppermute | solution.py:16
  39.8 22.2 %collective-permute-done.13 = f32[128,512]{1,0:T(8,128)S(1)} collective-permute-done((f32[128,512]{1,0:T(8,128)S(1)}, f32[128,512]{1,0:T(8,128)S(1)}, u32[]{:S(2)}, u32[]{:S(2)}) %collective-permute-start.13) | collective-permute-done | bytes 262176 | tf_op jit(solution)/shard_map/ppermute | solution.py:16
  62.0 20.4 %collective-permute-start.14 = (f32[128,512]{1,0:T(8,128)S(1)}, f32[128,512]{1,0:T(8,128)S(1)}, u32[]{:S(2)}, u32[]{:S(2)}) collective-permute-start(f32[128,512]{1,0:T(8,128)S(1)} %add.382), channel_id=1, source_target_pairs={{0,64},{64,0},{8,72},{72,8},{16,80},{80,16},{24,88},{88,24},{32,96... | collective-permute-start | bytes 786440 | tf_op jit(solution)/shard_map/ppermute | solution.py:16
  82.4 17.2 %collective-permute-done.14 = f32[128,512]{1,0:T(8,128)S(1)} collective-permute-done((f32[128,512]{1,0:T(8,128)S(1)}, f32[128,512]{1,0:T(8,128)S(1)}, u32[]{:S(2)}, u32[]{:S(2)}) %collective-permute-start.14) | collective-permute-done | bytes 262176 | tf_op jit(solution)/shard_map/ppermute | solution.py:16
  107.9 4.7 collective-permute-start.17
  115.8 6.5 collective-permute-done.18
  122.2 5.4 collective-permute-start.19
  127.6 7.8 collective-permute-done.19
  146.8 600.5 %while.29 = (s32[]{:T(128)}, bf16[32,256]{1,0:T(8,128)(2,1)}, bf16[4,32,256]{2,1,0:T(8,128)(2,1)}, f32[16,256]{1,0:T(8,128)}, f32[256]{0:T(256)}, /*index=5*/f32...) while((s32[]{:T(128)}, bf16[32,256]{1,0:T(8,128)(2,1)}, ...), condition=%wide.region_11.12_spmd, body=%wide.region_0.11_spmd.sunk | while | flops 48966160 | bytes 66561068 | solution.py:174
  161.2 4.8 collective-permute-start.1
  169.8 7.1 collective-permute-done.2
  176.9 5.3 collective-permute-start.3
  182.2 3.6 collective-permute-start.5
  187.0 4.4 collective-permute-start.6
  194.9 6.5 collective-permute-done.7
  201.3 9.4 %collective-permute-start.8 = (f32[32,32]{1,0:T(8,128)S(1)}, f32[32,32]{1,0:T(8,128)S(1)}, u32[]{:S(2)}, u32[]{:S(2)}) collective-permute-start(f32[32,32]{1,0:T(8,128)S(1)} %add.484), channel_id=1, source_target_pairs={{0,64},{64,0},{8,72},{72,8},{16,80},{80,16},{24,88},{88,24},{32,96... | collective-permute-start | bytes 12296 | tf_op jit(solution)/shard_map/while/body/eval_jaxpr/ppermute | solution.py:16
  210.7 3.8 collective-permute-done.8
  223.7 41.1 %collective-permute-done.10 = bf16[32,256]{1,0:T(8,128)(2,1)} collective-permute-done((bf16[32,256]{1,0:T(8,128)(2,1)S(1)}, bf16[32,256]{1,0:T(8,128)(2,1)}, u32[]{:S(2)}, u32[]{:S(2)}) %collective-permute-start.10) | collective-permute-done | bytes 16416 | tf_op jit(solution)/shard_map/while/body/eval_jaxpr/ppermute | solution.py:22
  271.0 34.4 %conditional.4 = (f32[32,256]{1,0:T(8,128)S(1)}, bf16[32,256]{1,0:T(8,128)(2,1)S(1)}, f32[32,512]{1,0:T(8,128)S(1)}, f32[32,32]{1,0:T(8,128)S(1)}, f32[16,256]{1,0:T(8,128)}, /*index=5*/f32[256]{0:T(256)}, f32[256]{0:T(256)}) conditional(s32[]{:T(128)} %convert_element_type.139, () %tuple.108, (f32[256]{0:T(256)}, f32[32,256]{1,0:T(8,128)S(1)}, ...), branch_computations={%region_1.1_spmd, %region_2.8_spmd} | conditional | flops 22315008 | bytes 50965668 | solution.py:138
  286.3 5.9 pad.222
  292.3 5.8 pad.221
  311.9 4.1 collective-permute-start.1
  320.5 7.0 collective-permute-done.2
  327.5 9.3 %collective-permute-start.3 = (f32[32,512]{1,0:T(8,128)S(1)}, f32[32,512]{1,0:T(8,128)S(1)}, u32[]{:S(2)}, u32[]{:S(2)}) collective-permute-start(f32[32,512]{1,0:T(8,128)S(1)} %add.480), channel_id=1, source_target_pairs={{0,64},{64,0},{8,72},{72,8},{16,80},{80,16},{24,88},{88,24},{32,96... | collective-permute-start | bytes 196616 | tf_op jit(solution)/shard_map/while/body/eval_jaxpr/ppermute | solution.py:16
  350.1 5.5 collective-permute-done.7
  355.7 4.7 collective-permute-start.8
  360.4 8.5 collective-permute-done.8
  377.5 3.7 conditional.5
  382.5 4.8 collective-permute-done.10
  393.4 34.4 %conditional.4 = (f32[32,256]{1,0:T(8,128)S(1)}, bf16[32,256]{1,0:T(8,128)(2,1)S(1)}, f32[32,512]{1,0:T(8,128)S(1)}, f32[32,32]{1,0:T(8,128)S(1)}, f32[16,256]{1,0:T(8,128)}, /*index=5*/f32[256]{0:T(256)}, f32[256]{0:T(256)}) conditional(s32[]{:T(128)} %convert_element_type.139, () %tuple.108, (f32[256]{0:T(256)}, f32[32,256]{1,0:T(8,128)S(1)}, ...), branch_computations={%region_1.1_spmd, %region_2.8_spmd} | conditional | flops 22315008 | bytes 50965668 | solution.py:138
  408.8 5.9 pad.222
  414.8 5.8 pad.221
  444.6 5.9 collective-permute-done.2
  450.5 4.1 collective-permute-start.3
  467.5 6.5 collective-permute-done.7
  474.0 10.0 %collective-permute-start.8 = (f32[32,32]{1,0:T(8,128)S(1)}, f32[32,32]{1,0:T(8,128)S(1)}, u32[]{:S(2)}, u32[]{:S(2)}) collective-permute-start(f32[32,32]{1,0:T(8,128)S(1)} %add.484), channel_id=1, source_target_pairs={{0,64},{64,0},{8,72},{72,8},{16,80},{80,16},{24,88},{88,24},{32,96... | collective-permute-start | bytes 12296 | tf_op jit(solution)/shard_map/while/body/eval_jaxpr/ppermute | solution.py:16
  484.0 4.1 collective-permute-done.8
  496.9 3.8 conditional.5
  502.0 5.0 collective-permute-done.10
  513.1 34.4 %conditional.4 = (f32[32,256]{1,0:T(8,128)S(1)}, bf16[32,256]{1,0:T(8,128)(2,1)S(1)}, f32[32,512]{1,0:T(8,128)S(1)}, f32[32,32]{1,0:T(8,128)S(1)}, f32[16,256]{1,0:T(8,128)}, /*index=5*/f32[256]{0:T(256)}, f32[256]{0:T(256)}) conditional(s32[]{:T(128)} %convert_element_type.139, () %tuple.108, (f32[256]{0:T(256)}, f32[32,256]{1,0:T(8,128)S(1)}, ...), branch_computations={%region_1.1_spmd, %region_2.8_spmd} | conditional | flops 22315008 | bytes 50965668 | solution.py:138
  528.4 5.9 pad.222
  534.4 5.8 pad.221
  556.2 4.5 collective-permute-done.1
  562.6 7.0 collective-permute-done.2
  569.7 10.2 %collective-permute-start.3 = (f32[32,512]{1,0:T(8,128)S(1)}, f32[32,512]{1,0:T(8,128)S(1)}, u32[]{:S(2)}, u32[]{:S(2)}) collective-permute-start(f32[32,512]{1,0:T(8,128)S(1)} %add.480), channel_id=1, source_target_pairs={{0,64},{64,0},{8,72},{72,8},{16,80},{80,16},{24,88},{88,24},{32,96... | collective-permute-start | bytes 196616 | tf_op jit(solution)/shard_map/while/body/eval_jaxpr/ppermute | solution.py:16
  592.5 6.2 collective-permute-done.7
  598.7 3.8 collective-permute-start.8
  602.5 9.4 %collective-permute-done.8 = f32[32,32]{1,0:T(8,128)S(1)} collective-permute-done((f32[32,32]{1,0:T(8,128)S(1)}, f32[32,32]{1,0:T(8,128)S(1)}, u32[]{:S(2)}, u32[]{:S(2)}) %collective-permute-start.8) | collective-permute-done | bytes 4128 | tf_op jit(solution)/shard_map/while/body/eval_jaxpr/ppermute | solution.py:16
  620.4 3.8 conditional.5
  625.5 4.8 collective-permute-done.10
  636.4 34.4 %conditional.4 = (f32[32,256]{1,0:T(8,128)S(1)}, bf16[32,256]{1,0:T(8,128)(2,1)S(1)}, f32[32,512]{1,0:T(8,128)S(1)}, f32[32,32]{1,0:T(8,128)S(1)}, f32[16,256]{1,0:T(8,128)}, /*index=5*/f32[256]{0:T(256)}, f32[256]{0:T(256)}) conditional(s32[]{:T(128)} %convert_element_type.139, () %tuple.108, (f32[256]{0:T(256)}, f32[32,256]{1,0:T(8,128)S(1)}, ...), branch_computations={%region_1.1_spmd, %region_2.8_spmd} | conditional | flops 22315008 | bytes 50965668 | solution.py:138
  651.7 5.9 pad.222
  657.7 5.8 pad.221
  686.0 7.6 collective-permute-done.2
  709.4 6.0 collective-permute-done.7
  715.4 11.1 %collective-permute-start.8 = (f32[32,32]{1,0:T(8,128)S(1)}, f32[32,32]{1,0:T(8,128)S(1)}, u32[]{:S(2)}, u32[]{:S(2)}) collective-permute-start(f32[32,32]{1,0:T(8,128)S(1)} %add.484), channel_id=1, source_target_pairs={{0,64},{64,0},{8,72},{72,8},{16,80},{80,16},{24,88},{88,24},{32,96... | collective-permute-start | bytes 12296 | tf_op jit(solution)/shard_map/while/body/eval_jaxpr/ppermute | solution.py:16
  737.5 3.7 conditional.5
  742.5 4.8 collective-permute-done.10
  755.4 79.6 %all-reduce.49 = (bf16[32,256]{1,0:T(8,128)(2,1)S(1)}, bf16[16,256]{1,0:T(8,128)(2,1)S(1)}, bf16[256]{0:T(256)(128)(2,1)S(1)}, bf16[256]{0:T(256)(128)(2,1)S(1)}) all-reduce(bf16[32,256]{1,0:T(8,128)(2,1)S(1)} %convert_element_type.104, ...), channel_id=4, replica_groups=mesh['section'=64,'dp'=8] {'dp'}, use_global_device_ids=true, to_apply=%region_14.15.clone | all-reduce | flops 12800 | bytes 51200
  841.0 41.1 %reduce-scatter.5.cloned.1.call-done = bf16[64,256]{1,0:T(8,128)(2,1)} async-done(((bf16[512,256]{1,0:T(8,128)(2,1)}), bf16[64,256]{1,0:T(8,128)(2,1)}) %reduce-scatter.5.cloned.1.call-update) | async-done | bytes 32784 | tf_op jit(solution)/shard_map/reduce_scatter | solution.py:180
  (1142 shorter events, 340.7 us)
Async XLA Ops:
  7.2 832.4 %reduce-scatter.3.cloned.1.call-start = ((), (), s32[]{:S(2)}) async-start(), calls=%async_computation.2 | async-start | bytes 294912 | tf_op jit(solution)/shard_map/reduce_scatter | solution.py:177
  11.3 7.7 collective-permute-start.11
  19.1 10.6 %collective-permute-start.12 = (f32[128,512]{1,0:T(8,128)S(1)}, f32[128,512]{1,0:T(8,128)S(1)}, u32[]{:S(2)}, u32[]{:S(2)}) collective-permute-start(f32[128,512]{1,0:T(8,128)S(1)} %add.380), channel_id=1, source_target_pairs={{0,16},{16,0},{8,24},{24,8},{32,48},{48,32},{40,56},{56,40},{64,80... | collective-permute-start | bytes 786440 | tf_op jit(solution)/shard_map/ppermute | solution.py:16
  29.7 32.3 %collective-permute-start.13 = (f32[128,512]{1,0:T(8,128)S(1)}, f32[128,512]{1,0:T(8,128)S(1)}, u32[]{:S(2)}, u32[]{:S(2)}) collective-permute-start(f32[128,512]{1,0:T(8,128)S(1)} %add.381), channel_id=1, source_target_pairs={{0,32},{32,0},{8,40},{40,8},{16,48},{48,16},{24,56},{56,24},{64,96... | collective-permute-start | bytes 786440 | tf_op jit(solution)/shard_map/ppermute | solution.py:16
  62.0 37.7 %collective-permute-start.14 = (f32[128,512]{1,0:T(8,128)S(1)}, f32[128,512]{1,0:T(8,128)S(1)}, u32[]{:S(2)}, u32[]{:S(2)}) collective-permute-start(f32[128,512]{1,0:T(8,128)S(1)} %add.382), channel_id=1, source_target_pairs={{0,64},{64,0},{8,72},{72,8},{16,80},{80,16},{24,88},{88,24},{32,96... | collective-permute-start | bytes 786440 | tf_op jit(solution)/shard_map/ppermute | solution.py:16
  99.7 41.2 %collective-permute-start.15 = (f32[128,512]{1,0:T(8,128)S(1)}, f32[128,512]{1,0:T(8,128)S(1)}, u32[]{:S(2)}, u32[]{:S(2)}) collective-permute-start(f32[128,512]{1,0:T(8,128)S(1)} %add.383), channel_id=1, source_target_pairs={{0,128},{128,0},{8,136},{136,8},{16,144},{144,16},{24,152},{152,24... | collective-permute-start | bytes 786440 | tf_op jit(solution)/shard_map/ppermute | solution.py:16
  103.1 4.8 collective-permute-start.16
  107.9 6.0 collective-permute-start.17
  113.8 8.4 collective-permute-start.18
  122.2 13.2 %collective-permute-start.19 = (f32[128,32]{0,1:T(8,128)S(1)}, f32[128,32]{0,1:T(8,128)S(1)}, u32[]{:S(2)}, u32[]{:S(2)}) collective-permute-start(f32[128,32]{0,1:T(8,128)S(1)} %add.387), channel_id=1, source_target_pairs={{0,64},{64,0},{8,72},{72,8},{16,80},{80,16},{24,88},{88,24},{32,96... | collective-permute-start | bytes 49160 | tf_op jit(solution)/shard_map/ppermute | solution.py:16
  135.4 4.7 collective-permute-start.20
  155.3 5.0 collective-permute-start
  161.2 6.6 collective-permute-start.1
  167.9 9.0 %collective-permute-start.2 = (f32[32,512]{1,0:T(8,128)S(1)}, f32[32,512]{1,0:T(8,128)S(1)}, u32[]{:S(2)}, u32[]{:S(2)}) collective-permute-start(f32[32,512]{1,0:T(8,128)S(1)} %add.479), channel_id=1, source_target_pairs={{0,32},{32,0},{8,40},{40,8},{16,48},{48,16},{24,56},{56,24},{64,96... | collective-permute-start | bytes 196616 | tf_op jit(solution)/shard_map/while/body/eval_jaxpr/ppermute | solution.py:16
  176.9 39.7 %collective-permute-start.3 = (f32[32,512]{1,0:T(8,128)S(1)}, f32[32,512]{1,0:T(8,128)S(1)}, u32[]{:S(2)}, u32[]{:S(2)}) collective-permute-start(f32[32,512]{1,0:T(8,128)S(1)} %add.480), channel_id=1, source_target_pairs={{0,64},{64,0},{8,72},{72,8},{16,80},{80,16},{24,88},{88,24},{32,96... | collective-permute-start | bytes 196616 | tf_op jit(solution)/shard_map/while/body/eval_jaxpr/ppermute | solution.py:16
  182.2 4.8 collective-permute-start.5
  187.0 6.0 collective-permute-start.6
  193.0 8.4 collective-permute-start.7
  201.3 13.2 %collective-permute-start.8 = (f32[32,32]{1,0:T(8,128)S(1)}, f32[32,32]{1,0:T(8,128)S(1)}, u32[]{:S(2)}, u32[]{:S(2)}) collective-permute-start(f32[32,32]{1,0:T(8,128)S(1)} %add.484), channel_id=1, source_target_pairs={{0,64},{64,0},{8,72},{72,8},{16,80},{80,16},{24,88},{88,24},{32,96... | collective-permute-start | bytes 12296 | tf_op jit(solution)/shard_map/while/body/eval_jaxpr/ppermute | solution.py:16
  214.5 5.3 collective-permute-start.9
  216.6 5.0 collective-permute-start.4
  222.4 42.4 %collective-permute-start.10 = (bf16[32,256]{1,0:T(8,128)(2,1)S(1)}, bf16[32,256]{1,0:T(8,128)(2,1)}, u32[]{:S(2)}, u32[]{:S(2)}) collective-permute-start(bf16[32,256]{1,0:T(8,128)(2,1)S(1)} %get-tuple-element.987), channel_id=1, source_target_pairs={{256,0},{264,8},{272,16},{280,24},{288,32},{296,40},{304,48},{312,... | collective-permute-start | bytes 49160 | tf_op jit(solution)/shard_map/while/body/eval_jaxpr/ppermute | solution.py:22
  306.0 5.0 collective-permute-start
  311.9 6.6 collective-permute-start.1
  318.6 8.9 %collective-permute-start.2 = (f32[32,512]{1,0:T(8,128)S(1)}, f32[32,512]{1,0:T(8,128)S(1)}, u32[]{:S(2)}, u32[]{:S(2)}) collective-permute-start(f32[32,512]{1,0:T(8,128)S(1)} %add.479), channel_id=1, source_target_pairs={{0,32},{32,0},{8,40},{40,8},{16,48},{48,16},{24,56},{56,24},{64,96... | collective-permute-start | bytes 196616 | tf_op jit(solution)/shard_map/while/body/eval_jaxpr/ppermute | solution.py:16
  327.5 43.9 %collective-permute-start.3 = (f32[32,512]{1,0:T(8,128)S(1)}, f32[32,512]{1,0:T(8,128)S(1)}, u32[]{:S(2)}, u32[]{:S(2)}) collective-permute-start(f32[32,512]{1,0:T(8,128)S(1)} %add.480), channel_id=1, source_target_pairs={{0,64},{64,0},{8,72},{72,8},{16,80},{80,16},{24,88},{88,24},{32,96... | collective-permute-start | bytes 196616 | tf_op jit(solution)/shard_map/while/body/eval_jaxpr/ppermute | solution.py:16
  341.3 6.0 collective-permute-start.6
  347.3 8.4 collective-permute-start.7
  355.7 13.2 %collective-permute-start.8 = (f32[32,32]{1,0:T(8,128)S(1)}, f32[32,32]{1,0:T(8,128)S(1)}, u32[]{:S(2)}, u32[]{:S(2)}) collective-permute-start(f32[32,32]{1,0:T(8,128)S(1)} %add.484), channel_id=1, source_target_pairs={{0,64},{64,0},{8,72},{72,8},{16,80},{80,16},{24,88},{88,24},{32,96... | collective-permute-start | bytes 12296 | tf_op jit(solution)/shard_map/while/body/eval_jaxpr/ppermute | solution.py:16
  368.9 5.3 collective-permute-start.9
  371.5 5.3 collective-permute-start.4
  381.2 6.1 collective-permute-start.10
  428.5 5.0 collective-permute-start
  434.4 6.6 collective-permute-start.1
  441.1 9.5 %collective-permute-start.2 = (f32[32,512]{1,0:T(8,128)S(1)}, f32[32,512]{1,0:T(8,128)S(1)}, u32[]{:S(2)}, u32[]{:S(2)}) collective-permute-start(f32[32,512]{1,0:T(8,128)S(1)} %add.479), channel_id=1, source_target_pairs={{0,32},{32,0},{8,40},{40,8},{16,48},{48,16},{24,56},{56,24},{64,96... | collective-permute-start | bytes 196616 | tf_op jit(solution)/shard_map/while/body/eval_jaxpr/ppermute | solution.py:16
  450.5 40.7 %collective-permute-start.3 = (f32[32,512]{1,0:T(8,128)S(1)}, f32[32,512]{1,0:T(8,128)S(1)}, u32[]{:S(2)}, u32[]{:S(2)}) collective-permute-start(f32[32,512]{1,0:T(8,128)S(1)} %add.480), channel_id=1, source_target_pairs={{0,64},{64,0},{8,72},{72,8},{16,80},{80,16},{24,88},{88,24},{32,96... | collective-permute-start | bytes 196616 | tf_op jit(solution)/shard_map/while/body/eval_jaxpr/ppermute | solution.py:16
  454.7 4.9 collective-permute-start.5
  459.6 6.0 collective-permute-start.6
  465.6 8.4 collective-permute-start.7
  474.0 14.1 %collective-permute-start.8 = (f32[32,32]{1,0:T(8,128)S(1)}, f32[32,32]{1,0:T(8,128)S(1)}, u32[]{:S(2)}, u32[]{:S(2)}) collective-permute-start(f32[32,32]{1,0:T(8,128)S(1)} %add.484), channel_id=1, source_target_pairs={{0,64},{64,0},{8,72},{72,8},{16,80},{80,16},{24,88},{88,24},{32,96... | collective-permute-start | bytes 12296 | tf_op jit(solution)/shard_map/while/body/eval_jaxpr/ppermute | solution.py:16
  488.1 5.3 collective-permute-start.9
  491.2 5.0 collective-permute-start.4
  500.7 6.3 collective-permute-start.10
  548.1 5.0 collective-permute-start
  554.1 6.6 collective-permute-start.1
  560.7 8.9 %collective-permute-start.2 = (f32[32,512]{1,0:T(8,128)S(1)}, f32[32,512]{1,0:T(8,128)S(1)}, u32[]{:S(2)}, u32[]{:S(2)}) collective-permute-start(f32[32,512]{1,0:T(8,128)S(1)} %add.479), channel_id=1, source_target_pairs={{0,32},{32,0},{8,40},{40,8},{16,48},{48,16},{24,56},{56,24},{64,96... | collective-permute-start | bytes 196616 | tf_op jit(solution)/shard_map/while/body/eval_jaxpr/ppermute | solution.py:16
  569.7 44.7 %collective-permute-start.3 = (f32[32,512]{1,0:T(8,128)S(1)}, f32[32,512]{1,0:T(8,128)S(1)}, u32[]{:S(2)}, u32[]{:S(2)}) collective-permute-start(f32[32,512]{1,0:T(8,128)S(1)} %add.480), channel_id=1, source_target_pairs={{0,64},{64,0},{8,72},{72,8},{16,80},{80,16},{24,88},{88,24},{32,96... | collective-permute-start | bytes 196616 | tf_op jit(solution)/shard_map/while/body/eval_jaxpr/ppermute | solution.py:16
  584.3 6.0 collective-permute-start.6
  590.3 8.4 collective-permute-start.7
  598.7 13.2 %collective-permute-start.8 = (f32[32,32]{1,0:T(8,128)S(1)}, f32[32,32]{1,0:T(8,128)S(1)}, u32[]{:S(2)}, u32[]{:S(2)}) collective-permute-start(f32[32,32]{1,0:T(8,128)S(1)} %add.484), channel_id=1, source_target_pairs={{0,64},{64,0},{8,72},{72,8},{16,80},{80,16},{24,88},{88,24},{32,96... | collective-permute-start | bytes 12296 | tf_op jit(solution)/shard_map/while/body/eval_jaxpr/ppermute | solution.py:16
  611.9 5.3 collective-permute-start.9
  614.4 5.3 collective-permute-start.4
  624.2 6.1 collective-permute-start.10
  671.4 5.0 collective-permute-start
  677.4 6.6 collective-permute-start.1
  684.0 9.6 %collective-permute-start.2 = (f32[32,512]{1,0:T(8,128)S(1)}, f32[32,512]{1,0:T(8,128)S(1)}, u32[]{:S(2)}, u32[]{:S(2)}) collective-permute-start(f32[32,512]{1,0:T(8,128)S(1)} %add.479), channel_id=1, source_target_pairs={{0,32},{32,0},{8,40},{40,8},{16,48},{48,16},{24,56},{56,24},{64,96... | collective-permute-start | bytes 196616 | tf_op jit(solution)/shard_map/while/body/eval_jaxpr/ppermute | solution.py:16
  693.6 38.1 %collective-permute-start.3 = (f32[32,512]{1,0:T(8,128)S(1)}, f32[32,512]{1,0:T(8,128)S(1)}, u32[]{:S(2)}, u32[]{:S(2)}) collective-permute-start(f32[32,512]{1,0:T(8,128)S(1)} %add.480), channel_id=1, source_target_pairs={{0,64},{64,0},{8,72},{72,8},{16,80},{80,16},{24,88},{88,24},{32,96... | collective-permute-start | bytes 196616 | tf_op jit(solution)/shard_map/while/body/eval_jaxpr/ppermute | solution.py:16
  701.0 6.0 collective-permute-start.6
  707.0 8.4 collective-permute-start.7
  715.4 13.2 %collective-permute-start.8 = (f32[32,32]{1,0:T(8,128)S(1)}, f32[32,32]{1,0:T(8,128)S(1)}, u32[]{:S(2)}, u32[]{:S(2)}) collective-permute-start(f32[32,32]{1,0:T(8,128)S(1)} %add.484), channel_id=1, source_target_pairs={{0,64},{64,0},{8,72},{72,8},{16,80},{80,16},{24,88},{88,24},{32,96... | collective-permute-start | bytes 12296 | tf_op jit(solution)/shard_map/while/body/eval_jaxpr/ppermute | solution.py:16
  728.6 5.3 collective-permute-start.9
  731.8 5.0 collective-permute-start.4
  741.2 6.1 collective-permute-start.10
  749.2 132.8 %reduce-scatter.5.cloned.1.call-start = ((), (), s32[]{:S(2)}) async-start(), calls=%async_computation.3 | async-start | bytes 294912 | tf_op jit(solution)/shard_map/reduce_scatter | solution.py:180
  (285 other events, 1525.4 us)
Sparse Core Ops, SparseCore 0:
  749.4 90.1 reduce-scatter.2
  842.6 39.4 reduce-scatter.4
where the time goes:
time: 902 us; the launch traced here: 890 us
  waiting for transfers between devices  322 us (36%)
  starting transfers between devices  253 us (28%)
  local copies, waits for them, and re-layouts  134 us (15%)
  blocking collectives  79.6 us (9%)
  other arithmetic  48.1 us (5%)
  matrix products  22.5 us (2%)
  between operations  16.2 us (2%)
  loops' own time  14.7 us (2%)
    ppermute x60, starting transfers between devices, swapped(): return lax.ppermute(block, axis, route)  247 us
    ppermute x60, waiting for transfers between devices, swapped(): return lax.ppermute(block, axis, route)  218 us
    unnamed x1, blocking collectives  79.6 us
    ppermute x5, waiting for transfers between devices, shifted(): return lax.ppermute(block, axis, route)  60.5 us
    pad x136, local copies, waits for them, and re-layouts, scan_core(): _, states = lax.associative_scan(combine, (decays, driven), axis=0)  54.7 us
    reduce_scatter x1, waiting for transfers between devices, per_device(): lax.psum_scatter(stashed[1].astype(jnp.bfloat16), 'dp', scatter_dimension...  41.1 us
    cond x296, local copies, waits for them, and re-layouts  36.8 us
  transfers between devices with their start and end apart: 67, of which 56 were waited for; matrix products, arithmetic and copies ran while one was open for 1% of the time, Pallas kernels for 0%

commit v1 on v0

v1 whole, which is shorter than its diff:
```python
import functools

import jax
import jax.numpy as jnp
import numpy as np
from jax import lax
from jax.experimental import pallas as pl
from jax.experimental.pallas import tpu as pltpu
from jax.sharding import Mesh
from jax.sharding import PartitionSpec as P

F32, BF16 = jnp.float32, jnp.bfloat16
LAYERS = 2
WIDTH = 640
NN = (((1,), (0,)), ((), ()))
NT = (((1,), (1,)), ((), ()))
TN = (((0,), (0,)), ((), ()))
NEAR = ("yl", "x")
BOTH = ("ly", "yl", "x")
REPLICAS = ("zl", "core")
VMEM_LIMIT = 48 * 1024 * 1024


def dot(a, b, dims=NN):
    return lax.dot_general(a, b, dims, preferred_element_type=F32)


def iota(shape, dim):
    return lax.broadcasted_iota(jnp.int32, shape, dim)


def one_hot(mask):
    return jnp.where(mask, 1.0, 0.0).astype(BF16)


def spread_matrix(micro, length):
    shape = (2 * micro * length, micro * length)
    r, c = iota(shape, 0), iota(shape, 1)
    return one_hot((r % micro) * length + r // (2 * micro) == c)


def gather_matrix(micro, length, order=None):
    shape = (micro * length, 2 * micro * length)
    r, c = iota(shape, 0), iota(shape, 1)
    which = r // length
    if order is not None:
        slot, which = which, jnp.zeros(shape, jnp.int32)
        for j in range(micro):
            which = jnp.where(slot == j, order[j], which)
    return one_hot(which * length + r % length == (c % micro) * length + c // (2 * micro))


def first_half(rows, micro, lanes=128):
    return (iota((rows, lanes), 0) // micro) % 2 == 0


def pick_half(half, wide):
    return jnp.where(half, wide[:, :128], wide[:, 128:])


def two_halves(half, value):
    return jnp.concatenate([jnp.where(half, value, 0.0), jnp.where(half, 0.0, value)], axis=1)


def two_terms(value):
    high = value.astype(BF16)
    return high, (value - high.astype(F32)).astype(BF16)


def project_kernel(x_ref, wl_ref, ws_ref, out_ref):
    rank, doubled = wl_ref.shape[1], ws_ref.shape[0]
    x = x_ref[...]
    out_ref[:, :rank] = dot(x, wl_ref[...]).astype(BF16)
    out_ref[:, rank:] = jnp.zeros((x.shape[0], WIDTH - rank), BF16)
    out_ref[:, rank:rank + doubled] = dot(x, ws_ref[...], NT).astype(BF16)


def tick_kernel(micro, length, states, rank, from_above, *refs):
    x_ref, side_ref, cat_ref, wd_ref, rate_ref, bias_ref, skip_ref, *refs = refs
    if from_above:
        up_cat_ref, up_core_ref, up_low_ref, up_sel_ref, *refs = refs
        send_ref, core_ref, dpre_ref, rate_out, bias_out, skip_out, *refs = refs
    else:
        send_ref, core_ref, *refs = refs
    A, H, Bv, Cv, R, D, DX, X, G, SG, DP = refs
    rows = 2 * micro * length
    doubled = 2 * states
    half = first_half(rows, micro)
    T = spread_matrix(micro, length)
    slabs = (length, 2 * micro, 128)

    def tile(row):
        return pick_half(first_half(2 * micro, micro), row)

    x8 = pick_half(half, dot(T, x_ref[...])).reshape(slabs)
    g8 = pick_half(half, dot(T, side_ref[...]))
    if from_above:
        up = dot(T, up_cat_ref[...]).astype(BF16)
        wide = dot(up[:, :rank], up_low_ref[...], NT) + dot(up[:, rank:rank + doubled], up_sel_ref[...])
        incoming = up_core_ref[...].reshape(rows, 128) + pick_half(half, wide)
        g8 = g8 + incoming.astype(BF16).astype(F32)
    cat8 = dot(T, cat_ref[...]).astype(BF16)
    pre8 = pick_half(half, dot(cat8[:, :rank], wd_ref[...])).reshape(slabs) + tile(bias_ref[...])[None]
    step8 = jax.nn.softplus(pre8)
    X[...] = x8
    G[...] = g8.reshape(slabs)
    D[...] = step8
    DX[...] = step8 * x8
    SG[...] = jax.nn.sigmoid(pre8)
    for n in range(states):
        R[n] = tile(rate_ref[n:n + 1, :])
    wide_shape = (2 * doubled, states * 128)
    lane, row = iota(wide_shape, 1) // 128, iota(wide_shape, 0) % doubled
    terms = cat8[:, rank:rank + 2 * doubled]
    Bv[...] = dot(terms, one_hot(lane == row)).reshape(length, 2 * micro, states * 128)
    Cv[...] = dot(terms, one_hot(lane + states == row)).reshape(length, 2 * micro, states * 128)

    zero = jnp.zeros((2 * micro, 128), F32)
    for n in range(states):
        H[0, n] = zero

    def forward(t, h):
        d, dx = D[t], DX[t]
        out = []
        for n in range(states):
            a = jnp.exp(-(d * R[n]))
            h_n = a * h[n] + dx * Bv[t, :, n * 128:(n + 1) * 128]
            A[t, n] = a
            H[t + 1, n] = h_n
            out.append(h_n)
        return tuple(out)

    lax.fori_loop(0, length, forward, (zero,) * states)
    skip8 = tile(skip_ref[...])

    def backward(i, carry):
        later, acc, bias_acc, skip_acc = carry
        t = length - 1 - i
        d, dx, g, xv = D[t], DX[t], G[t], X[t]
        u, w = [zero, zero], [zero, zero]
        passed, sums = [], []
        for n in range(states):
            at = slice(n * 128, (n + 1) * 128)
            lam = Cv[t, :, at] * g + later[n]
            u[n % 2] = u[n % 2] + lam * Bv[t, :, at]
            Cv[t, :, at] = g * H[t + 1, n]
            Bv[t, :, at] = lam * dx
            back = A[t, n] * lam
            q = back * H[t, n]
            w[n % 2] = w[n % 2] + q * R[n]
            passed.append(back)
            if from_above:
                sums.append(acc[n] + d * q)
        u, w = u[0] + u[1], w[0] + w[1]
        dpre = (u * xv - w) * SG[t]
        DP[t] = dpre
        core_ref[t] = g + (u * d + skip8 * g)
        return tuple(passed), tuple(sums), bias_acc + dpre, skip_acc + g * xv

    start = ((zero,) * states, (zero,) * (states if from_above else 0), zero, zero)
    _, acc, bias_acc, skip_acc = lax.fori_loop(0, length, backward, start)

    S = gather_matrix(micro, length)
    dpre_half = dot(S, two_halves(half, DP[...].reshape(rows, 128)).astype(BF16)).astype(BF16)
    if from_above:
        lower = first_half(2 * micro, micro)
        for n in range(states):
            rate_out[n:n + 1, :] = -jnp.sum(two_halves(lower, acc[n]), axis=0, keepdims=True)
        bias_out[...] = jnp.sum(two_halves(lower, bias_acc), axis=0, keepdims=True)
        skip_out[...] = jnp.sum(two_halves(lower, skip_acc), axis=0, keepdims=True)
        dpre_ref[...] = dpre_half
    send_ref[:, :rank] = dot(dpre_half, wd_ref[...], NT).astype(BF16)
    sum_shape = (states * 128, doubled)
    depth, place = iota(sum_shape, 0) // 128, iota(sum_shape, 1)
    b_flat = Bv[...].reshape(rows, states * 128).astype(BF16)
    c_flat = Cv[...].reshape(rows, states * 128).astype(BF16)
    ds8 = dot(b_flat, one_hot(depth == place)) + dot(c_flat, one_hot(depth + states == place))
    high, low = two_terms(ds8)
    send_ref[:, rank:] = jnp.zeros((micro * length, WIDTH - rank), BF16)
    send_ref[:, rank:rank + doubled] = (dot(S, high) + dot(S, low)).astype(BF16)


def finish_kernel(micro, length, states, rank, replicas,
                  plan_ref, cat_ref, low_ref, x_ref, wl_ref, ws_ref, dpre_ref, core_ref, rate_ref, bias_ref, skip_ref,
                  grad_ref, send_ref, small):
    rows = 2 * micro * length
    doubled = 2 * states
    channels = x_ref.shape[1]
    half = first_half(rows, micro)
    T = spread_matrix(micro, length)
    cat = cat_ref[...]
    cat8 = dot(T, cat).astype(BF16)
    wide = dot(cat8[:, :rank], wl_ref[...], NT) + dot(cat8[:, rank:rank + doubled], ws_ref[...])
    grad8 = core_ref[...].reshape(rows, 128) + pick_half(half, wide)
    S = gather_matrix(micro, length, [plan_ref[j] for j in range(micro)])
    grad_ref[...] = dot(S, two_halves(half, grad8).astype(BF16)).astype(BF16)
    x = x_ref[...]
    own = channels // replicas
    part_low = dot(x, cat[:, :rank], TN).astype(BF16)
    send_ref[:, :own, :] = part_low.reshape(replicas, own, rank)
    part_delta = dot(low_ref[:, :rank], dpre_ref[...], TN).astype(BF16)
    part_delta = part_delta.reshape(replicas, rank // replicas, channels)
    deep = rank // replicas // 2
    send_ref[:, own:own + deep, :channels] = part_delta[:, :deep]
    send_ref[:, own:own + deep, channels:] = part_delta[:, deep:]
    part_sel = dot(cat[:, rank:rank + doubled], x, TN)
    small[...] = jnp.zeros(small.shape, F32)
    ds, dr = doubled // replicas, states // replicas
    for r in range(replicas):
        small[r, 0:ds, 0:channels] = part_sel[r * ds:(r + 1) * ds, :]
        small[r, 0:dr, channels:] = rate_ref[r * dr:(r + 1) * dr, :]
        small[r, dr:dr + 1, channels:channels + own] = bias_ref[:, r * own:(r + 1) * own]
        small[r, dr + 1:dr + 2, channels:channels + own] = skip_ref[:, r * own:(r + 1) * own]
    send_ref[:, own + deep:, :] = small[...].astype(BF16)


def total_kernel(got_ref, low_ref, delta_ref, sel_ref, rate_ref, bias_ref, skip_ref):
    total = got_ref[0].astype(F32)
    for r in range(1, got_ref.shape[0]):
        total = total + got_ref[r].astype(F32)
    own, channels = low_ref.shape[0], delta_ref.shape[1]
    deep = delta_ref.shape[0] // 2
    low_ref[...] = total[:own]
    delta_ref[:deep] = total[own:own + deep, :channels]
    delta_ref[deep:] = total[own:own + deep, channels:]
    rest = total[own + deep:]
    ds, dr = sel_ref.shape[0], rate_ref.shape[0]
    sel_ref[...] = rest[:ds, :channels]
    rate_ref[...] = rest[:dr, channels:]
    bias_ref[...] = rest[dr:dr + 1, channels:channels + own]
    skip_ref[...] = rest[dr + 1:dr + 2, channels:channels + own]


def call(kernel, outs, scratch, *args, scalars=0):
    vmem = pl.BlockSpec(memory_space=pltpu.VMEM)
    smem = pl.BlockSpec(memory_space=pltpu.SMEM)
    return pl.pallas_call(
        kernel,
        out_shape=[jax.ShapeDtypeStruct(*out) for out in outs],
        in_specs=[smem] * scalars + [vmem] * (len(args) - scalars),
        out_specs=[vmem] * len(outs),
        scratch_shapes=[pltpu.VMEM(shape, F32) for shape in scratch],
        compiler_params=pltpu.CompilerParams(vmem_limit_bytes=VMEM_LIMIT),
    )(*args)


def exchange(blocks, axes):
    return lax.all_to_all(blocks, axes, 0, 0)


def to_all(block, axes):
    count = lax.axis_size(axes)
    return exchange(jnp.broadcast_to(block[None], (count,) + block.shape), axes)


def total(blocks):
    return jnp.sum(blocks.astype(F32), axis=0)


def scattered_sum(rows, axes, first=0):
    count = lax.axis_size(axes)
    got = exchange(rows.reshape(count, rows.shape[0] // count, rows.shape[1]), axes)
    return total(to_all(total(got[first:]).astype(BF16), "zh"))


def per_device(x_saved, side_grad, plan, w_low, w_delta, w_select, decay_rate, delta_bias, skip_gain):
    micro, length, channels = x_saved.shape
    tokens = micro * length
    rank, doubled, states = w_low.shape[1], w_select.shape[0], decay_rate.shape[0]
    replicas = lax.axis_size(REPLICAS)
    x = x_saved.reshape(tokens, channels)
    side = side_grad.reshape(tokens, channels)
    bias, skip = delta_bias.reshape(1, channels), skip_gain.reshape(1, channels)
    down = [(1, 0)]

    part = call(project_kernel, [((tokens, WIDTH), BF16)], [], x, w_low, w_select)[0]
    up_low = lax.ppermute(w_low, "ly", down)
    up_sel = lax.ppermute(w_select, "ly", down)
    summed = scattered_sum(part, NEAR)
    selected = summed[:, rank:rank + doubled]
    high = lax.reduce_precision(selected, 8, 7)
    rest = jnp.zeros((summed.shape[0], WIDTH - rank - 2 * doubled), F32)
    packed = jnp.concatenate([summed[:, :rank], high, selected - high, rest], axis=1).astype(BF16)
    cat = to_all(packed, NEAR).reshape(tokens, WIDTH)

    slabs = (length, 2 * micro, 128)
    wide = (length, 2 * micro, states * 128)
    scratch = [(length, states, 2 * micro, 128), (length + 1, states, 2 * micro, 128), wide, wide,
               (states, 2 * micro, 128)] + [slabs] * 6
    shared = (x, side, cat, w_delta, decay_rate, bias, skip)
    send, core = call(
        functools.partial(tick_kernel, micro, length, states, rank, False),
        [((tokens, WIDTH), BF16), (slabs, F32)], scratch, *shared)
    up_core = lax.ppermute(core, "ly", down)
    upper = lax.axis_size(BOTH) // LAYERS
    up_cat = to_all(scattered_sum(send, BOTH, upper).astype(BF16), BOTH).reshape(tokens, WIDTH)

    send, core, dpre, rate_part, bias_part, skip_part = call(
        functools.partial(tick_kernel, micro, length, states, rank, True),
        [((tokens, WIDTH), BF16), (slabs, F32), ((tokens, channels), BF16), ((states, channels), F32),
         ((1, channels), F32), ((1, channels), F32)],
        scratch, *shared, up_cat, up_core, up_low, up_sel)
    down_cat = to_all(scattered_sum(send, NEAR).astype(BF16), NEAR).reshape(tokens, WIDTH)

    own, deep = channels // replicas, rank // replicas
    packed_rows = own + deep // 2 + 16
    grad, partials = call(
        functools.partial(finish_kernel, micro, length, states, rank, replicas),
        [((tokens, channels), BF16), ((replicas, packed_rows, rank), BF16)],
        [(replicas, 16, rank)],
        plan, down_cat, cat, x, w_low, w_select, dpre, core, rate_part, bias_part, skip_part, scalars=1)
    got = exchange(partials, REPLICAS)
    sums = call(
        total_kernel,
        [((own, rank), F32), ((deep, channels), F32), ((doubled // replicas, channels), F32),
         ((states // replicas, channels), F32), ((1, own), F32), ((1, own), F32)], [], got)
    return (grad.reshape(micro, length, channels), *sums[:4], sums[4].reshape(own), sums[5].reshape(own))


def solution(mesh):
    axes = ("ly", "yl", "zh", "x") + REPLICAS
    fine = Mesh(np.asarray(mesh.devices).reshape(2, 2, 4, 4, 4, 2), axes)
    section, dp = axes[:4], REPLICAS
    in_specs = (
        P(None, dp, section),
        P(None, dp, section),
        P(),
        P(section, None),
        P(None, section),
        P(None, section),
        P(None, section),
        P(section),
        P(section),
    )
    out_specs = (
        P(None, dp, section),
        P(section + dp, None),
        P(dp, section),
        P(dp, section),
        P(dp, section),
        P(section + dp),
        P(section + dp),
    )
    return jax.shard_map(per_device, mesh=fine, in_specs=in_specs, out_specs=out_specs, check_vma=False)
```

time: 902 us -> 169 us (0.19); the launches traced: 890 us -> 168 us
  waiting for transfers between devices: 322 us -> 27.2 us
  starting transfers between devices: 253 us -> 25.9 us
  local copies, waits for them, and re-layouts: 134 us -> 5.89 us
  other arithmetic: 48.1 us -> 0.2 us
  matrix products: 22.5 us -> 0 us
  blocking collectives: 79.6 us -> 97.2 us
  between operations: 16.2 us -> 0.84 us
  loops' own time: 14.7 us -> 0 us
  Pallas kernels: 0 us -> 11.1 us
    ppermute x65 -> x3, waiting for transfers between devices: 278 us -> 5.23 us  [the longest x1 5.22 us: per_device(): up_sel = lax.ppermute(w_select, 'ly', down)]
    ppermute x65 -> x3, starting transfers between devices: 253 us -> 3.88 us  [the longest x1 1.29 us: per_device(): up_low = lax.ppermute(w_low, 'ly', down)]
    all_to_all x0 -> x7, blocking collectives: none -> 97.2 us  [exchange(): return lax.all_to_all(blocks, axes, 0, 0)]
    unnamed x1 -> x0, blocking collectives: 79.6 us -> none
    pad x136 -> x0, local copies, waits for them, and re-layouts: 54.7 us -> none  [scan_core(): _, states = lax.associative_scan(combine, (decays, driven), axis=0)]
    reduce_scatter x2 -> x0, waiting for transfers between devices: 43.9 us -> none  [the longest x1 41.1 us: per_device(): lax.psum_scatter(stashed[1].astype(jnp.bfloat16), 'dp', scatter_dimension...]
    cond x296 -> x0, local copies, waits for them, and re-layouts: 36.8 us -> none
    dot_general x34 -> x0, matrix products: 22.5 us -> none  [the longest x4 6.95 us: scan_pullback(): jnp.dot(lowrank, w_step, preferred_element_type=jnp.float32) + biases]
  transfers between devices with their start and end apart: 67 -> 6, of which waited for: 56 -> 3; matrix products, arithmetic and copies ran while one was open for 1% -> 0% of each run, Pallas kernels for 0% -> 0%
where the time goes in v1:
time: 169 us; the launch traced here: 168 us
  blocking collectives  97.2 us (58%)
  waiting for transfers between devices  27.2 us (16%)
  starting transfers between devices  25.9 us (15%)
  Pallas kernels  11.1 us (7%)
  local copies, waits for them, and re-layouts  5.89 us (3%)
    all_to_all x7, blocking collectives, exchange(): return lax.all_to_all(blocks, axes, 0, 0)  97.2 us
    all_to_all x3, waiting for transfers between devices, exchange(): return lax.all_to_all(blocks, axes, 0, 0)  22 us
    all_to_all x3, starting transfers between devices, exchange(): return lax.all_to_all(blocks, axes, 0, 0)  22 us
    pallas_call x5, Pallas kernels, call(): pl.pallas_call(kernel, out_shape=[jax.ShapeDtypeStruct(*out) for out in o...  11.1 us
    ppermute x1, waiting for transfers between devices, per_device(): up_sel = lax.ppermute(w_select, 'ly', down)  5.22 us
    unnamed x24, local copies, waits for them, and re-layouts  3.84 us
  transfers between devices with their start and end apart: 6, of which 3 were waited for; matrix products, arithmetic and copies ran while one was open for 0% of the time, Pallas kernels for 0%

profile of v1, /device:TPU:1, one launch (start us, length us, event | category | flops | bytes accessed | tf_op | source)
XLA Modules:
  0.0 168.4 jit_solution(14408047266857540572)
XLA Ops:
  0.6 0.0 copy-start
  0.6 0.9 copy-done
  1.6 0.0 copy-start.2
  1.6 0.8 copy-done.2
  2.4 0.0 copy-start.7
  2.4 0.7 copy-done.7
  3.1 0.2 shard_map.144
  3.4 11.3 %all_to_all.50 = bf16[8,16,640]{2,1,0:T(8,128)(2,1)S(1)} all-to-all(bf16[8,16,640]{2,1,0:T(8,128)(2,1)S(1)} %bitcast.21), channel_id=1, replica_groups=mesh['ly'=2,'yl'=2,'zh'=4,'x'=4,'zl'=4,'core'=2] {'yl','x'}, dimensions={0} | all-to-all | bytes 327680 | tf_op jit(solution)/shard_map/all_to_all | solution.py:248
  14.6 0.6 broadcast_in_dim.14
  15.3 15.1 %all-to-all-start.1 = ((bf16[4,16,640]{2,1,0:T(8,128)(2,1)}), bf16[4,16,640]{2,1,0:T(8,128)(2,1)S(1)}, u32[]{:S(2)}, u32[]{:S(2)}) async-start(bf16[4,16,640]{2,1,0:T(8,128)(2,1)} %broadcast_in_dim.14), calls=%async_computation.1 | async-start | bytes 163840 | tf_op jit(solution)/shard_map/all_to_all | solution.py:248
  30.4 0.1 pad.3.clone
  30.5 11.7 %all-to-all-done.1 = bf16[4,16,640]{2,1,0:T(8,128)(2,1)S(1)} async-done(((bf16[4,16,640]{2,1,0:T(8,128)(2,1)}), bf16[4,16,640]{2,1,0:T(8,128)(2,1)S(1)}, u32[]{:S(2)}, u32[]{:S(2)}) %all-to-all-start.1) | async-done | bytes 81952 | tf_op jit(solution)/shard_map/all_to_all | solution.py:248
  42.2 0.1 maximum_maximum_fusion
  42.3 0.0 copy-start.4
  42.3 0.0 copy-start.3
  42.3 0.0 copy-start.5
  42.3 0.0 copy-start.6
  42.3 0.0 copy-start.10
  42.4 8.1 %all_to_all.51 = bf16[8,16,640]{2,1,0:T(8,128)(2,1)S(1)} all-to-all(bf16[8,16,640]{2,1,0:T(8,128)(2,1)S(1)} %broadcast_in_dim.16), channel_id=1, replica_groups=mesh['ly'=2,'yl'=2,'zh'=4,'x'=4,'zl'=4,'core'=2] {'yl','x'}, dimensions={0} | all-to-all | bytes 327680 | tf_op jit(solution)/shard_map/all_to_all | solution.py:248
  50.5 0.0 copy-start.9
  50.5 0.0 copy-done.4
  50.5 0.0 copy-done.3
  50.5 0.0 copy-done.5
  50.5 0.0 copy-done.6
  50.5 0.0 copy-done.10
  50.5 0.6 copy-done.9
  51.2 3.9 %shard_map.145 = (bf16[128,640]{1,0:T(8,128)(2,1)S(1)}, f32[32,8,128]{2,1,0:T(8,128)S(1)}) custom-call(bf16[128,256]{1,0:T(8,128)(2,1)S(1)} %bitcast.17, bf16[128,256]{1,0:T(8,128)(2,1)S(1)} %bitcast.23, bf16[128,640]{1,0:T(8,128)(2,1)S(1)} %bitcast.13, bf16[512,256]{1,0:T(8,128)(2,1)S(1)} %copy-done.4, f32[16,256]{1,0:T(8,128)S(1)} %copy-done.6, ...), custom_call_target="tpu_custom_call" | custom-call | tf_op jit(solution)/shard_map/pallas_call | solution.py:237
  55.1 0.0 copy-start.1
  55.1 11.6 %all_to_all.52 = bf16[16,8,640]{2,1,0:T(8,128)(2,1)S(1)} all-to-all(bf16[16,8,640]{2,1,0:T(8,128)(2,1)S(1)} %bitcast.26), channel_id=1, replica_groups=mesh['ly'=2,'yl'=2,'zh'=4,'x'=4,'zl'=4,'core'=2] {'ly','yl','x'}, dimensions={0} | all-to-all | bytes 327680 | tf_op jit(solution)/shard_map/all_to_all | solution.py:248
  66.8 0.6 broadcast_in_dim.17
  67.4 3.3 %all-to-all-start.4 = ((bf16[4,8,640]{2,1,0:T(8,128)(2,1)}), bf16[4,8,640]{2,1,0:T(8,128)(2,1)S(1)}, u32[]{:S(2)}, u32[]{:S(2)}) async-start(bf16[4,8,640]{2,1,0:T(8,128)(2,1)} %broadcast_in_dim.17), calls=%async_computation.4 | async-start | bytes 81920 | tf_op jit(solution)/shard_map/all_to_all | solution.py:248
  70.7 0.0 copy-done.1
  70.7 1.3 collective-permute-start.1
  72.0 10.3 %all-to-all-done.4 = bf16[4,8,640]{2,1,0:T(8,128)(2,1)S(1)} async-done(((bf16[4,8,640]{2,1,0:T(8,128)(2,1)}), bf16[4,8,640]{2,1,0:T(8,128)(2,1)S(1)}, u32[]{:S(2)}, u32[]{:S(2)}) %all-to-all-start.4) | async-done | bytes 40992 | tf_op jit(solution)/shard_map/all_to_all | solution.py:248
  82.3 0.7 broadcast_in_dim.18
  83.0 0.0 copy-start.8
  83.0 3.6 %all-to-all-start.5 = ((bf16[16,8,640]{2,1,0:T(8,128)(2,1)}), bf16[16,8,640]{2,1,0:T(8,128)(2,1)S(1)}, u32[]{:S(2)}, u32[]{:S(2)}) async-start(bf16[16,8,640]{2,1,0:T(8,128)(2,1)} %broadcast_in_dim.18), calls=%async_computation.5 | async-start | bytes 327680 | tf_op jit(solution)/shard_map/all_to_all | solution.py:248
  86.6 1.3 collective-permute-start
  87.9 0.0 copy-done.8
  88.0 1.3 collective-permute-start.2
  89.3 5.2 %collective-permute-done.2.refs_10_ = bf16[32,256]{1,0:T(8,128)(2,1)S(1)} collective-permute-done((bf16[32,256]{1,0:T(8,128)(2,1)S(1)}, bf16[32,256]{1,0:T(8,128)(2,1)S(1)}, u32[]{:S(2)}, u32[]{:S(2)}) %collective-permute-start.2) | collective-permute-done | bytes 16416 | tf_op jit(solution)/shard_map/ppermute | solution.py:278
  94.5 0.0 collective-permute-done.1.refs_9_
  94.5 0.0 collective-permute-done.refs_8_
  94.5 0.0 all-to-all-done.5
  94.5 4.4 %shard_map.146 = (bf16[128,640]{1,0:T(8,128)(2,1)S(1)}, f32[32,8,128]{2,1,0:T(8,128)S(1)}, bf16[128,256]{1,0:T(8,128)(2,1)S(1)}, f32[16,256]{1,0:T(8,128)S(1)}, ...) custom-call(bf16[128,256]{1,0:T(8,128)(2,1)S(1)} %bitcast.18, bf16[128,256]{1,0:T(8,128)(2,1)S(1)} %bitcast.24, ...), custom_call_target="tpu_custom_call" | custom-call | tf_op jit(solution)/shard_map/pallas_call | solution.py:237
  98.9 9.9 %all_to_all.53 = bf16[8,16,640]{2,1,0:T(8,128)(2,1)S(1)} all-to-all(bf16[8,16,640]{2,1,0:T(8,128)(2,1)S(1)} %bitcast.25), channel_id=1, replica_groups=mesh['ly'=2,'yl'=2,'zh'=4,'x'=4,'zl'=4,'core'=2] {'yl','x'}, dimensions={0} | all-to-all | bytes 327680 | tf_op jit(solution)/shard_map/all_to_all | solution.py:248
  108.9 14.9 %all_to_all.54 = bf16[4,16,640]{2,1,0:T(8,128)(2,1)S(1)} all-to-all(bf16[4,16,640]{2,1,0:T(8,128)(2,1)S(1)} %broadcast_in_dim.19), channel_id=1, replica_groups=mesh['ly'=2,'yl'=2,'zh'=4,'x'=4,'zl'=4,'core'=2] {'zh'}, dimensions={0} | all-to-all | bytes 163840 | tf_op jit(solution)/shard_map/all_to_all | solution.py:248
  123.8 8.3 %all_to_all.55 = bf16[8,16,640]{2,1,0:T(8,128)(2,1)S(1)} all-to-all(bf16[8,16,640]{2,1,0:T(8,128)(2,1)S(1)} %broadcast_in_dim.20), channel_id=1, replica_groups=mesh['ly'=2,'yl'=2,'zh'=4,'x'=4,'zl'=4,'core'=2] {'yl','x'}, dimensions={0} | all-to-all | bytes 327680 | tf_op jit(solution)/shard_map/all_to_all | solution.py:248
  132.1 0.0 copy-start.11
  132.1 0.7 copy-done.11
  132.8 1.9 %shard_map.147 = (bf16[128,256]{1,0:T(8,128)(2,1)}, bf16[8,80,512]{2,1,0:T(8,128)(2,1)S(1)}) custom-call(s32[4]{0:T(128)S(1)} %copy-done.11, bf16[128,640]{1,0:T(8,128)(2,1)S(1)} %bitcast.22, bf16[128,640]{1,0:T(8,128)(2,1)S(1)} %bitcast.15, bf16[128,256]{1,0:T(8,128)(2,1)S(1)} %bitcast.19, bf16[256,512]{1,0:T(8,128)(2,1)S(1)} %copy-done.1, ...), custom_call_target="tpu_custom_call" | custom-call | tf_op jit(solution)/shard_map/pallas_call | solution.py:237
  134.6 33.1 %all_to_all.56.got_ref = bf16[8,80,512]{2,1,0:T(8,128)(2,1)S(1)} all-to-all(bf16[8,80,512]{2,1,0:T(8,128)(2,1)S(1)} %get-tuple-element.32), channel_id=1, replica_groups=mesh['ly'=2,'yl'=2,'zh'=4,'x'=4,'zl'=4,'core'=2] {'zl','core'}, dimensions={0} | all-to-all | bytes 1310720 | tf_op jit(solution)/shard_map/all_to_all | solution.py:248
  167.7 0.7 shard_map.148
  (12 shorter events, 0.2 us)
Async XLA Ops:
  0.6 1.0 copy-start
  1.6 0.8 copy-start.2
  2.4 0.7 copy-start.7
  15.3 26.9 %all-to-all-start.1 = ((bf16[4,16,640]{2,1,0:T(8,128)(2,1)}), bf16[4,16,640]{2,1,0:T(8,128)(2,1)S(1)}, u32[]{:S(2)}, u32[]{:S(2)}) async-start(bf16[4,16,640]{2,1,0:T(8,128)(2,1)} %broadcast_in_dim.14), calls=%async_computation.1 | async-start | bytes 163840 | tf_op jit(solution)/shard_map/all_to_all | solution.py:248
  42.3 8.2 %copy-start.4 = (bf16[512,256]{1,0:T(8,128)(2,1)S(1)}, bf16[512,256]{1,0:T(8,128)(2,1)}, u32[]{:S(2)}) copy-start(bf16[512,256]{1,0:T(8,128)(2,1)} %refs_3_.3) | copy-start | bytes 786436
  42.3 8.2 %copy-start.3 = (bf16[4,32,256]{2,1,0:T(8,128)(2,1)S(1)}, bf16[4,32,256]{2,1,0:T(8,128)(2,1)}, u32[]{:S(2)}) copy-start(bf16[4,32,256]{2,1,0:T(8,128)(2,1)} %param.9) | copy-start | bytes 196612
  42.3 8.2 %copy-start.5 = (bf16[4,32,256]{2,1,0:T(8,128)(2,1)S(1)}, bf16[4,32,256]{2,1,0:T(8,128)(2,1)}, u32[]{:S(2)}) copy-start(bf16[4,32,256]{2,1,0:T(8,128)(2,1)} %param.10) | copy-start | bytes 196612
  42.3 8.2 %copy-start.6 = (f32[16,256]{1,0:T(8,128)S(1)}, f32[16,256]{1,0:T(8,128)}, u32[]{:S(2)}) copy-start(f32[16,256]{1,0:T(8,128)} %refs_4_.3) | copy-start | bytes 49156
  42.3 8.2 %copy-start.10 = (f32[256]{0:T(256)S(1)}, f32[256]{0:T(256)}, u32[]{:S(2)}) copy-start(f32[256]{0:T(256)} %param.17) | copy-start | bytes 3076
  50.5 0.7 copy-start.9
  55.1 15.6 %copy-start.1 = (bf16[256,512]{1,0:T(8,128)(2,1)S(1)}, bf16[256,512]{1,0:T(8,128)(2,1)}, u32[]{:S(2)}) copy-start(bf16[256,512]{1,0:T(8,128)(2,1)} %wl_ref.3) | copy-start | bytes 786436
  67.4 14.9 %all-to-all-start.4 = ((bf16[4,8,640]{2,1,0:T(8,128)(2,1)}), bf16[4,8,640]{2,1,0:T(8,128)(2,1)S(1)}, u32[]{:S(2)}, u32[]{:S(2)}) async-start(bf16[4,8,640]{2,1,0:T(8,128)(2,1)} %broadcast_in_dim.17), calls=%async_computation.4 | async-start | bytes 81920 | tf_op jit(solution)/shard_map/all_to_all | solution.py:248
  70.7 23.8 %collective-permute-start.1 = (bf16[256,512]{1,0:T(8,128)(2,1)S(1)}, bf16[256,512]{1,0:T(8,128)(2,1)S(1)}, u32[]{:S(2)}, u32[]{:S(2)}) collective-permute-start(bf16[256,512]{1,0:T(8,128)(2,1)S(1)} %copy-done.1), channel_id=1, source_target_pairs={{256,0},{257,1},{258,2},{259,3},{260,4},{261,5},{262,6},{263,7},{2... | collective-permute-start | bytes 786440 | tf_op jit(solution)/shard_map/ppermute | solution.py:277
  83.0 5.0 %copy-start.8 = (bf16[32,256]{1,0:T(8,128)(2,1)S(1)}, bf16[32,256]{1,0:T(8,128)(2,1)}, u32[]{:S(2)}) copy-start(bf16[32,256]{1,0:T(8,128)(2,1)} %ws_ref.3) | copy-start | bytes 49156
  83.0 11.5 %all-to-all-start.5 = ((bf16[16,8,640]{2,1,0:T(8,128)(2,1)}), bf16[16,8,640]{2,1,0:T(8,128)(2,1)S(1)}, u32[]{:S(2)}, u32[]{:S(2)}) async-start(bf16[16,8,640]{2,1,0:T(8,128)(2,1)} %broadcast_in_dim.18), calls=%async_computation.5 | async-start | bytes 327680 | tf_op jit(solution)/shard_map/all_to_all | solution.py:248
  86.6 7.8 %collective-permute-start = (f32[32,8,128]{2,1,0:T(8,128)S(1)}, f32[32,8,128]{2,1,0:T(8,128)S(1)}, u32[]{:S(2)}, u32[]{:S(2)}) collective-permute-start(f32[32,8,128]{2,1,0:T(8,128)S(1)} %get-tuple-element.24), channel_id=1, source_target_pairs={{256,0},{257,1},{258,2},{259,3},{260,4},{261,5},{262,6},{263,7},{2... | collective-permute-start | bytes 393224 | tf_op jit(solution)/shard_map/ppermute | solution.py:294
  88.0 6.5 %collective-permute-start.2 = (bf16[32,256]{1,0:T(8,128)(2,1)S(1)}, bf16[32,256]{1,0:T(8,128)(2,1)S(1)}, u32[]{:S(2)}, u32[]{:S(2)}) collective-permute-start(bf16[32,256]{1,0:T(8,128)(2,1)S(1)} %copy-done.8), channel_id=1, source_target_pairs={{256,0},{257,1},{258,2},{259,3},{260,4},{261,5},{262,6},{263,7},{2... | collective-permute-start | bytes 49160 | tf_op jit(solution)/shard_map/ppermute | solution.py:278
  132.1 0.7 copy-start.11

commit v2 on v1

v2 whole, which is shorter than its diff:
```python
import functools

import jax
import jax.numpy as jnp
import numpy as np
from jax import lax
from jax.experimental import pallas as pl
from jax.experimental.pallas import tpu as pltpu
from jax.sharding import Mesh
from jax.sharding import PartitionSpec as P

F32, BF16 = jnp.float32, jnp.bfloat16
WIDTH = 640
NN = (((1,), (0,)), ((), ()))
NT = (((1,), (1,)), ((), ()))
TN = (((0,), (0,)), ((), ()))
NEAR = ("yl", "x")
REPLICAS = ("zl", "core")
VMEM_LIMIT = 48 * 1024 * 1024
PROJECT_LIMIT = 60 * 1024 * 1024
SEL_ROWS = 8
UNROLL = 1


def dot(a, b, dims=NN):
    return lax.dot_general(a, b, dims, preferred_element_type=F32)


def iota(shape, dim):
    return lax.broadcasted_iota(jnp.int32, shape, dim)


def one_hot(mask):
    return jnp.where(mask, 1.0, 0.0).astype(BF16)


def spread_matrix(micro, length):
    shape = (2 * micro * length, micro * length)
    r, c = iota(shape, 0), iota(shape, 1)
    return one_hot((r % micro) * length + r // (2 * micro) == c)


def gather_matrix(micro, length, order=None):
    shape = (micro * length, 2 * micro * length)
    r, c = iota(shape, 0), iota(shape, 1)
    which = r // length
    if order is not None:
        slot, which = which, jnp.zeros(shape, jnp.int32)
        for j in range(micro):
            which = jnp.where(slot == j, order[j], which)
    return one_hot(which * length + r % length == (c % micro) * length + c // (2 * micro))


def first_half(rows, micro, lanes=128):
    return (iota((rows, lanes), 0) // micro) % 2 == 0


def pick_half(half, wide):
    return jnp.where(half, wide[:, :128], wide[:, 128:])


def two_halves(half, value):
    return jnp.concatenate([jnp.where(half, value, 0.0), jnp.where(half, 0.0, value)], axis=1)


def two_terms(value):
    high = value.astype(BF16)
    return high, (value - high.astype(F32)).astype(BF16)


def fetch(sources, targets, sems):
    copies = [pltpu.make_async_copy(src, dst, sems.at[i]) for i, (src, dst) in enumerate(zip(sources, targets))]
    for copy in copies:
        copy.start()
    return copies


def project_kernel(x_hbm, ws_hbm, wl_hbm, rate_hbm, bias_hbm, skip_hbm, out_ref, const_ref,
                   x_ref, ws_ref, wl_ref, rate_ref, bias_ref, skip_ref, sems):
    copies = fetch((x_hbm, wl_hbm, ws_hbm, rate_hbm, bias_hbm, skip_hbm),
                   (x_ref, wl_ref, ws_ref, rate_ref, bias_ref, skip_ref), sems)
    rank, doubled, states = wl_ref.shape[1], ws_ref.shape[0], rate_ref.shape[0]
    const_ref[...] = jnp.zeros(const_ref.shape, F32)
    out_ref[:, rank:] = jnp.zeros((x_ref.shape[0], WIDTH - rank), BF16)
    for copy in copies:
        copy.wait()
    x = x_ref[...]
    out_ref[:, :rank] = dot(x, wl_ref[...]).astype(BF16)
    out_ref[:, rank:rank + doubled] = dot(x, ws_ref[...], NT).astype(BF16)
    const_ref[:states, :] = rate_ref[...]
    const_ref[states:states + 1, :] = bias_ref[...]
    const_ref[states + 1:states + 2, :] = skip_ref[...]


def forward(micro, length, states, rank, x, cat, wd, const_ref, A, H, Bv, Cv, R, X, D, DX, SG):
    rows = 2 * micro * length
    doubled = 2 * states
    half = first_half(rows, micro)
    lower = first_half(2 * micro, micro)
    T = spread_matrix(micro, length)
    slabs = (length, 2 * micro, 128)
    cat8 = dot(T, cat).astype(BF16)
    x8 = pick_half(half, dot(T, x)).reshape(slabs)
    wide_shape = (2 * doubled, states * 128)
    lane, row = iota(wide_shape, 1) // 128, iota(wide_shape, 0) % doubled
    terms = cat8[:, rank:rank + 2 * doubled]
    Bv[...] = dot(terms, one_hot(lane == row)).reshape(length, 2 * micro, states * 128)
    Cv[...] = dot(terms, one_hot(lane + states == row)).reshape(length, 2 * micro, states * 128)
    pre8 = pick_half(half, dot(cat8[:, :rank], wd)).reshape(slabs)
    pre8 = pre8 + pick_half(lower, const_ref[states:states + 1, :])[None]
    step8 = jax.nn.softplus(pre8)
    X[...] = x8
    D[...] = step8
    DX[...] = step8 * x8
    SG[...] = jax.nn.sigmoid(pre8)
    zero = jnp.zeros((2 * micro, 128), F32)
    for n in range(states):
        R[n] = pick_half(lower, const_ref[n:n + 1, :])
        H[0, n] = zero

    def ahead(t, h):
        d, dx = D[t], DX[t]
        out = []
        for n in range(states):
            a = jnp.exp(-(d * R[n]))
            h_n = a * h[n] + dx * Bv[t, :, n * 128:(n + 1) * 128]
            A[t, n] = a
            H[t + 1, n] = h_n
            out.append(h_n)
        return tuple(out)

    lax.fori_loop(0, length, ahead, (zero,) * states, unroll=UNROLL)


def backward(micro, length, states, rank, sums, wd, const_ref, G, A, H, Bv, Cv, R, X, D, DX, SG,
             send_ref, core_ref, Pb, Pc, DP):
    rows = 2 * micro * length
    doubled = 2 * states
    half = first_half(rows, micro)
    zero = jnp.zeros((2 * micro, 128), F32)
    skip8 = pick_half(first_half(2 * micro, micro), const_ref[states + 1:states + 2, :])

    def back(i, carry):
        later, acc, bias_acc, skip_acc = carry
        t = length - 1 - i
        d, dx, g, xv = D[t], DX[t], G[t], X[t]
        u, w = [zero, zero], [zero, zero]
        passed, added = [], []
        for n in range(states):
            at = slice(n * 128, (n + 1) * 128)
            lam = Cv[t, :, at] * g + later[n]
            u[n % 2] = u[n % 2] + lam * Bv[t, :, at]
            Pc[t, :, at] = g * H[t + 1, n]
            Pb[t, :, at] = lam * dx
            through = A[t, n] * lam
            q = through * H[t, n]
            w[n % 2] = w[n % 2] + q * R[n]
            passed.append(through)
            if sums:
                added.append(acc[n] + d * q)
        u, w = u[0] + u[1], w[0] + w[1]
        dpre = (u * xv - w) * SG[t]
        DP[t] = dpre
        core_ref[t] = g + (u * d + skip8 * g)
        if sums:
            bias_acc, skip_acc = bias_acc + dpre, skip_acc + g * xv
        return tuple(passed), tuple(added), bias_acc, skip_acc

    start = ((zero,) * states, (zero,) * (states if sums else 0), zero, zero)
    _, acc, bias_acc, skip_acc = lax.fori_loop(0, length, back, start, unroll=UNROLL)
    S = gather_matrix(micro, length)
    dpre_half = dot(S, two_halves(half, DP[...].reshape(rows, 128)).astype(BF16)).astype(BF16)
    send_ref[:, :rank] = dot(dpre_half, wd, NT).astype(BF16)
    sum_shape = (states * 128, doubled)
    depth, place = iota(sum_shape, 0) // 128, iota(sum_shape, 1)
    b_flat = Pb[...].reshape(rows, states * 128).astype(BF16)
    c_flat = Pc[...].reshape(rows, states * 128).astype(BF16)
    ds8 = dot(b_flat, one_hot(depth == place)) + dot(c_flat, one_hot(depth + states == place))
    high, low = two_terms(ds8)
    send_ref[:, rank:] = jnp.zeros((micro * length, WIDTH - rank), BF16)
    send_ref[:, rank:rank + doubled] = (dot(S, high) + dot(S, low)).astype(BF16)
    return dpre_half, acc, bias_acc, skip_acc


def tick_kernel(micro, length, states, rank, from_above, *refs):
    x_ref, side_ref, cat_ref, wd_ref, const_ref, *refs = refs
    if from_above:
        above_ref, send_ref, core_ref, dpre_ref, rate_out, ends_ref, *refs = refs
    else:
        send_ref, core_ref, *refs = refs
    G, Pb, Pc, DP, *state = refs
    rows = 2 * micro * length
    channels = x_ref.shape[1]
    half = first_half(rows, micro)
    T = spread_matrix(micro, length)
    g8 = pick_half(half, dot(T, side_ref[...]))
    if from_above:
        g8 = g8 + pick_half(half, dot(T, above_ref[...]))
    G[...] = g8.reshape(G.shape)
    forward(micro, length, states, rank, x_ref[...], cat_ref[...], wd_ref[...], const_ref, *state)
    dpre_half, acc, bias_acc, skip_acc = backward(
        micro, length, states, rank, from_above, wd_ref[...], const_ref, G, *state, send_ref, core_ref, Pb, Pc, DP)
    if from_above:
        dpre_ref[...] = dpre_half
        for n in range(states):
            rate_out[n] = acc[n]
        ends_ref[0] = bias_acc
        ends_ref[1] = skip_acc


def layer_grad(micro, length, states, rank, cat_ref, wl_ref, ws_ref, core_ref):
    rows = 2 * micro * length
    half = first_half(rows, micro)
    cat8 = dot(spread_matrix(micro, length), cat_ref[...]).astype(BF16)
    wide = dot(cat8[:, :rank], wl_ref[...], NT) + dot(cat8[:, rank:rank + 2 * states], ws_ref[...])
    return two_halves(half, core_ref[...].reshape(rows, 128) + pick_half(half, wide)).astype(BF16)


def hand_kernel(micro, length, states, rank, cat_ref, wl_ref, ws_ref, core_ref, grad_ref):
    grad8 = layer_grad(micro, length, states, rank, cat_ref, wl_ref, ws_ref, core_ref)
    grad_ref[...] = dot(gather_matrix(micro, length), grad8).astype(BF16)


def order_kernel(micro, length, states, rank, plan_hbm, cat_ref, wl_ref, ws_ref, core_ref, grad_ref, plan_ref, sems):
    copies = fetch((plan_hbm,), (plan_ref,), sems)
    grad8 = layer_grad(micro, length, states, rank, cat_ref, wl_ref, ws_ref, core_ref)
    copies[0].wait()
    S = gather_matrix(micro, length, [plan_ref[j] for j in range(micro)])
    grad_ref[...] = dot(S, grad8).astype(BF16)


def part_kernel(micro, replicas, cat_ref, down_ref, x_ref, dpre_ref, rate_ref, ends_ref, send_ref, small):
    states = rate_ref.shape[0]
    channels, rank = x_ref.shape[1], (send_ref.shape[2] - 128) // 2
    own, deep, doubled = channels // replicas, rank // replicas, 2 * states
    share, rate_share = doubled // replicas, states // replicas
    x, down = x_ref[...], down_ref[...]
    send_ref[:, :, :rank] = dot(x, down[:, :rank], TN).astype(BF16).reshape(replicas, own, rank)
    delta = dot(cat_ref[:, :rank], dpre_ref[...], TN).astype(BF16).reshape(replicas, deep, channels)
    send_ref[:, :, rank:rank + channels] = delta[:, :own]
    send_ref[:, :, rank + channels:2 * rank] = delta[:, own:]
    select = dot(down[:, rank:rank + doubled], x, TN)
    lower = first_half(2 * micro, micro)

    def row_of(value):
        return jnp.sum(two_halves(lower, value), axis=0, keepdims=True)

    small[...] = jnp.zeros(small.shape, F32)
    for r in range(replicas):
        for k in range(2):
            small[r, k * share:(k + 1) * share, :] = select[r * share:(r + 1) * share, k * 128:(k + 1) * 128]
    for n in range(states):
        row = -row_of(rate_ref[n])
        at = SEL_ROWS + 2 * (n % rate_share)
        small[n // rate_share, at:at + 1, :] = row[:, :128]
        small[n // rate_share, at + 1:at + 2, :] = row[:, 128:]
    at = SEL_ROWS + 2 * rate_share
    for k in range(2):
        row = row_of(ends_ref[k])
        for r in range(replicas):
            small[r, at + k:at + k + 1, :own] = row[:, r * own:(r + 1) * own]
    send_ref[:, :, 2 * rank:] = small[...].astype(BF16)


def total_kernel(got_ref, low_ref, delta_ref, sel_ref, rate_ref, bias_ref, skip_ref):
    own, rank = low_ref.shape
    channels = delta_ref.shape[1]

    def summed(lanes):
        value = got_ref[0, :, lanes].astype(F32)
        for r in range(1, got_ref.shape[0]):
            value = value + got_ref[r, :, lanes].astype(F32)
        return value

    low_ref[...] = summed(slice(0, rank))
    delta_ref[:own] = summed(slice(rank, rank + channels))
    delta_ref[own:] = summed(slice(rank + channels, 2 * rank))
    small = summed(slice(2 * rank, 2 * rank + 128))
    rows, share = sel_ref.shape[0], rate_ref.shape[0]
    for k in range(2):
        sel_ref[:, k * 128:(k + 1) * 128] = small[k * rows:(k + 1) * rows]
        for n in range(share):
            at = SEL_ROWS + 2 * n + k
            rate_ref[n:n + 1, k * 128:(k + 1) * 128] = small[at:at + 1]
    at = SEL_ROWS + 2 * share
    bias_ref[...] = small[at:at + 1, :own]
    skip_ref[...] = small[at + 1:at + 2, :own]


def call(kernel, outs, scratch, *args, far=0, limit=VMEM_LIMIT):
    vmem = pl.BlockSpec(memory_space=pltpu.VMEM)
    hbm = pl.BlockSpec(memory_space=pl.ANY)
    return pl.pallas_call(
        kernel,
        out_shape=[jax.ShapeDtypeStruct(*out) for out in outs],
        in_specs=[hbm] * far + [vmem] * (len(args) - far),
        out_specs=[vmem] * len(outs),
        scratch_shapes=[pltpu.VMEM(s, F32) if isinstance(s, tuple) else s for s in scratch],
        compiler_params=pltpu.CompilerParams(vmem_limit_bytes=limit),
    )(*args)


def exchange(blocks, axes):
    return lax.all_to_all(blocks, axes, 0, 0)


def to_all(block, axes):
    count = lax.axis_size(axes)
    return exchange(jnp.broadcast_to(block[None], (count,) + block.shape), axes)


def total(blocks):
    return jnp.sum(blocks.astype(F32), axis=0)


def scattered_sum(rows, axes):
    count = lax.axis_size(axes)
    got = exchange(rows.reshape(count, rows.shape[0] // count, rows.shape[1]), axes)
    return total(to_all(total(got).astype(BF16), "zh"))


def per_device(x_saved, side_grad, plan, w_low, w_delta, w_select, decay_rate, delta_bias, skip_gain):
    micro, length, channels = x_saved.shape
    tokens = micro * length
    rank, doubled, states = w_low.shape[1], w_select.shape[0], decay_rate.shape[0]
    replicas = lax.axis_size(REPLICAS)
    x = x_saved.reshape(tokens, channels)
    side = side_grad.reshape(tokens, channels)
    bias, skip = delta_bias.reshape(1, channels), skip_gain.reshape(1, channels)

    sources = (x, w_select, w_low, decay_rate, bias, skip)
    part, const = call(
        project_kernel, [((tokens, WIDTH), BF16), ((states + 8, channels), F32)],
        [pltpu.VMEM(a.shape, a.dtype) for a in sources] + [pltpu.SemaphoreType.DMA((len(sources),))],
        *sources, far=len(sources), limit=PROJECT_LIMIT)
    summed = scattered_sum(part, NEAR)
    selected = summed[:, rank:rank + doubled]
    high = lax.reduce_precision(selected, 8, 7)
    rest = summed[:, rank + 2 * doubled:]
    packed = jnp.concatenate([summed[:, :rank], high, selected - high, rest], axis=1).astype(BF16)
    cat = to_all(packed, NEAR).reshape(tokens, WIDTH)

    dims = (micro, length, states, rank)
    slab, flat = (length, 2 * micro, 128), (length, 2 * micro, states * 128)
    send_out = ((tokens, WIDTH), BF16)
    scratch = [slab, flat, flat, slab, (length, states, 2 * micro, 128), (length + 1, states, 2 * micro, 128),
               flat, flat, (states, 2 * micro, 128), slab, slab, slab, slab]
    shared = (x, side, cat, w_delta, const)
    send, core = call(
        functools.partial(tick_kernel, *dims, False), [send_out, (slab, F32)], scratch, *shared)
    cat_up = to_all(scattered_sum(send, NEAR).astype(BF16), NEAR).reshape(tokens, WIDTH)
    handed, = call(
        functools.partial(hand_kernel, *dims), [((tokens, channels), BF16)], [], cat_up, w_low, w_select, core)
    above = lax.ppermute(handed, "ly", [(1, 0)])

    send, core, dpre, rate_sum, end_sums = call(
        functools.partial(tick_kernel, *dims, True),
        [send_out, (slab, F32), ((tokens, channels), BF16), ((states, 2 * micro, 128), F32),
         ((2, 2 * micro, 128), F32)], scratch, *shared, above)
    down_cat = to_all(scattered_sum(send, NEAR).astype(BF16), NEAR).reshape(tokens, WIDTH)

    own = channels // replicas
    partials, = call(
        functools.partial(part_kernel, micro, replicas), [((replicas, own, 2 * rank + 128), BF16)],
        [(replicas, own, 128)], cat, down_cat, x, dpre, rate_sum, end_sums)
    got = exchange(partials, REPLICAS)
    grad, = call(
        functools.partial(order_kernel, *dims), [((tokens, channels), BF16)],
        [pltpu.SMEM((micro,), jnp.int32), pltpu.SemaphoreType.DMA((1,))],
        plan, down_cat, w_low, w_select, core, far=1)
    sums = call(
        total_kernel,
        [((own, rank), F32), ((rank // replicas, channels), F32), ((doubled // replicas, channels), F32),
         ((states // replicas, channels), F32), ((1, own), F32), ((1, own), F32)], [], got)
    return (grad.reshape(micro, length, channels), *sums[:4], sums[4].reshape(own), sums[5].reshape(own))


def solution(mesh):
    axes = ("ly", "yl", "zh", "x") + REPLICAS
    fine = Mesh(np.asarray(mesh.devices).reshape(2, 2, 4, 4, 4, 2), axes)
    section, dp = axes[:4], REPLICAS
    in_specs = (
        P(None, dp, section),
        P(None, dp, section),
        P(),
        P(section, None),
        P(None, section),
        P(None, section),
        P(None, section),
        P(section),
        P(section),
    )
    out_specs = (
        P(None, dp, section),
        P(section + dp, None),
        P(dp, section),
        P(dp, section),
        P(dp, section),
        P(section + dp),
        P(section + dp),
    )
    return jax.shard_map(per_device, mesh=fine, in_specs=in_specs, out_specs=out_specs, check_vma=False)
```

time: 169 us -> 162 us (0.959)
  blocking collectives: 97.2 us -> 107 us
  waiting for transfers between devices: 27.2 us -> 19 us
  starting transfers between devices: 25.9 us -> 19.4 us
  local copies, waits for them, and re-layouts: 5.89 us -> 0.84 us
  Pallas kernels: 11.1 us -> 14.3 us
    all_to_all x7 -> x9, blocking collectives: 97.2 us -> 107 us  [exchange(): return lax.all_to_all(blocks, axes, 0, 0)]
    all_to_all x3 -> x1, waiting for transfers between devices: 22 us -> 13.8 us  [exchange(): return lax.all_to_all(blocks, axes, 0, 0)]
    all_to_all x3 -> x1, starting transfers between devices: 22 us -> 18.1 us  [exchange(): return lax.all_to_all(blocks, axes, 0, 0)]
    pallas_call x5 -> x7, Pallas kernels: 11.1 us -> 14.3 us  [call(): pl.pallas_call(kernel, out_shape=[jax.ShapeDtypeStruct(*out) for out in o...]
    unnamed x24 -> x14, local copies, waits for them, and re-layouts: 3.84 us -> 0.69 us
    ppermute x3 -> x1, starting transfers between devices: 3.88 us -> 1.29 us  [per_device(): above = lax.ppermute(handed, 'ly', [(1, 0)])]
    broadcast_in_dim x6, local copies, waits for them, and re-layouts: 1.96 us -> 0.07 us  [to_all(): return exchange(jnp.broadcast_to(block[None], (count,) + block.shape), axes)]
    ppermute x3 -> x1, waiting for transfers between devices: 5.23 us -> 5.21 us  [per_device(): above = lax.ppermute(handed, 'ly', [(1, 0)])]
  transfers between devices with their start and end apart: 6 -> 2, of which waited for: 3 -> 2; matrix products, arithmetic and copies ran while one was open for 0% -> 0% of each run, Pallas kernels for 0% -> 1%
where the time goes in v2:
time: 162 us
  blocking collectives  107 us (66%)
  starting transfers between devices  19.4 us (12%)
  waiting for transfers between devices  19 us (12%)
  Pallas kernels  14.3 us (9%)
    all_to_all x9, blocking collectives, exchange(): return lax.all_to_all(blocks, axes, 0, 0)  107 us
    all_to_all x1, starting transfers between devices, exchange(): return lax.all_to_all(blocks, axes, 0, 0)  18.1 us
    pallas_call x7, Pallas kernels, call(): pl.pallas_call(kernel, out_shape=[jax.ShapeDtypeStruct(*out) for out in o...  14.3 us
    all_to_all x1, waiting for transfers between devices, exchange(): return lax.all_to_all(blocks, axes, 0, 0)  13.8 us
    ppermute x1, waiting for transfers between devices, per_device(): above = lax.ppermute(handed, 'ly', [(1, 0)])  5.21 us
  transfers between devices with their start and end apart: 2, of which 2 were waited for; matrix products, arithmetic and copies ran while one was open for 0% of the time, Pallas kernels for 1%

profile of v2, /device:TPU:1, one launch (start us, length us, event | category | flops | bytes accessed | tf_op | source)
XLA Modules:
  0.0 161.8 jit_solution(201885394230784433)
XLA Ops:
  0.6 1.9 %shard_map.144 = (bf16[128,640]{1,0:T(8,128)(2,1)}, f32[24,256]{1,0:T(8,128)}) custom-call(bf16[128,256]{1,0:T(8,128)(2,1)} %bitcast.18, bf16[32,256]{1,0:T(8,128)(2,1)} %ws_ref.3, bf16[256,512]{1,0:T(8,128)(2,1)} %wl_ref.3, f32[16,256]{1,0:T(8,128)} %rate_hbm.1, f32[1,256]{1,0:T(1,128)} %bitcast.29, f32[1,256]{1,0:T(1,128)} %bitcast.30), custom_call_target="tpu_custom_call" | custom-call | tf_op jit(solution)/shard_map/pallas_call | solution.py:293
  2.6 11.5 %all_to_all.50 = bf16[8,16,640]{2,1,0:T(8,128)(2,1)S(1)} all-to-all(bf16[8,16,640]{2,1,0:T(8,128)(2,1)} %bitcast.27), channel_id=1, replica_groups=mesh['ly'=2,'yl'=2,'zh'=4,'x'=4,'zl'=4,'core'=2] {'yl','x'}, dimensions={0} | all-to-all | bytes 327680 | tf_op jit(solution)/shard_map/all_to_all | solution.py:304
  14.1 26.7 %all_to_all.51 = bf16[4,16,640]{2,1,0:T(8,128)(2,1)S(1)} all-to-all(bf16[4,16,640]{2,1,0:T(8,128)(2,1)S(1)} %broadcast_in_dim.12), channel_id=1, replica_groups=mesh['ly'=2,'yl'=2,'zh'=4,'x'=4,'zl'=4,'core'=2] {'zh'}, dimensions={0} | all-to-all | bytes 163840 | tf_op jit(solution)/shard_map/all_to_all | solution.py:304
  40.8 0.1 slice.16
  40.9 0.1 pad_maximum_fusion
  41.0 0.0 copy-start.2
  41.0 0.0 copy-start.1
  41.0 0.0 copy-start.3
  41.0 0.0 copy-start.5
  41.0 8.1 %all_to_all.52 = bf16[8,16,640]{2,1,0:T(8,128)(2,1)S(1)} all-to-all(bf16[8,16,640]{2,1,0:T(8,128)(2,1)S(1)} %broadcast_in_dim.13), channel_id=1, replica_groups=mesh['ly'=2,'yl'=2,'zh'=4,'x'=4,'zl'=4,'core'=2] {'yl','x'}, dimensions={0} | all-to-all | bytes 327680 | tf_op jit(solution)/shard_map/all_to_all | solution.py:304
  49.2 0.0 copy-done.2
  49.2 0.0 copy-done.1
  49.2 0.0 copy-done.3
  49.2 0.0 copy-done.5
  49.2 4.1 %shard_map.145 = (bf16[128,640]{1,0:T(8,128)(2,1)S(1)}, f32[32,8,128]{2,1,0:T(8,128)S(1)}) custom-call(bf16[128,256]{1,0:T(8,128)(2,1)S(1)} %bitcast.19, bf16[128,256]{1,0:T(8,128)(2,1)S(1)} %bitcast.23, bf16[128,640]{1,0:T(8,128)(2,1)S(1)} %bitcast.13, bf16[512,256]{1,0:T(8,128)(2,1)S(1)} %copy-done.2, f32[24,256]{1,0:T(8,128)S(1)} %copy-done.5), custom_call_target="tpu_custom_call" | custom-call | tf_op jit(solution)/shard_map/pallas_call | solution.py:293
  53.3 8.0 %all_to_all.53 = bf16[8,16,640]{2,1,0:T(8,128)(2,1)S(1)} all-to-all(bf16[8,16,640]{2,1,0:T(8,128)(2,1)S(1)} %bitcast.26), channel_id=1, replica_groups=mesh['ly'=2,'yl'=2,'zh'=4,'x'=4,'zl'=4,'core'=2] {'yl','x'}, dimensions={0} | all-to-all | bytes 327680 | tf_op jit(solution)/shard_map/all_to_all | solution.py:304
  61.3 14.2 %all_to_all.54 = bf16[4,16,640]{2,1,0:T(8,128)(2,1)S(1)} all-to-all(bf16[4,16,640]{2,1,0:T(8,128)(2,1)S(1)} %broadcast_in_dim.14), channel_id=1, replica_groups=mesh['ly'=2,'yl'=2,'zh'=4,'x'=4,'zl'=4,'core'=2] {'zh'}, dimensions={0} | all-to-all | bytes 163840 | tf_op jit(solution)/shard_map/all_to_all | solution.py:304
  75.5 0.0 copy-start
  75.5 0.0 copy-start.4
  75.5 8.1 %all_to_all.55 = bf16[8,16,640]{2,1,0:T(8,128)(2,1)S(1)} all-to-all(bf16[8,16,640]{2,1,0:T(8,128)(2,1)S(1)} %broadcast_in_dim.15), channel_id=1, replica_groups=mesh['ly'=2,'yl'=2,'zh'=4,'x'=4,'zl'=4,'core'=2] {'yl','x'}, dimensions={0} | all-to-all | bytes 327680 | tf_op jit(solution)/shard_map/all_to_all | solution.py:304
  83.7 0.0 copy-done
  83.7 0.0 copy-done.4
  83.7 0.7 shard_map.146
  84.4 1.3 collective-permute-start
  85.7 5.2 %collective-permute-done.refs_5_ = bf16[128,256]{1,0:T(8,128)(2,1)S(1)} collective-permute-done((bf16[128,256]{1,0:T(8,128)(2,1)S(1)}, bf16[128,256]{1,0:T(8,128)(2,1)S(1)}, u32[]{:S(2)}, u32[]{:S(2)}) %collective-permute-start) | collective-permute-done | bytes 65568 | tf_op jit(solution)/shard_map/ppermute | solution.py:354
  90.9 4.3 %shard_map.147 = (bf16[128,640]{1,0:T(8,128)(2,1)S(1)}, f32[32,8,128]{2,1,0:T(8,128)S(1)}, bf16[128,256]{1,0:T(8,128)(2,1)S(1)}, f32[16,8,128]{2,1,0:T(8,128)S(1)}, f32[2,8,128]{2,1,0:T(8,128)S(1)}) custom-call(bf16[128,256]{1,0:T(8,128)(2,1)S(1)} %bitcast.20, bf16[128,256]{1,0:T(8,128)(2,1)S(1)} %bitcast.24, bf16[128,640]{1,0:T(8,128)(2,1)S(1)} %bitcast.14, ...), custom_call_target="tpu_custom_call" | custom-call | tf_op jit(solution)/shard_map/pallas_call | solution.py:293
  95.3 8.2 %all_to_all.56 = bf16[8,16,640]{2,1,0:T(8,128)(2,1)S(1)} all-to-all(bf16[8,16,640]{2,1,0:T(8,128)(2,1)S(1)} %bitcast.25), channel_id=1, replica_groups=mesh['ly'=2,'yl'=2,'zh'=4,'x'=4,'zl'=4,'core'=2] {'yl','x'}, dimensions={0} | all-to-all | bytes 327680 | tf_op jit(solution)/shard_map/all_to_all | solution.py:304
  103.5 14.3 %all_to_all.57 = bf16[4,16,640]{2,1,0:T(8,128)(2,1)S(1)} all-to-all(bf16[4,16,640]{2,1,0:T(8,128)(2,1)S(1)} %broadcast_in_dim.16), channel_id=1, replica_groups=mesh['ly'=2,'yl'=2,'zh'=4,'x'=4,'zl'=4,'core'=2] {'zh'}, dimensions={0} | all-to-all | bytes 163840 | tf_op jit(solution)/shard_map/all_to_all | solution.py:304
  117.9 8.0 %all_to_all.58 = bf16[8,16,640]{2,1,0:T(8,128)(2,1)S(1)} all-to-all(bf16[8,16,640]{2,1,0:T(8,128)(2,1)S(1)} %broadcast_in_dim.17), channel_id=1, replica_groups=mesh['ly'=2,'yl'=2,'zh'=4,'x'=4,'zl'=4,'core'=2] {'yl','x'}, dimensions={0} | all-to-all | bytes 327680 | tf_op jit(solution)/shard_map/all_to_all | solution.py:304
  125.9 1.1 shard_map.149
  127.0 18.1 %all-to-all-start.9 = ((bf16[8,32,1152]{2,1,0:T(8,128)(2,1)}), bf16[8,32,1152]{2,1,0:T(8,128)(2,1)S(1)}, u32[]{:S(2)}, u32[]{:S(2)}) async-start(bf16[8,32,1152]{2,1,0:T(8,128)(2,1)} %shard_map.149), calls=%async_computation.9 | async-start | bytes 1179648 | tf_op jit(solution)/shard_map/all_to_all | solution.py:304
  145.2 0.0 copy-start.6
  145.2 0.7 copy-done.6
  145.8 1.4 shard_map.148
  147.2 13.8 %all-to-all-done.9.got_ref = bf16[8,32,1152]{2,1,0:T(8,128)(2,1)S(1)} async-done(((bf16[8,32,1152]{2,1,0:T(8,128)(2,1)}), bf16[8,32,1152]{2,1,0:T(8,128)(2,1)S(1)}, u32[]{:S(2)}, u32[]{:S(2)}) %all-to-all-start.9) | async-done | bytes 589856 | tf_op jit(solution)/shard_map/all_to_all | solution.py:304
  161.1 0.7 shard_map.150
  (15 shorter events, 0.2 us)
Async XLA Ops:
  41.0 8.2 %copy-start.2 = (bf16[512,256]{1,0:T(8,128)(2,1)S(1)}, bf16[512,256]{1,0:T(8,128)(2,1)}, u32[]{:S(2)}) copy-start(bf16[512,256]{1,0:T(8,128)(2,1)} %refs_3_.3) | copy-start | bytes 786436
  41.0 8.2 %copy-start.1 = (bf16[4,32,256]{2,1,0:T(8,128)(2,1)S(1)}, bf16[4,32,256]{2,1,0:T(8,128)(2,1)}, u32[]{:S(2)}) copy-start(bf16[4,32,256]{2,1,0:T(8,128)(2,1)} %param.9) | copy-start | bytes 196612
  41.0 8.2 %copy-start.3 = (bf16[4,32,256]{2,1,0:T(8,128)(2,1)S(1)}, bf16[4,32,256]{2,1,0:T(8,128)(2,1)}, u32[]{:S(2)}) copy-start(bf16[4,32,256]{2,1,0:T(8,128)(2,1)} %param.10) | copy-start | bytes 196612
  41.0 8.2 %copy-start.5 = (f32[24,256]{1,0:T(8,128)S(1)}, f32[24,256]{1,0:T(8,128)}, u32[]{:S(2)}) copy-start(f32[24,256]{1,0:T(8,128)} %get-tuple-element.23.refs_4_) | copy-start | bytes 73732
  75.5 8.2 %copy-start = (bf16[256,512]{1,0:T(8,128)(2,1)S(1)}, bf16[256,512]{1,0:T(8,128)(2,1)}, u32[]{:S(2)}) copy-start(bf16[256,512]{1,0:T(8,128)(2,1)} %wl_ref.3) | copy-start | bytes 786436
  75.5 8.2 %copy-start.4 = (bf16[32,256]{1,0:T(8,128)(2,1)S(1)}, bf16[32,256]{1,0:T(8,128)(2,1)}, u32[]{:S(2)}) copy-start(bf16[32,256]{1,0:T(8,128)(2,1)} %ws_ref.3) | copy-start | bytes 49156
  84.4 6.5 %collective-permute-start = (bf16[128,256]{1,0:T(8,128)(2,1)S(1)}, bf16[128,256]{1,0:T(8,128)(2,1)S(1)}, u32[]{:S(2)}, u32[]{:S(2)}) collective-permute-start(bf16[128,256]{1,0:T(8,128)(2,1)S(1)} %shard_map.146), channel_id=1, source_target_pairs={{256,0},{257,1},{258,2},{259,3},{260,4},{261,5},{262,6},{263,7},{2... | collective-permute-start | bytes 196616 | tf_op jit(solution)/shard_map/ppermute | solution.py:354
  127.0 34.0 %all-to-all-start.9 = ((bf16[8,32,1152]{2,1,0:T(8,128)(2,1)}), bf16[8,32,1152]{2,1,0:T(8,128)(2,1)S(1)}, u32[]{:S(2)}, u32[]{:S(2)}) async-start(bf16[8,32,1152]{2,1,0:T(8,128)(2,1)} %shard_map.149), calls=%async_computation.9 | async-start | bytes 1179648 | tf_op jit(solution)/shard_map/all_to_all | solution.py:304
  145.2 0.7 copy-start.6

commit v3 on v2

--- a/solution.py
+++ b/solution.py
@@ -19,7 +19,7 @@
 VMEM_LIMIT = 48 * 1024 * 1024
 PROJECT_LIMIT = 60 * 1024 * 1024
 SEL_ROWS = 8
-UNROLL = 1
+UNROLL = 32
 
 
 def dot(a, b, dims=NN):
@@ -40,15 +40,10 @@
     return one_hot((r % micro) * length + r // (2 * micro) == c)
 
 
-def gather_matrix(micro, length, order=None):
+def gather_matrix(micro, length):
     shape = (micro * length, 2 * micro * length)
     r, c = iota(shape, 0), iota(shape, 1)
-    which = r // length
-    if order is not None:
-        slot, which = which, jnp.zeros(shape, jnp.int32)
-        for j in range(micro):
-            which = jnp.where(slot == j, order[j], which)
-    return one_hot(which * length + r % length == (c % micro) * length + c // (2 * micro))
+    return one_hot(r == (c % micro) * length + c // (2 * micro))
 
 
 def first_half(rows, micro, lanes=128):
@@ -92,21 +87,45 @@
     const_ref[states + 1:states + 2, :] = skip_ref[...]
 
 
-def forward(micro, length, states, rank, x, cat, wd, const_ref, A, H, Bv, Cv, R, X, D, DX, SG):
+def state_lanes(states):
+    shape = (2 * states, 2 * states * 128)
+    return one_hot(iota(shape, 1) // 128 == iota(shape, 0))
+
+
+def grouped_sums(value, count, group=8):
+    shape = (group * 128, group)
+    ones = one_hot(iota(shape, 0) // 128 == iota(shape, 1))
+    parts = [dot(value[:, at * 128:(at + group) * 128], ones) for at in range(0, count, group)]
+    return jnp.concatenate(parts, axis=1)
+
+
+def put_rows(ref, micro, value):
+    length = value.shape[0] // micro
+    for k in range(2):
+        for m in range(micro):
+            ref[pl.ds(k * micro + m, length, stride=2 * micro), :] = value[m * length:(m + 1) * length, k * 128:(k + 1) * 128]
+
+
+def get_rows(ref, micro):
+    length = ref.shape[0] // (2 * micro)
+    return jnp.concatenate([jnp.concatenate(
+        [ref[pl.ds(k * micro + m, length, stride=2 * micro), :] for m in range(micro)], axis=0)
+        for k in range(2)], axis=1)
+
+
+def forward(micro, length, states, rank, x, cat, wd, const_ref, DP, A, H, BC, R, X, D, DX, SG):
     rows = 2 * micro * length
     doubled = 2 * states
     half = first_half(rows, micro)
     lower = first_half(2 * micro, micro)
     T = spread_matrix(micro, length)
     slabs = (length, 2 * micro, 128)
-    cat8 = dot(T, cat).astype(BF16)
+    cat8 = dot(T, cat[:, rank:rank + 2 * doubled]).astype(BF16)
     x8 = pick_half(half, dot(T, x)).reshape(slabs)
-    wide_shape = (2 * doubled, states * 128)
-    lane, row = iota(wide_shape, 1) // 128, iota(wide_shape, 0) % doubled
-    terms = cat8[:, rank:rank + 2 * doubled]
-    Bv[...] = dot(terms, one_hot(lane == row)).reshape(length, 2 * micro, states * 128)
-    Cv[...] = dot(terms, one_hot(lane + states == row)).reshape(length, 2 * micro, states * 128)
-    pre8 = pick_half(half, dot(cat8[:, :rank], wd)).reshape(slabs)
+    pick = state_lanes(states)
+    BC[...] = dot(cat8, jnp.concatenate([pick, pick], axis=0)).reshape(BC.shape)
+    put_rows(DP, micro, dot(cat[:, :rank], wd))
+    pre8 = DP[...].reshape(slabs)
     pre8 = pre8 + pick_half(lower, const_ref[states:states + 1, :])[None]
     step8 = jax.nn.softplus(pre8)
     X[...] = x8
@@ -123,7 +142,7 @@
         out = []
         for n in range(states):
             a = jnp.exp(-(d * R[n]))
-            h_n = a * h[n] + dx * Bv[t, :, n * 128:(n + 1) * 128]
+            h_n = a * h[n] + dx * BC[t, :, n * 128:(n + 1) * 128]
             A[t, n] = a
             H[t + 1, n] = h_n
             out.append(h_n)
@@ -132,8 +151,8 @@
     lax.fori_loop(0, length, ahead, (zero,) * states, unroll=UNROLL)
 
 
-def backward(micro, length, states, rank, sums, wd, const_ref, G, A, H, Bv, Cv, R, X, D, DX, SG,
-             send_ref, core_ref, Pb, Pc, DP):
+def backward(micro, length, states, rank, sums, wd, const_ref, G, A, H, BC, R, X, D, DX, SG,
+             send_ref, core_ref, products, DP, C):
     rows = 2 * micro * length
     doubled = 2 * states
     half = first_half(rows, micro)
@@ -141,45 +160,50 @@
     skip8 = pick_half(first_half(2 * micro, micro), const_ref[states + 1:states + 2, :])
 
     def back(i, carry):
-        later, acc, bias_acc, skip_acc = carry
-        t = length - 1 - i
-        d, dx, g, xv = D[t], DX[t], G[t], X[t]
+        later, bias_acc, skip_acc = carry
+        pair = length // 2 - 1 - i
+        times = (2 * pair, 2 * pair + 1)
+        d, dx, g, xv = ([ref[t] for t in times] for ref in (D, DX, G, X))
         u, w = [zero, zero], [zero, zero]
-        passed, added = [], []
+        passed = []
         for n in range(states):
-            at = slice(n * 128, (n + 1) * 128)
-            lam = Cv[t, :, at] * g + later[n]
-            u[n % 2] = u[n % 2] + lam * Bv[t, :, at]
-            Pc[t, :, at] = g * H[t + 1, n]
-            Pb[t, :, at] = lam * dx
-            through = A[t, n] * lam
-            q = through * H[t, n]
-            w[n % 2] = w[n % 2] + q * R[n]
+            rate = R[n]
+            b_at, c_at = (slice(at * 128, (at + 1) * 128) for at in (n, states + n))
+            h = [H[times[0] + k, n] for k in range(3)]
+            lam, q = [None, None], [None, None]
+            through = later[n]
+            for k in (1, 0):
+                lam[k] = BC[times[k], :, c_at] * g[k] + through
+                through = A[times[k], n] * lam[k]
+                q[k] = through * h[k]
+                u[k] = u[k] + lam[k] * BC[times[k], :, b_at]
+                w[k] = w[k] + q[k] * rate
+            for at, value in ((b_at, [lam[k] * dx[k] for k in range(2)]),
+                              (c_at, [g[k] * h[k + 1] for k in range(2)])):
+                products[pair, :, at] = jnp.concatenate(value, axis=0).astype(BF16)
             passed.append(through)
-            if sums:
-                added.append(acc[n] + d * q)
-        u, w = u[0] + u[1], w[0] + w[1]
-        dpre = (u * xv - w) * SG[t]
-        DP[t] = dpre
-        core_ref[t] = g + (u * d + skip8 * g)
-        if sums:
-            bias_acc, skip_acc = bias_acc + dpre, skip_acc + g * xv
-        return tuple(passed), tuple(added), bias_acc, skip_acc
-
-    start = ((zero,) * states, (zero,) * (states if sums else 0), zero, zero)
-    _, acc, bias_acc, skip_acc = lax.fori_loop(0, length, back, start, unroll=UNROLL)
+            if sums is not None:
+                sums[n] = sums[n] + (d[0] * q[0] + d[1] * q[1])
+        for k in range(2):
+            dpre = (u[k] * xv[k] - w[k]) * SG[times[k]]
+            DP[pl.ds(times[k] * 2 * micro, 2 * micro), :] = dpre
+            C[pl.ds(times[k] * 2 * micro, 2 * micro), :] = g[k] + (u[k] * d[k] + skip8 * g[k])
+            if sums is not None:
+                bias_acc, skip_acc = bias_acc + dpre, skip_acc + g[k] * xv[k]
+        return tuple(passed), bias_acc, skip_acc
+
+    if sums is not None:
+        sums[...] = jnp.zeros(sums.shape, F32)
+    start = ((zero,) * states, zero, zero)
+    _, bias_acc, skip_acc = lax.fori_loop(0, length // 2, back, start, unroll=16)
     S = gather_matrix(micro, length)
-    dpre_half = dot(S, two_halves(half, DP[...].reshape(rows, 128)).astype(BF16)).astype(BF16)
+    core_ref[...] = get_rows(C, micro)
+    dpre_half = get_rows(DP, micro).astype(BF16)
     send_ref[:, :rank] = dot(dpre_half, wd, NT).astype(BF16)
-    sum_shape = (states * 128, doubled)
-    depth, place = iota(sum_shape, 0) // 128, iota(sum_shape, 1)
-    b_flat = Pb[...].reshape(rows, states * 128).astype(BF16)
-    c_flat = Pc[...].reshape(rows, states * 128).astype(BF16)
-    ds8 = dot(b_flat, one_hot(depth == place)) + dot(c_flat, one_hot(depth + states == place))
-    high, low = two_terms(ds8)
+    high, low = two_terms(grouped_sums(products[...].reshape(rows, doubled * 128), doubled))
     send_ref[:, rank:] = jnp.zeros((micro * length, WIDTH - rank), BF16)
     send_ref[:, rank:rank + doubled] = (dot(S, high) + dot(S, low)).astype(BF16)
-    return dpre_half, acc, bias_acc, skip_acc
+    return dpre_half, bias_acc, skip_acc
 
 
 def tick_kernel(micro, length, states, rank, from_above, *refs):
@@ -188,7 +212,7 @@
         above_ref, send_ref, core_ref, dpre_ref, rate_out, ends_ref, *refs = refs
     else:
         send_ref, core_ref, *refs = refs
-    G, Pb, Pc, DP, *state = refs
+    G, products, DP, C, *state = refs
     rows = 2 * micro * length
     channels = x_ref.shape[1]
     half = first_half(rows, micro)
@@ -197,36 +221,31 @@
     if from_above:
         g8 = g8 + pick_half(half, dot(T, above_ref[...]))
     G[...] = g8.reshape(G.shape)
-    forward(micro, length, states, rank, x_ref[...], cat_ref[...], wd_ref[...], const_ref, *state)
-    dpre_half, acc, bias_acc, skip_acc = backward(
-        micro, length, states, rank, from_above, wd_ref[...], const_ref, G, *state, send_ref, core_ref, Pb, Pc, DP)
+    forward(micro, length, states, rank, x_ref[...], cat_ref[...], wd_ref[...], const_ref, DP, *state)
+    dpre_half, bias_acc, skip_acc = backward(
+        micro, length, states, rank, rate_out if from_above else None, wd_ref[...], const_ref, G, *state, send_ref, core_ref, products, DP, C)
     if from_above:
         dpre_ref[...] = dpre_half
-        for n in range(states):
-            rate_out[n] = acc[n]
         ends_ref[0] = bias_acc
         ends_ref[1] = skip_acc
 
 
-def layer_grad(micro, length, states, rank, cat_ref, wl_ref, ws_ref, core_ref):
-    rows = 2 * micro * length
-    half = first_half(rows, micro)
-    cat8 = dot(spread_matrix(micro, length), cat_ref[...]).astype(BF16)
-    wide = dot(cat8[:, :rank], wl_ref[...], NT) + dot(cat8[:, rank:rank + 2 * states], ws_ref[...])
-    return two_halves(half, core_ref[...].reshape(rows, 128) + pick_half(half, wide)).astype(BF16)
-
-
-def hand_kernel(micro, length, states, rank, cat_ref, wl_ref, ws_ref, core_ref, grad_ref):
-    grad8 = layer_grad(micro, length, states, rank, cat_ref, wl_ref, ws_ref, core_ref)
-    grad_ref[...] = dot(gather_matrix(micro, length), grad8).astype(BF16)
-
-
-def order_kernel(micro, length, states, rank, plan_hbm, cat_ref, wl_ref, ws_ref, core_ref, grad_ref, plan_ref, sems):
+def layer_grad(cat_ref, wl_ref, ws_ref, core_ref):
+    rank, doubled = wl_ref.shape[1], ws_ref.shape[0]
+    value = core_ref[...] + dot(cat_ref[:, :rank], wl_ref[...], NT)
+    return (value + dot(cat_ref[:, rank:rank + doubled], ws_ref[...])).astype(BF16)
+
+
+def hand_kernel(cat_ref, wl_ref, ws_ref, core_ref, grad_ref):
+    grad_ref[...] = layer_grad(cat_ref, wl_ref, ws_ref, core_ref)
+
+
+def order_kernel(plan_hbm, cat_ref, wl_ref, ws_ref, core_ref, grad_ref, held, plan_ref, sems):
     copies = fetch((plan_hbm,), (plan_ref,), sems)
-    grad8 = layer_grad(micro, length, states, rank, cat_ref, wl_ref, ws_ref, core_ref)
+    held[...] = layer_grad(cat_ref, wl_ref, ws_ref, core_ref).reshape(held.shape)
     copies[0].wait()
-    S = gather_matrix(micro, length, [plan_ref[j] for j in range(micro)])
-    grad_ref[...] = dot(S, grad8).astype(BF16)
+    for j in range(grad_ref.shape[0]):
+        grad_ref[j] = held[plan_ref[j]]
 
 
 def part_kernel(micro, replicas, cat_ref, down_ref, x_ref, dpre_ref, rate_ref, ends_ref, send_ref, small):
@@ -341,21 +360,22 @@
     cat = to_all(packed, NEAR).reshape(tokens, WIDTH)
 
     dims = (micro, length, states, rank)
-    slab, flat = (length, 2 * micro, 128), (length, 2 * micro, states * 128)
+    slab, rows_all = (length, 2 * micro, 128), 2 * tokens
     send_out = ((tokens, WIDTH), BF16)
-    scratch = [slab, flat, flat, slab, (length, states, 2 * micro, 128), (length + 1, states, 2 * micro, 128),
-               flat, flat, (states, 2 * micro, 128), slab, slab, slab, slab]
+    scratch = [slab, pltpu.VMEM((length // 2, 4 * micro, doubled * 128), BF16), (rows_all, 128), (rows_all, 128),
+               (length, states, 2 * micro, 128), (length + 1, states, 2 * micro, 128),
+               (length, 2 * micro, doubled * 128), (states, 2 * micro, 128), slab, slab, slab, slab]
     shared = (x, side, cat, w_delta, const)
     send, core = call(
-        functools.partial(tick_kernel, *dims, False), [send_out, (slab, F32)], scratch, *shared)
+        functools.partial(tick_kernel, *dims, False), [send_out, ((tokens, channels), F32)], scratch, *shared)
     cat_up = to_all(scattered_sum(send, NEAR).astype(BF16), NEAR).reshape(tokens, WIDTH)
     handed, = call(
-        functools.partial(hand_kernel, *dims), [((tokens, channels), BF16)], [], cat_up, w_low, w_select, core)
+        hand_kernel, [((tokens, channels), BF16)], [], cat_up, w_low, w_select, core)
     above = lax.ppermute(handed, "ly", [(1, 0)])
 
     send, core, dpre, rate_sum, end_sums = call(
         functools.partial(tick_kernel, *dims, True),
-        [send_out, (slab, F32), ((tokens, channels), BF16), ((states, 2 * micro, 128), F32),
+        [send_out, ((tokens, channels), F32), ((tokens, channels), BF16), ((states, 2 * micro, 128), F32),
          ((2, 2 * micro, 128), F32)], scratch, *shared, above)
     down_cat = to_all(scattered_sum(send, NEAR).astype(BF16), NEAR).reshape(tokens, WIDTH)
 
@@ -365,14 +385,14 @@
         [(replicas, own, 128)], cat, down_cat, x, dpre, rate_sum, end_sums)
     got = exchange(partials, REPLICAS)
     grad, = call(
-        functools.partial(order_kernel, *dims), [((tokens, channels), BF16)],
-        [pltpu.SMEM((micro,), jnp.int32), pltpu.SemaphoreType.DMA((1,))],
+        order_kernel, [((micro, length, channels), BF16)],
+        [pltpu.VMEM((micro, length, channels), BF16), pltpu.SMEM((micro,), jnp.int32), pltpu.SemaphoreType.DMA((1,))],
         plan, down_cat, w_low, w_select, core, far=1)
     sums = call(
         total_kernel,
         [((own, rank), F32), ((rank // replicas, channels), F32), ((doubled // replicas, channels), F32),
          ((states // replicas, channels), F32), ((1, own), F32), ((1, own), F32)], [], got)
-    return (grad.reshape(micro, length, channels), *sums[:4], sums[4].reshape(own), sums[5].reshape(own))
+    return (grad, *sums[:4], sums[4].reshape(own), sums[5].reshape(own))
 
 
 def solution(mesh):

time: 162 us -> 160 us (0.988)
  Pallas kernels: 14.3 us -> 11.9 us
    pallas_call x7, Pallas kernels: 14.3 us -> 11.9 us  [call(): pl.pallas_call(kernel, out_shape=[jax.ShapeDtypeStruct(*out) for out in o...]
where the time goes in v3:
time: 160 us
  blocking collectives  107 us (67%)
  waiting for transfers between devices  19.7 us (12%)
  starting transfers between devices  19.4 us (12%)
  Pallas kernels  11.9 us (7%)
    all_to_all x9, blocking collectives, exchange(): return lax.all_to_all(blocks, axes, 0, 0)  107 us
    all_to_all x1, starting transfers between devices, exchange(): return lax.all_to_all(blocks, axes, 0, 0)  18.1 us
    all_to_all x1, waiting for transfers between devices, exchange(): return lax.all_to_all(blocks, axes, 0, 0)  14 us
    pallas_call x7, Pallas kernels, call(): pl.pallas_call(kernel, out_shape=[jax.ShapeDtypeStruct(*out) for out in o...  11.9 us
    ppermute x1, waiting for transfers between devices, per_device(): above = lax.ppermute(handed, 'ly', [(1, 0)])  5.63 us
  transfers between devices with their start and end apart: 2, of which 2 were waited for; matrix products, arithmetic and copies ran while one was open for 0% of the time, Pallas kernels for 1%

profile of v3, /device:TPU:1, one launch (start us, length us, event | category | flops | bytes accessed | tf_op | source)
XLA Modules:
  0.0 159.6 jit_solution(17872656556872968424)
XLA Ops:
  0.6 1.9 %shard_map.144 = (bf16[128,640]{1,0:T(8,128)(2,1)}, f32[24,256]{1,0:T(8,128)}) custom-call(bf16[128,256]{1,0:T(8,128)(2,1)} %bitcast.17, bf16[32,256]{1,0:T(8,128)(2,1)} %ws_ref.3, bf16[256,512]{1,0:T(8,128)(2,1)} %wl_ref.3, f32[16,256]{1,0:T(8,128)} %rate_hbm.1, f32[1,256]{1,0:T(1,128)} %bitcast.27, f32[1,256]{1,0:T(1,128)} %bitcast.28), custom_call_target="tpu_custom_call" | custom-call | tf_op jit(solution)/shard_map/pallas_call | solution.py:312
  2.6 11.5 %all_to_all.50 = bf16[8,16,640]{2,1,0:T(8,128)(2,1)S(1)} all-to-all(bf16[8,16,640]{2,1,0:T(8,128)(2,1)} %bitcast.26), channel_id=1, replica_groups=mesh['ly'=2,'yl'=2,'zh'=4,'x'=4,'zl'=4,'core'=2] {'yl','x'}, dimensions={0} | all-to-all | bytes 327680 | tf_op jit(solution)/shard_map/all_to_all | solution.py:323
  14.1 26.7 %all_to_all.51 = bf16[4,16,640]{2,1,0:T(8,128)(2,1)S(1)} all-to-all(bf16[4,16,640]{2,1,0:T(8,128)(2,1)S(1)} %broadcast_in_dim.12), channel_id=1, replica_groups=mesh['ly'=2,'yl'=2,'zh'=4,'x'=4,'zl'=4,'core'=2] {'zh'}, dimensions={0} | all-to-all | bytes 163840 | tf_op jit(solution)/shard_map/all_to_all | solution.py:323
  40.8 0.1 slice.16
  40.9 0.1 pad_maximum_fusion
  41.0 0.0 copy-start.2
  41.0 0.0 copy-start.1
  41.0 0.0 copy-start.3
  41.0 0.0 copy-start.5
  41.0 8.1 %all_to_all.52 = bf16[8,16,640]{2,1,0:T(8,128)(2,1)S(1)} all-to-all(bf16[8,16,640]{2,1,0:T(8,128)(2,1)S(1)} %broadcast_in_dim.13), channel_id=1, replica_groups=mesh['ly'=2,'yl'=2,'zh'=4,'x'=4,'zl'=4,'core'=2] {'yl','x'}, dimensions={0} | all-to-all | bytes 327680 | tf_op jit(solution)/shard_map/all_to_all | solution.py:323
  49.2 0.0 copy-done.2
  49.2 0.0 copy-done.1
  49.2 0.0 copy-done.3
  49.2 0.0 copy-done.5
  49.2 3.2 %shard_map.145 = (bf16[128,640]{1,0:T(8,128)(2,1)S(1)}, f32[128,256]{1,0:T(8,128)S(1)}) custom-call(bf16[128,256]{1,0:T(8,128)(2,1)S(1)} %bitcast.18, bf16[128,256]{1,0:T(8,128)(2,1)S(1)} %bitcast.22, bf16[128,640]{1,0:T(8,128)(2,1)S(1)} %bitcast.12, bf16[512,256]{1,0:T(8,128)(2,1)S(1)} %copy-done.2, f32[24,256]{1,0:T(8,128)S(1)} %copy-done.5), custom_call_target="tpu_custom_call" | custom-call | tf_op jit(solution)/shard_map/pallas_call | solution.py:312
  52.4 8.0 %all_to_all.53 = bf16[8,16,640]{2,1,0:T(8,128)(2,1)S(1)} all-to-all(bf16[8,16,640]{2,1,0:T(8,128)(2,1)S(1)} %bitcast.25), channel_id=1, replica_groups=mesh['ly'=2,'yl'=2,'zh'=4,'x'=4,'zl'=4,'core'=2] {'yl','x'}, dimensions={0} | all-to-all | bytes 327680 | tf_op jit(solution)/shard_map/all_to_all | solution.py:323
  60.4 14.2 %all_to_all.54 = bf16[4,16,640]{2,1,0:T(8,128)(2,1)S(1)} all-to-all(bf16[4,16,640]{2,1,0:T(8,128)(2,1)S(1)} %broadcast_in_dim.14), channel_id=1, replica_groups=mesh['ly'=2,'yl'=2,'zh'=4,'x'=4,'zl'=4,'core'=2] {'zh'}, dimensions={0} | all-to-all | bytes 163840 | tf_op jit(solution)/shard_map/all_to_all | solution.py:323
  74.6 0.0 copy-start
  74.6 0.0 copy-start.4
  74.7 8.1 %all_to_all.55 = bf16[8,16,640]{2,1,0:T(8,128)(2,1)S(1)} all-to-all(bf16[8,16,640]{2,1,0:T(8,128)(2,1)S(1)} %broadcast_in_dim.15), channel_id=1, replica_groups=mesh['ly'=2,'yl'=2,'zh'=4,'x'=4,'zl'=4,'core'=2] {'yl','x'}, dimensions={0} | all-to-all | bytes 327680 | tf_op jit(solution)/shard_map/all_to_all | solution.py:323
  82.8 0.0 copy-done
  82.8 0.0 copy-done.4
  82.8 0.2 shard_map.146
  83.0 1.3 collective-permute-start
  84.3 5.6 %collective-permute-done.refs_5_ = bf16[128,256]{1,0:T(8,128)(2,1)S(1)} collective-permute-done((bf16[128,256]{1,0:T(8,128)(2,1)S(1)}, bf16[128,256]{1,0:T(8,128)(2,1)S(1)}, u32[]{:S(2)}, u32[]{:S(2)}) %collective-permute-start) | collective-permute-done | bytes 65568 | tf_op jit(solution)/shard_map/ppermute | solution.py:374
  90.0 3.4 %shard_map.147 = (bf16[128,640]{1,0:T(8,128)(2,1)S(1)}, f32[128,256]{1,0:T(8,128)S(1)}, bf16[128,256]{1,0:T(8,128)(2,1)S(1)}, f32[16,8,128]{2,1,0:T(8,128)S(1)}, f32[2,8,128]{2,1,0:T(8,128)S(1)}) custom-call(bf16[128,256]{1,0:T(8,128)(2,1)S(1)} %bitcast.19, bf16[128,256]{1,0:T(8,128)(2,1)S(1)} %bitcast.23, bf16[128,640]{1,0:T(8,128)(2,1)S(1)} %bitcast.13, ...), custom_call_target="tpu_custom_call" | custom-call | tf_op jit(solution)/shard_map/pallas_call | solution.py:312
  93.4 8.0 %all_to_all.56 = bf16[8,16,640]{2,1,0:T(8,128)(2,1)S(1)} all-to-all(bf16[8,16,640]{2,1,0:T(8,128)(2,1)S(1)} %bitcast.24), channel_id=1, replica_groups=mesh['ly'=2,'yl'=2,'zh'=4,'x'=4,'zl'=4,'core'=2] {'yl','x'}, dimensions={0} | all-to-all | bytes 327680 | tf_op jit(solution)/shard_map/all_to_all | solution.py:323
  101.5 14.2 %all_to_all.57 = bf16[4,16,640]{2,1,0:T(8,128)(2,1)S(1)} all-to-all(bf16[4,16,640]{2,1,0:T(8,128)(2,1)S(1)} %broadcast_in_dim.16), channel_id=1, replica_groups=mesh['ly'=2,'yl'=2,'zh'=4,'x'=4,'zl'=4,'core'=2] {'zh'}, dimensions={0} | all-to-all | bytes 163840 | tf_op jit(solution)/shard_map/all_to_all | solution.py:323
  115.7 8.0 %all_to_all.58 = bf16[8,16,640]{2,1,0:T(8,128)(2,1)S(1)} all-to-all(bf16[8,16,640]{2,1,0:T(8,128)(2,1)S(1)} %broadcast_in_dim.17), channel_id=1, replica_groups=mesh['ly'=2,'yl'=2,'zh'=4,'x'=4,'zl'=4,'core'=2] {'yl','x'}, dimensions={0} | all-to-all | bytes 327680 | tf_op jit(solution)/shard_map/all_to_all | solution.py:323
  123.7 1.1 shard_map.149
  124.8 18.1 %all-to-all-start.9 = ((bf16[8,32,1152]{2,1,0:T(8,128)(2,1)}), bf16[8,32,1152]{2,1,0:T(8,128)(2,1)S(1)}, u32[]{:S(2)}, u32[]{:S(2)}) async-start(bf16[8,32,1152]{2,1,0:T(8,128)(2,1)} %shard_map.149), calls=%async_computation.9 | async-start | bytes 1179648 | tf_op jit(solution)/shard_map/all_to_all | solution.py:323
  142.9 0.0 copy-start.6
  142.9 0.7 copy-done.6
  143.6 1.2 shard_map.148
  144.8 14.0 %all-to-all-done.9.got_ref = bf16[8,32,1152]{2,1,0:T(8,128)(2,1)S(1)} async-done(((bf16[8,32,1152]{2,1,0:T(8,128)(2,1)}), bf16[8,32,1152]{2,1,0:T(8,128)(2,1)S(1)}, u32[]{:S(2)}, u32[]{:S(2)}) %all-to-all-start.9) | async-done | bytes 589856 | tf_op jit(solution)/shard_map/all_to_all | solution.py:323
  158.9 0.7 shard_map.150
  (15 shorter events, 0.2 us)
Async XLA Ops:
  41.0 8.2 %copy-start.2 = (bf16[512,256]{1,0:T(8,128)(2,1)S(1)}, bf16[512,256]{1,0:T(8,128)(2,1)}, u32[]{:S(2)}) copy-start(bf16[512,256]{1,0:T(8,128)(2,1)} %refs_3_.3) | copy-start | bytes 786436
  41.0 8.2 %copy-start.1 = (bf16[4,32,256]{2,1,0:T(8,128)(2,1)S(1)}, bf16[4,32,256]{2,1,0:T(8,128)(2,1)}, u32[]{:S(2)}) copy-start(bf16[4,32,256]{2,1,0:T(8,128)(2,1)} %param.9) | copy-start | bytes 196612
  41.0 8.2 %copy-start.3 = (bf16[4,32,256]{2,1,0:T(8,128)(2,1)S(1)}, bf16[4,32,256]{2,1,0:T(8,128)(2,1)}, u32[]{:S(2)}) copy-start(bf16[4,32,256]{2,1,0:T(8,128)(2,1)} %param.10) | copy-start | bytes 196612
  41.0 8.2 %copy-start.5 = (f32[24,256]{1,0:T(8,128)S(1)}, f32[24,256]{1,0:T(8,128)}, u32[]{:S(2)}) copy-start(f32[24,256]{1,0:T(8,128)} %get-tuple-element.23.refs_4_) | copy-start | bytes 73732
  74.6 8.2 %copy-start = (bf16[256,512]{1,0:T(8,128)(2,1)S(1)}, bf16[256,512]{1,0:T(8,128)(2,1)}, u32[]{:S(2)}) copy-start(bf16[256,512]{1,0:T(8,128)(2,1)} %wl_ref.3) | copy-start | bytes 786436
  74.6 8.2 %copy-start.4 = (bf16[32,256]{1,0:T(8,128)(2,1)S(1)}, bf16[32,256]{1,0:T(8,128)(2,1)}, u32[]{:S(2)}) copy-start(bf16[32,256]{1,0:T(8,128)(2,1)} %ws_ref.3) | copy-start | bytes 49156
  83.0 6.9 %collective-permute-start = (bf16[128,256]{1,0:T(8,128)(2,1)S(1)}, bf16[128,256]{1,0:T(8,128)(2,1)S(1)}, u32[]{:S(2)}, u32[]{:S(2)}) collective-permute-start(bf16[128,256]{1,0:T(8,128)(2,1)S(1)} %shard_map.146), channel_id=1, source_target_pairs={{256,0},{257,1},{258,2},{259,3},{260,4},{261,5},{262,6},{263,7},{2... | collective-permute-start | bytes 196616 | tf_op jit(solution)/shard_map/ppermute | solution.py:374
  124.8 34.0 %all-to-all-start.9 = ((bf16[8,32,1152]{2,1,0:T(8,128)(2,1)}), bf16[8,32,1152]{2,1,0:T(8,128)(2,1)S(1)}, u32[]{:S(2)}, u32[]{:S(2)}) async-start(bf16[8,32,1152]{2,1,0:T(8,128)(2,1)} %shard_map.149), calls=%async_computation.9 | async-start | bytes 1179648 | tf_op jit(solution)/shard_map/all_to_all | solution.py:323
  142.9 0.7 copy-start.6

commit v4 on v3

--- a/solution.py
+++ b/solution.py
@@ -19,7 +19,7 @@
 VMEM_LIMIT = 48 * 1024 * 1024
 PROJECT_LIMIT = 60 * 1024 * 1024
 SEL_ROWS = 8
-UNROLL = 32
+TILE = 16
 
 
 def dot(a, b, dims=NN):
@@ -70,10 +70,10 @@
     return copies
 
 
-def project_kernel(x_hbm, ws_hbm, wl_hbm, rate_hbm, bias_hbm, skip_hbm, out_ref, const_ref,
-                   x_ref, ws_ref, wl_ref, rate_ref, bias_ref, skip_ref, sems):
-    copies = fetch((x_hbm, wl_hbm, ws_hbm, rate_hbm, bias_hbm, skip_hbm),
-                   (x_ref, wl_ref, ws_ref, rate_ref, bias_ref, skip_ref), sems)
+def project_kernel(x_hbm, ws_hbm, wl_hbm, rate_hbm, bias_hbm, skip_hbm, plan_hbm, out_ref, const_ref, order_ref,
+                   x_ref, ws_ref, wl_ref, rate_ref, bias_ref, skip_ref, plan_ref, sems):
+    copies = fetch((x_hbm, wl_hbm, ws_hbm, rate_hbm, bias_hbm, skip_hbm, plan_hbm),
+                   (x_ref, wl_ref, ws_ref, rate_ref, bias_ref, skip_ref, plan_ref), sems)
     rank, doubled, states = wl_ref.shape[1], ws_ref.shape[0], rate_ref.shape[0]
     const_ref[...] = jnp.zeros(const_ref.shape, F32)
     out_ref[:, rank:] = jnp.zeros((x_ref.shape[0], WIDTH - rank), BF16)
@@ -85,6 +85,8 @@
     const_ref[:states, :] = rate_ref[...]
     const_ref[states:states + 1, :] = bias_ref[...]
     const_ref[states + 1:states + 2, :] = skip_ref[...]
+    for j in range(plan_ref.shape[0]):
+        order_ref[j:j + 1, :] = jnp.full((1, order_ref.shape[1]), plan_ref[j], jnp.int32)
 
 
 def state_lanes(states):
@@ -148,7 +150,7 @@
             out.append(h_n)
         return tuple(out)
 
-    lax.fori_loop(0, length, ahead, (zero,) * states, unroll=UNROLL)
+    lax.fori_loop(0, length, ahead, (zero,) * states, unroll=length)
 
 
 def backward(micro, length, states, rank, sums, wd, const_ref, G, A, H, BC, R, X, D, DX, SG,
@@ -195,7 +197,7 @@
     if sums is not None:
         sums[...] = jnp.zeros(sums.shape, F32)
     start = ((zero,) * states, zero, zero)
-    _, bias_acc, skip_acc = lax.fori_loop(0, length // 2, back, start, unroll=16)
+    _, bias_acc, skip_acc = lax.fori_loop(0, length // 2, back, start, unroll=length // 2)
     S = gather_matrix(micro, length)
     core_ref[...] = get_rows(C, micro)
     dpre_half = get_rows(DP, micro).astype(BF16)
@@ -240,24 +242,16 @@
     grad_ref[...] = layer_grad(cat_ref, wl_ref, ws_ref, core_ref)
 
 
-def order_kernel(plan_hbm, cat_ref, wl_ref, ws_ref, core_ref, grad_ref, held, plan_ref, sems):
-    copies = fetch((plan_hbm,), (plan_ref,), sems)
-    held[...] = layer_grad(cat_ref, wl_ref, ws_ref, core_ref).reshape(held.shape)
-    copies[0].wait()
-    for j in range(grad_ref.shape[0]):
-        grad_ref[j] = held[plan_ref[j]]
-
-
-def part_kernel(micro, replicas, cat_ref, down_ref, x_ref, dpre_ref, rate_ref, ends_ref, send_ref, small):
-    states = rate_ref.shape[0]
-    channels, rank = x_ref.shape[1], (send_ref.shape[2] - 128) // 2
+def part_kernel(micro, order_ref, cat_ref, down_ref, x_ref, wl_ref, ws_ref, core_ref, dpre_ref, rate_ref, ends_ref,
+                send_ref, grad_ref, small):
+    cores, groups, tile, _ = send_ref.shape
+    replicas, states = cores * groups, rate_ref.shape[0]
+    channels, rank = wl_ref.shape
     own, deep, doubled = channels // replicas, rank // replicas, 2 * states
     share, rate_share = doubled // replicas, states // replicas
     x, down = x_ref[...], down_ref[...]
-    send_ref[:, :, :rank] = dot(x, down[:, :rank], TN).astype(BF16).reshape(replicas, own, rank)
-    delta = dot(cat_ref[:, :rank], dpre_ref[...], TN).astype(BF16).reshape(replicas, deep, channels)
-    send_ref[:, :, rank:rank + channels] = delta[:, :own]
-    send_ref[:, :, rank + channels:2 * rank] = delta[:, own:]
+    low = dot(x, down[:, :rank], TN).astype(BF16)
+    delta = dot(cat_ref[:, :rank], dpre_ref[...], TN).astype(BF16)
     select = dot(down[:, rank:rank + doubled], x, TN)
     lower = first_half(2 * micro, micro)
 
@@ -278,29 +272,48 @@
         row = row_of(ends_ref[k])
         for r in range(replicas):
             small[r, at + k:at + k + 1, :own] = row[:, r * own:(r + 1) * own]
-    send_ref[:, :, 2 * rank:] = small[...].astype(BF16)
+    for r in range(replicas):
+        to = (r % cores, r // cores)
+        for i in range(own // tile):
+            send_ref[*to, :, i * rank:(i + 1) * rank] = low[r * own + i * tile:r * own + (i + 1) * tile]
+        first = own // tile * rank
+        for i in range(deep // tile):
+            lanes = slice(first + i * channels, first + (i + 1) * channels)
+            send_ref[*to, :, lanes] = delta[r * deep + i * tile:r * deep + (i + 1) * tile]
+        send_ref[*to, :, first + deep // tile * channels:] = small[r].astype(BF16)
+    grad = layer_grad(down_ref, wl_ref, ws_ref, core_ref).astype(F32).reshape(grad_ref.shape)
+    for j in range(micro):
+        which = order_ref[j:j + 1, :]
+        value = grad[0]
+        for m in range(1, micro):
+            value = jnp.where(which == m, grad[m], value)
+        grad_ref[j] = value.astype(BF16)
 
 
 def total_kernel(got_ref, low_ref, delta_ref, sel_ref, rate_ref, bias_ref, skip_ref):
+    tile = got_ref.shape[1]
     own, rank = low_ref.shape
-    channels = delta_ref.shape[1]
-
-    def summed(lanes):
-        value = got_ref[0, :, lanes].astype(F32)
+    deep, channels = delta_ref.shape
+
+    def summed(start, lanes):
+        value = got_ref[0, :, start:start + lanes].astype(F32)
         for r in range(1, got_ref.shape[0]):
-            value = value + got_ref[r, :, lanes].astype(F32)
+            value = value + got_ref[r, :, start:start + lanes].astype(F32)
         return value
 
-    low_ref[...] = summed(slice(0, rank))
-    delta_ref[:own] = summed(slice(rank, rank + channels))
-    delta_ref[own:] = summed(slice(rank + channels, 2 * rank))
-    small = summed(slice(2 * rank, 2 * rank + 128))
+    for i in range(own // tile):
+        low_ref[i * tile:(i + 1) * tile] = summed(i * rank, rank)
+    first = own // tile * rank
+    for i in range(deep // tile):
+        delta_ref[i * tile:(i + 1) * tile] = summed(first + i * channels, channels)
+    small = summed(first + deep // tile * channels, 128)
     rows, share = sel_ref.shape[0], rate_ref.shape[0]
     for k in range(2):
-        sel_ref[:, k * 128:(k + 1) * 128] = small[k * rows:(k + 1) * rows]
+        lanes = slice(k * 128, (k + 1) * 128)
+        sel_ref[:, lanes] = small[k * rows:(k + 1) * rows]
         for n in range(share):
             at = SEL_ROWS + 2 * n + k
-            rate_ref[n:n + 1, k * 128:(k + 1) * 128] = small[at:at + 1]
+            rate_ref[n:n + 1, lanes] = small[at:at + 1]
     at = SEL_ROWS + 2 * share
     bias_ref[...] = small[at:at + 1, :own]
     skip_ref[...] = small[at + 1:at + 2, :own]
@@ -347,10 +360,11 @@
     side = side_grad.reshape(tokens, channels)
     bias, skip = delta_bias.reshape(1, channels), skip_gain.reshape(1, channels)
 
-    sources = (x, w_select, w_low, decay_rate, bias, skip)
-    part, const = call(
-        project_kernel, [((tokens, WIDTH), BF16), ((states + 8, channels), F32)],
-        [pltpu.VMEM(a.shape, a.dtype) for a in sources] + [pltpu.SemaphoreType.DMA((len(sources),))],
+    sources = (x, w_select, w_low, decay_rate, bias, skip, plan)
+    part, const, order = call(
+        project_kernel, [((tokens, WIDTH), BF16), ((states + 8, channels), F32), ((8, channels), jnp.int32)],
+        [pltpu.VMEM(a.shape, a.dtype) for a in sources[:-1]]
+        + [pltpu.SMEM(plan.shape, plan.dtype), pltpu.SemaphoreType.DMA((len(sources),))],
         *sources, far=len(sources), limit=PROJECT_LIMIT)
     summed = scattered_sum(part, NEAR)
     selected = summed[:, rank:rank + doubled]
@@ -379,18 +393,18 @@
          ((2, 2 * micro, 128), F32)], scratch, *shared, above)
     down_cat = to_all(scattered_sum(send, NEAR).astype(BF16), NEAR).reshape(tokens, WIDTH)
 
-    own = channels // replicas
-    partials, = call(
-        functools.partial(part_kernel, micro, replicas), [((replicas, own, 2 * rank + 128), BF16)],
-        [(replicas, own, 128)], cat, down_cat, x, dpre, rate_sum, end_sums)
-    got = exchange(partials, REPLICAS)
-    grad, = call(
-        order_kernel, [((micro, length, channels), BF16)],
-        [pltpu.VMEM((micro, length, channels), BF16), pltpu.SMEM((micro,), jnp.int32), pltpu.SemaphoreType.DMA((1,))],
-        plan, down_cat, w_low, w_select, core, far=1)
+    own, deep = channels // replicas, rank // replicas
+    lanes = own // TILE * rank + deep // TILE * channels + 128
+    groups, cores = (lax.axis_size(axis) for axis in REPLICAS)
+    partials, grad = call(
+        functools.partial(part_kernel, micro),
+        [((cores, groups, TILE, lanes), BF16), ((micro, length, channels), BF16)], [(replicas, TILE, 128)],
+        order, cat, down_cat, x, w_low, w_select, core, dpre, rate_sum, end_sums)
+    pairs = total(exchange(partials, "core")).astype(BF16)
+    got = exchange(pairs, "zl")
     sums = call(
         total_kernel,
-        [((own, rank), F32), ((rank // replicas, channels), F32), ((doubled // replicas, channels), F32),
+        [((own, rank), F32), ((deep, channels), F32), ((doubled // replicas, channels), F32),
          ((states // replicas, channels), F32), ((1, own), F32), ((1, own), F32)], [], got)
     return (grad, *sums[:4], sums[4].reshape(own), sums[5].reshape(own))
 

time: 160 us -> 156 us (0.975)
  blocking collectives: 107 us -> 136 us
  starting transfers between devices: 19.4 us -> 1.29 us
  waiting for transfers between devices: 19.7 us -> 5.64 us
    all_to_all x9 -> x11, blocking collectives: 107 us -> 136 us  [exchange(): return lax.all_to_all(blocks, axes, 0, 0)]
    all_to_all x1 -> x0, starting transfers between devices: 18.1 us -> none  [exchange(): return lax.all_to_all(blocks, axes, 0, 0)]
    all_to_all x1 -> x0, waiting for transfers between devices: 14 us -> none  [exchange(): return lax.all_to_all(blocks, axes, 0, 0)]
    pallas_call x7 -> x6, Pallas kernels: 11.9 us -> 10.5 us  [call(): pl.pallas_call(kernel, out_shape=[jax.ShapeDtypeStruct(*out) for out in o...]
  transfers between devices with their start and end apart: 2 -> 1, of which waited for: 2 -> 1; matrix products, arithmetic and copies ran while one was open for 0% -> 0% of each run, Pallas kernels for 1% -> 0%
where the time goes in v4:
time: 156 us; the launch traced here: 155 us
  blocking collectives  136 us (87%)
  Pallas kernels  10.5 us (7%)
  waiting for transfers between devices  5.64 us (4%)
    all_to_all x11, blocking collectives, exchange(): return lax.all_to_all(blocks, axes, 0, 0)  136 us
    pallas_call x6, Pallas kernels, call(): pl.pallas_call(kernel, out_shape=[jax.ShapeDtypeStruct(*out) for out in o...  10.5 us
    ppermute x1, waiting for transfers between devices, per_device(): above = lax.ppermute(handed, 'ly', [(1, 0)])  5.64 us
  transfers between devices with their start and end apart: 1, of which 1 were waited for; matrix products, arithmetic and copies ran while one was open for 0% of the time, Pallas kernels for 0%

profile of v4, /device:TPU:1, one launch (start us, length us, event | category | flops | bytes accessed | tf_op | source)
XLA Modules:
  0.0 155.2 jit_solution(1952363320402299602)
XLA Ops:
  0.6 1.9 %shard_map.144 = (bf16[128,640]{1,0:T(8,128)(2,1)}, f32[24,256]{1,0:T(8,128)}, s32[8,256]{1,0:T(8,128)}) custom-call(bf16[128,256]{1,0:T(8,128)(2,1)} %bitcast.15, bf16[32,256]{1,0:T(8,128)(2,1)} %ws_ref.3, bf16[256,512]{1,0:T(8,128)(2,1)} %wl_ref.3, f32[16,256]{1,0:T(8,128)} %rate_hbm.1, f32[1,256]{1,0:T(1,128)} %bitcast.26, f32[1,256]{1,0:T(1,128)} %bitcast.27, ...), custom_call_target="tpu_custom_call" | custom-call | tf_op jit(solution)/shard_map/pallas_call | solution.py:325
  2.6 11.5 %all_to_all.55 = bf16[8,16,640]{2,1,0:T(8,128)(2,1)S(1)} all-to-all(bf16[8,16,640]{2,1,0:T(8,128)(2,1)} %bitcast.25), channel_id=1, replica_groups=mesh['ly'=2,'yl'=2,'zh'=4,'x'=4,'zl'=4,'core'=2] {'yl','x'}, dimensions={0} | all-to-all | bytes 327680 | tf_op jit(solution)/shard_map/all_to_all | solution.py:336
  14.1 26.7 %all_to_all.56 = bf16[4,16,640]{2,1,0:T(8,128)(2,1)S(1)} all-to-all(bf16[4,16,640]{2,1,0:T(8,128)(2,1)S(1)} %broadcast_in_dim.12), channel_id=1, replica_groups=mesh['ly'=2,'yl'=2,'zh'=4,'x'=4,'zl'=4,'core'=2] {'zh'}, dimensions={0} | all-to-all | bytes 163840 | tf_op jit(solution)/shard_map/all_to_all | solution.py:336
  40.8 0.1 slice.16
  40.9 0.1 pad_maximum_fusion
  41.0 0.0 copy-start.1
  41.0 0.0 copy-start.2
  41.0 0.0 copy-start.3
  41.0 0.0 copy-start.5
  41.0 8.1 %all_to_all.57 = bf16[8,16,640]{2,1,0:T(8,128)(2,1)S(1)} all-to-all(bf16[8,16,640]{2,1,0:T(8,128)(2,1)S(1)} %broadcast_in_dim.13), channel_id=1, replica_groups=mesh['ly'=2,'yl'=2,'zh'=4,'x'=4,'zl'=4,'core'=2] {'yl','x'}, dimensions={0} | all-to-all | bytes 327680 | tf_op jit(solution)/shard_map/all_to_all | solution.py:336
  49.2 0.0 copy-done.1
  49.2 0.0 copy-done.2
  49.2 0.0 copy-done.3
  49.2 0.0 copy-done.5
  49.2 3.2 %shard_map.145 = (bf16[128,640]{1,0:T(8,128)(2,1)S(1)}, f32[128,256]{1,0:T(8,128)S(1)}) custom-call(bf16[128,256]{1,0:T(8,128)(2,1)S(1)} %bitcast.16, bf16[128,256]{1,0:T(8,128)(2,1)S(1)} %bitcast.21, bf16[128,640]{1,0:T(8,128)(2,1)S(1)} %bitcast.12, bf16[512,256]{1,0:T(8,128)(2,1)S(1)} %copy-done.1, f32[24,256]{1,0:T(8,128)S(1)} %copy-done.5), custom_call_target="tpu_custom_call" | custom-call | tf_op jit(solution)/shard_map/pallas_call | solution.py:325
  52.4 8.0 %all_to_all.58 = bf16[8,16,640]{2,1,0:T(8,128)(2,1)S(1)} all-to-all(bf16[8,16,640]{2,1,0:T(8,128)(2,1)S(1)} %bitcast.24), channel_id=1, replica_groups=mesh['ly'=2,'yl'=2,'zh'=4,'x'=4,'zl'=4,'core'=2] {'yl','x'}, dimensions={0} | all-to-all | bytes 327680 | tf_op jit(solution)/shard_map/all_to_all | solution.py:336
  60.4 14.2 %all_to_all.59 = bf16[4,16,640]{2,1,0:T(8,128)(2,1)S(1)} all-to-all(bf16[4,16,640]{2,1,0:T(8,128)(2,1)S(1)} %broadcast_in_dim.14), channel_id=1, replica_groups=mesh['ly'=2,'yl'=2,'zh'=4,'x'=4,'zl'=4,'core'=2] {'zh'}, dimensions={0} | all-to-all | bytes 163840 | tf_op jit(solution)/shard_map/all_to_all | solution.py:336
  74.6 0.0 copy-start
  74.7 0.0 copy-start.4
  74.7 8.1 %all_to_all.60 = bf16[8,16,640]{2,1,0:T(8,128)(2,1)S(1)} all-to-all(bf16[8,16,640]{2,1,0:T(8,128)(2,1)S(1)} %broadcast_in_dim.15), channel_id=1, replica_groups=mesh['ly'=2,'yl'=2,'zh'=4,'x'=4,'zl'=4,'core'=2] {'yl','x'}, dimensions={0} | all-to-all | bytes 327680 | tf_op jit(solution)/shard_map/all_to_all | solution.py:336
  82.8 0.0 copy-done
  82.8 0.0 copy-done.4
  82.8 0.2 shard_map.146
  83.1 1.3 collective-permute-start
  84.4 5.6 %collective-permute-done.refs_5_ = bf16[128,256]{1,0:T(8,128)(2,1)S(1)} collective-permute-done((bf16[128,256]{1,0:T(8,128)(2,1)S(1)}, bf16[128,256]{1,0:T(8,128)(2,1)S(1)}, u32[]{:S(2)}, u32[]{:S(2)}) %collective-permute-start) | collective-permute-done | bytes 65568 | tf_op jit(solution)/shard_map/ppermute | solution.py:388
  90.0 3.4 %shard_map.147 = (bf16[128,640]{1,0:T(8,128)(2,1)S(1)}, f32[128,256]{1,0:T(8,128)S(1)}, bf16[128,256]{1,0:T(8,128)(2,1)S(1)}, f32[16,8,128]{2,1,0:T(8,128)S(1)}, f32[2,8,128]{2,1,0:T(8,128)S(1)}) custom-call(bf16[128,256]{1,0:T(8,128)(2,1)S(1)} %bitcast.17, bf16[128,256]{1,0:T(8,128)(2,1)S(1)} %bitcast.22, bf16[128,640]{1,0:T(8,128)(2,1)S(1)} %bitcast.13, ...), custom_call_target="tpu_custom_call" | custom-call | tf_op jit(solution)/shard_map/pallas_call | solution.py:325
  93.4 8.0 %all_to_all.61 = bf16[8,16,640]{2,1,0:T(8,128)(2,1)S(1)} all-to-all(bf16[8,16,640]{2,1,0:T(8,128)(2,1)S(1)} %bitcast.23), channel_id=1, replica_groups=mesh['ly'=2,'yl'=2,'zh'=4,'x'=4,'zl'=4,'core'=2] {'yl','x'}, dimensions={0} | all-to-all | bytes 327680 | tf_op jit(solution)/shard_map/all_to_all | solution.py:336
  101.5 14.2 %all_to_all.62 = bf16[4,16,640]{2,1,0:T(8,128)(2,1)S(1)} all-to-all(bf16[4,16,640]{2,1,0:T(8,128)(2,1)S(1)} %broadcast_in_dim.16), channel_id=1, replica_groups=mesh['ly'=2,'yl'=2,'zh'=4,'x'=4,'zl'=4,'core'=2] {'zh'}, dimensions={0} | all-to-all | bytes 163840 | tf_op jit(solution)/shard_map/all_to_all | solution.py:336
  115.7 8.0 %all_to_all.63 = bf16[8,16,640]{2,1,0:T(8,128)(2,1)S(1)} all-to-all(bf16[8,16,640]{2,1,0:T(8,128)(2,1)S(1)} %broadcast_in_dim.17), channel_id=1, replica_groups=mesh['ly'=2,'yl'=2,'zh'=4,'x'=4,'zl'=4,'core'=2] {'yl','x'}, dimensions={0} | all-to-all | bytes 327680 | tf_op jit(solution)/shard_map/all_to_all | solution.py:336
  123.7 0.0 copy-start.6
  123.7 0.7 copy-done.6
  124.4 1.0 shard_map.148
  125.4 18.5 %all_to_all.64 = bf16[2,4,16,2176]{3,2,1,0:T(8,128)(2,1)S(1)} all-to-all(bf16[2,4,16,2176]{3,2,1,0:T(8,128)(2,1)S(1)} %get-tuple-element.36), channel_id=1, replica_groups=mesh['ly'=2,'yl'=2,'zh'=4,'x'=4,'zl'=4,'core'=2] {'core'}, dimensions={0} | all-to-all | bytes 1114112 | tf_op jit(solution)/shard_map/all_to_all | solution.py:336
  143.9 0.2 reduce_sum.87
  144.1 10.4 %all_to_all.65.got_ref = bf16[4,16,2176]{2,1,0:T(8,128)(2,1)S(1)} all-to-all(bf16[4,16,2176]{2,1,0:T(8,128)(2,1)S(1)} %reduce_sum.87), channel_id=1, replica_groups=mesh['ly'=2,'yl'=2,'zh'=4,'x'=4,'zl'=4,'core'=2] {'zl'}, dimensions={0} | all-to-all | bytes 557056 | tf_op jit(solution)/shard_map/all_to_all | solution.py:336
  154.5 0.7 shard_map.149
  (15 shorter events, 0.2 us)
Async XLA Ops:
  41.0 8.2 %copy-start.1 = (bf16[512,256]{1,0:T(8,128)(2,1)S(1)}, bf16[512,256]{1,0:T(8,128)(2,1)}, u32[]{:S(2)}) copy-start(bf16[512,256]{1,0:T(8,128)(2,1)} %refs_3_.3) | copy-start | bytes 786436
  41.0 8.2 %copy-start.2 = (bf16[4,32,256]{2,1,0:T(8,128)(2,1)S(1)}, bf16[4,32,256]{2,1,0:T(8,128)(2,1)}, u32[]{:S(2)}) copy-start(bf16[4,32,256]{2,1,0:T(8,128)(2,1)} %param.9) | copy-start | bytes 196612
  41.0 8.2 %copy-start.3 = (bf16[4,32,256]{2,1,0:T(8,128)(2,1)S(1)}, bf16[4,32,256]{2,1,0:T(8,128)(2,1)}, u32[]{:S(2)}) copy-start(bf16[4,32,256]{2,1,0:T(8,128)(2,1)} %param.10) | copy-start | bytes 196612
  41.0 8.2 %copy-start.5 = (f32[24,256]{1,0:T(8,128)S(1)}, f32[24,256]{1,0:T(8,128)}, u32[]{:S(2)}) copy-start(f32[24,256]{1,0:T(8,128)} %get-tuple-element.27.refs_4_) | copy-start | bytes 73732
  74.6 8.2 %copy-start = (bf16[256,512]{1,0:T(8,128)(2,1)S(1)}, bf16[256,512]{1,0:T(8,128)(2,1)}, u32[]{:S(2)}) copy-start(bf16[256,512]{1,0:T(8,128)(2,1)} %wl_ref.3) | copy-start | bytes 786436
  74.7 8.2 %copy-start.4 = (bf16[32,256]{1,0:T(8,128)(2,1)S(1)}, bf16[32,256]{1,0:T(8,128)(2,1)}, u32[]{:S(2)}) copy-start(bf16[32,256]{1,0:T(8,128)(2,1)} %ws_ref.3) | copy-start | bytes 49156
  83.1 6.9 %collective-permute-start = (bf16[128,256]{1,0:T(8,128)(2,1)S(1)}, bf16[128,256]{1,0:T(8,128)(2,1)S(1)}, u32[]{:S(2)}, u32[]{:S(2)}) collective-permute-start(bf16[128,256]{1,0:T(8,128)(2,1)S(1)} %shard_map.146), channel_id=1, source_target_pairs={{256,0},{257,1},{258,2},{259,3},{260,4},{261,5},{262,6},{263,7},{2... | collective-permute-start | bytes 196616 | tf_op jit(solution)/shard_map/ppermute | solution.py:388
  123.7 0.7 copy-start.6

commit v5 on v4

--- a/solution.py
+++ b/solution.py
@@ -16,7 +16,7 @@
 TN = (((0,), (0,)), ((), ()))
 NEAR = ("yl", "x")
 REPLICAS = ("zl", "core")
-VMEM_LIMIT = 48 * 1024 * 1024
+VMEM_LIMIT = 24 * 1024 * 1024
 PROJECT_LIMIT = 60 * 1024 * 1024
 SEL_ROWS = 8
 TILE = 16
@@ -70,7 +70,7 @@
     return copies
 
 
-def project_kernel(x_hbm, ws_hbm, wl_hbm, rate_hbm, bias_hbm, skip_hbm, plan_hbm, out_ref, const_ref, order_ref,
+def project_kernel(x_hbm, ws_hbm, wl_hbm, rate_hbm, bias_hbm, skip_hbm, plan_hbm, out_ref, const_ref,
                    x_ref, ws_ref, wl_ref, rate_ref, bias_ref, skip_ref, plan_ref, sems):
     copies = fetch((x_hbm, wl_hbm, ws_hbm, rate_hbm, bias_hbm, skip_hbm, plan_hbm),
                    (x_ref, wl_ref, ws_ref, rate_ref, bias_ref, skip_ref, plan_ref), sems)
@@ -86,7 +86,8 @@
     const_ref[states:states + 1, :] = bias_ref[...]
     const_ref[states + 1:states + 2, :] = skip_ref[...]
     for j in range(plan_ref.shape[0]):
-        order_ref[j:j + 1, :] = jnp.full((1, order_ref.shape[1]), plan_ref[j], jnp.int32)
+        at = states + 2 + j
+        const_ref[at:at + 1, :] = jnp.full((1, const_ref.shape[1]), plan_ref[j], jnp.int32).astype(F32)
 
 
 def state_lanes(states):
@@ -115,7 +116,7 @@
         for k in range(2)], axis=1)
 
 
-def forward(micro, length, states, rank, x, cat, wd, const_ref, DP, A, H, BC, R, X, D, DX, SG):
+def prepare(micro, length, states, rank, x, cat, wd, const_ref, DP, Q, R, X, D, DX, SG):
     rows = 2 * micro * length
     doubled = 2 * states
     half = first_half(rows, micro)
@@ -124,8 +125,7 @@
     slabs = (length, 2 * micro, 128)
     cat8 = dot(T, cat[:, rank:rank + 2 * doubled]).astype(BF16)
     x8 = pick_half(half, dot(T, x)).reshape(slabs)
-    pick = state_lanes(states)
-    BC[...] = dot(cat8, jnp.concatenate([pick, pick], axis=0)).reshape(BC.shape)
+    Q[...] = cat8
     put_rows(DP, micro, dot(cat[:, :rank], wd))
     pre8 = DP[...].reshape(slabs)
     pre8 = pre8 + pick_half(lower, const_ref[states:states + 1, :])[None]
@@ -134,9 +134,16 @@
     D[...] = step8
     DX[...] = step8 * x8
     SG[...] = jax.nn.sigmoid(pre8)
+    for n in range(states):
+        R[n] = pick_half(lower, const_ref[n:n + 1, :])
+    R[states] = pick_half(lower, const_ref[states + 1:states + 2, :])
+
+
+def forward(micro, length, states, A, H, BC, Q, R, X, D, DX, SG):
+    pick = state_lanes(states)
+    BC[...] = dot(Q[...], jnp.concatenate([pick, pick], axis=0)).reshape(BC.shape)
     zero = jnp.zeros((2 * micro, 128), F32)
     for n in range(states):
-        R[n] = pick_half(lower, const_ref[n:n + 1, :])
         H[0, n] = zero
 
     def ahead(t, h):
@@ -153,13 +160,13 @@
     lax.fori_loop(0, length, ahead, (zero,) * states, unroll=length)
 
 
-def backward(micro, length, states, rank, sums, wd, const_ref, G, A, H, BC, R, X, D, DX, SG,
+def backward(micro, length, states, rank, sums, wd_ref, copies, G, A, H, BC, Q, R, X, D, DX, SG,
              send_ref, core_ref, products, DP, C):
     rows = 2 * micro * length
     doubled = 2 * states
     half = first_half(rows, micro)
     zero = jnp.zeros((2 * micro, 128), F32)
-    skip8 = pick_half(first_half(2 * micro, micro), const_ref[states + 1:states + 2, :])
+    skip8 = R[states]
 
     def back(i, carry):
         later, bias_acc, skip_acc = carry
@@ -201,35 +208,47 @@
     S = gather_matrix(micro, length)
     core_ref[...] = get_rows(C, micro)
     dpre_half = get_rows(DP, micro).astype(BF16)
-    send_ref[:, :rank] = dot(dpre_half, wd, NT).astype(BF16)
+    for copy in copies:
+        copy.wait()
+    send_ref[:, :rank] = dot(dpre_half, wd_ref[...], NT).astype(BF16)
     high, low = two_terms(grouped_sums(products[...].reshape(rows, doubled * 128), doubled))
     send_ref[:, rank:] = jnp.zeros((micro * length, WIDTH - rank), BF16)
     send_ref[:, rank:rank + doubled] = (dot(S, high) + dot(S, low)).astype(BF16)
     return dpre_half, bias_acc, skip_acc
 
 
-def tick_kernel(micro, length, states, rank, from_above, *refs):
-    x_ref, side_ref, cat_ref, wd_ref, const_ref, *refs = refs
-    if from_above:
-        above_ref, send_ref, core_ref, dpre_ref, rate_out, ends_ref, *refs = refs
-    else:
-        send_ref, core_ref, *refs = refs
-    G, products, DP, C, *state = refs
-    rows = 2 * micro * length
-    channels = x_ref.shape[1]
-    half = first_half(rows, micro)
-    T = spread_matrix(micro, length)
-    g8 = pick_half(half, dot(T, side_ref[...]))
-    if from_above:
-        g8 = g8 + pick_half(half, dot(T, above_ref[...]))
-    G[...] = g8.reshape(G.shape)
-    forward(micro, length, states, rank, x_ref[...], cat_ref[...], wd_ref[...], const_ref, DP, *state)
+def spread_rows(micro, length, ref):
+    half = first_half(2 * micro * length, micro)
+    return pick_half(half, dot(spread_matrix(micro, length), ref[...])).reshape(length, 2 * micro, 128)
+
+
+def upper_kernel(micro, length, states, rank, x_ref, side_ref, cat_ref, wd_ref, const_ref, send_ref, core_ref,
+                 G, products, DP, C, *state):
+    G[...] = spread_rows(micro, length, side_ref)
+    prepare(micro, length, states, rank, x_ref[...], cat_ref[...], wd_ref[...], const_ref, DP, *state[3:])
+    forward(micro, length, states, *state)
+    backward(micro, length, states, rank, None, wd_ref, (), G, *state, send_ref, core_ref, products, DP, C)
+
+
+def ahead_kernel(micro, length, states, rank, x_any, side_any, cat_any, wd_any, const_any, *refs):
+    *outs, DP, x_ref, side_ref, cat_ref, wd_ref, const_ref, sems = refs
+    for copy in fetch((x_any, side_any, cat_any, wd_any, const_any), (x_ref, side_ref, cat_ref, wd_ref, const_ref), sems):
+        copy.wait()
+    outs[0][...] = spread_rows(micro, length, side_ref)
+    prepare(micro, length, states, rank, x_ref[...], cat_ref[...], wd_ref[...], const_ref, DP, *outs[1:])
+
+
+def lower_kernel(micro, length, states, rank, wd_any, above_ref, side_ref, *refs):
+    *ready, send_ref, core_ref, dpre_ref, rate_ref, ends_ref, G, products, DP, C, A, H, BC, wd_ref, sems = refs
+    state = (A, H, BC, *ready)
+    copies = fetch((wd_any,), (wd_ref,), sems)
+    G[...] = side_ref[...] + spread_rows(micro, length, above_ref)
+    forward(micro, length, states, *state)
     dpre_half, bias_acc, skip_acc = backward(
-        micro, length, states, rank, rate_out if from_above else None, wd_ref[...], const_ref, G, *state, send_ref, core_ref, products, DP, C)
-    if from_above:
-        dpre_ref[...] = dpre_half
-        ends_ref[0] = bias_acc
-        ends_ref[1] = skip_acc
+        micro, length, states, rank, rate_ref, wd_ref, copies, G, *state, send_ref, core_ref, products, DP, C)
+    dpre_ref[...] = dpre_half
+    ends_ref[0] = bias_acc
+    ends_ref[1] = skip_acc
 
 
 def layer_grad(cat_ref, wl_ref, ws_ref, core_ref):
@@ -242,7 +261,7 @@
     grad_ref[...] = layer_grad(cat_ref, wl_ref, ws_ref, core_ref)
 
 
-def part_kernel(micro, order_ref, cat_ref, down_ref, x_ref, wl_ref, ws_ref, core_ref, dpre_ref, rate_ref, ends_ref,
+def part_kernel(micro, const_ref, cat_ref, down_ref, x_ref, wl_ref, ws_ref, core_ref, dpre_ref, rate_ref, ends_ref,
                 send_ref, grad_ref, small):
     cores, groups, tile, _ = send_ref.shape
     replicas, states = cores * groups, rate_ref.shape[0]
@@ -283,10 +302,10 @@
         send_ref[*to, :, first + deep // tile * channels:] = small[r].astype(BF16)
     grad = layer_grad(down_ref, wl_ref, ws_ref, core_ref).astype(F32).reshape(grad_ref.shape)
     for j in range(micro):
-        which = order_ref[j:j + 1, :]
+        which = const_ref[states + 2 + j:states + 3 + j, :]
         value = grad[0]
         for m in range(1, micro):
-            value = jnp.where(which == m, grad[m], value)
+            value = jnp.where(which == float(m), grad[m], value)
         grad_ref[j] = value.astype(BF16)
 
 
@@ -361,8 +380,8 @@
     bias, skip = delta_bias.reshape(1, channels), skip_gain.reshape(1, channels)
 
     sources = (x, w_select, w_low, decay_rate, bias, skip, plan)
-    part, const, order = call(
-        project_kernel, [((tokens, WIDTH), BF16), ((states + 8, channels), F32), ((8, channels), jnp.int32)],
+    part, const = call(
+        project_kernel, [((tokens, WIDTH), BF16), ((states + 8, channels), F32)],
         [pltpu.VMEM(a.shape, a.dtype) for a in sources[:-1]]
         + [pltpu.SMEM(plan.shape, plan.dtype), pltpu.SemaphoreType.DMA((len(sources),))],
         *sources, far=len(sources), limit=PROJECT_LIMIT)
@@ -374,23 +393,29 @@
     cat = to_all(packed, NEAR).reshape(tokens, WIDTH)
 
     dims = (micro, length, states, rank)
-    slab, rows_all = (length, 2 * micro, 128), 2 * tokens
-    send_out = ((tokens, WIDTH), BF16)
-    scratch = [slab, pltpu.VMEM((length // 2, 4 * micro, doubled * 128), BF16), (rows_all, 128), (rows_all, 128),
-               (length, states, 2 * micro, 128), (length + 1, states, 2 * micro, 128),
-               (length, 2 * micro, doubled * 128), (states, 2 * micro, 128), slab, slab, slab, slab]
-    shared = (x, side, cat, w_delta, const)
+    slab, rows_all = (length, 2 * micro, 128), (2 * tokens, 128)
+    send_out, grad_out = ((tokens, WIDTH), BF16), (tokens, channels)
+    scratch = [slab, pltpu.VMEM((length // 2, 4 * micro, doubled * 128), BF16), rows_all, rows_all]
+    state = [(length, states, 2 * micro, 128), (length + 1, states, 2 * micro, 128),
+             (length, 2 * micro, doubled * 128), (states + 1, 2 * micro, 128), slab, slab, slab, slab]
+    state.insert(3, pltpu.VMEM((2 * tokens, 2 * doubled), BF16))
     send, core = call(
-        functools.partial(tick_kernel, *dims, False), [send_out, ((tokens, channels), F32)], scratch, *shared)
+        functools.partial(upper_kernel, *dims), [send_out, (grad_out, F32)], scratch + state,
+        x, side, cat, w_delta, const)
     cat_up = to_all(scattered_sum(send, NEAR).astype(BF16), NEAR).reshape(tokens, WIDTH)
-    handed, = call(
-        hand_kernel, [((tokens, channels), BF16)], [], cat_up, w_low, w_select, core)
+    handed, = call(hand_kernel, [(grad_out, BF16)], [], cat_up, w_low, w_select, core)
     above = lax.ppermute(handed, "ly", [(1, 0)])
+    held_cat, _ = lax.optimization_barrier((cat, handed))
+    early = (x, side, held_cat, w_delta, const)
+    ahead = call(
+        functools.partial(ahead_kernel, *dims), [(slab, F32), ((2 * tokens, 2 * doubled), BF16)] + [(shape, F32) for shape in state[4:]],
+        [rows_all] + [pltpu.VMEM(a.shape, a.dtype) for a in early] + [pltpu.SemaphoreType.DMA((len(early),))],
+        *early, far=len(early))
 
     send, core, dpre, rate_sum, end_sums = call(
-        functools.partial(tick_kernel, *dims, True),
-        [send_out, ((tokens, channels), F32), ((tokens, channels), BF16), ((states, 2 * micro, 128), F32),
-         ((2, 2 * micro, 128), F32)], scratch, *shared, above)
+        functools.partial(lower_kernel, *dims),
+        [send_out, (grad_out, F32), (grad_out, BF16), ((states, 2 * micro, 128), F32), ((2, 2 * micro, 128), F32)],
+        scratch + state[:3] + [pltpu.VMEM(w_delta.shape, BF16), pltpu.SemaphoreType.DMA((1,))], w_delta, above, *ahead, far=1)
     down_cat = to_all(scattered_sum(send, NEAR).astype(BF16), NEAR).reshape(tokens, WIDTH)
 
     own, deep = channels // replicas, rank // replicas
@@ -399,7 +424,7 @@
     partials, grad = call(
         functools.partial(part_kernel, micro),
         [((cores, groups, TILE, lanes), BF16), ((micro, length, channels), BF16)], [(replicas, TILE, 128)],
-        order, cat, down_cat, x, w_low, w_select, core, dpre, rate_sum, end_sums)
+        const, cat, down_cat, x, w_low, w_select, core, dpre, rate_sum, end_sums)
     pairs = total(exchange(partials, "core")).astype(BF16)
     got = exchange(pairs, "zl")
     sums = call(

time: 156 us -> 155 us (level)
    pallas_call x6 -> x7, Pallas kernels: 10.5 us -> 10.6 us  [call(): pl.pallas_call(kernel, out_shape=[jax.ShapeDtypeStruct(*out) for out in o...]
  transfers between devices with their start and end apart: 1 -> 1, of which waited for: 1 -> 1; matrix products, arithmetic and copies ran while one was open for 0% -> 0% of each run, Pallas kernels for 0% -> 1%
where the time goes in v5:
time: 155 us; the launch traced here: 154 us
  blocking collectives  136 us (88%)
  Pallas kernels  10.6 us (7%)
  waiting for transfers between devices  4.78 us (3%)
    all_to_all x11, blocking collectives, exchange(): return lax.all_to_all(blocks, axes, 0, 0)  136 us
    pallas_call x7, Pallas kernels, call(): pl.pallas_call(kernel, out_shape=[jax.ShapeDtypeStruct(*out) for out in o...  10.6 us
    ppermute x1, waiting for transfers between devices, per_device(): above = lax.ppermute(handed, 'ly', [(1, 0)])  4.78 us
  transfers between devices with their start and end apart: 1, of which 1 were waited for; matrix products, arithmetic and copies ran while one was open for 0% of the time, Pallas kernels for 1%

profile of v5, /device:TPU:1, one launch (start us, length us, event | category | flops | bytes accessed | tf_op | source)
XLA Modules:
  0.0 153.9 jit_solution(397595278087130518)
XLA Ops:
  0.6 1.9 %shard_map.144 = (bf16[128,640]{1,0:T(8,128)(2,1)}, f32[24,256]{1,0:T(8,128)}) custom-call(bf16[128,256]{1,0:T(8,128)(2,1)} %bitcast.15, bf16[32,256]{1,0:T(8,128)(2,1)} %ws_ref.3, bf16[256,512]{1,0:T(8,128)(2,1)} %wl_ref.3, f32[16,256]{1,0:T(8,128)} %rate_hbm.1, f32[1,256]{1,0:T(1,128)} %bitcast.26, f32[1,256]{1,0:T(1,128)} %bitcast.27, s32[4]{0:T(128)} %plan_hbm.1), custom_call_target="tpu_custom_call" | custom-call | tf_op jit(solution)/shard_map/pallas_call | solution.py:344
  2.6 11.5 %all_to_all.55 = bf16[8,16,640]{2,1,0:T(8,128)(2,1)S(1)} all-to-all(bf16[8,16,640]{2,1,0:T(8,128)(2,1)} %bitcast.25), channel_id=1, replica_groups=mesh['ly'=2,'yl'=2,'zh'=4,'x'=4,'zl'=4,'core'=2] {'yl','x'}, dimensions={0} | all-to-all | bytes 327680 | tf_op jit(solution)/shard_map/all_to_all | solution.py:355
  14.1 26.7 %all_to_all.56 = bf16[4,16,640]{2,1,0:T(8,128)(2,1)S(1)} all-to-all(bf16[4,16,640]{2,1,0:T(8,128)(2,1)S(1)} %broadcast_in_dim.12), channel_id=1, replica_groups=mesh['ly'=2,'yl'=2,'zh'=4,'x'=4,'zl'=4,'core'=2] {'zh'}, dimensions={0} | all-to-all | bytes 163840 | tf_op jit(solution)/shard_map/all_to_all | solution.py:355
  40.8 0.1 slice.16
  40.9 0.1 pad_maximum_fusion
  41.0 0.0 copy-start
  41.0 0.0 copy-start.2
  41.0 0.0 copy-start.3
  41.0 0.0 copy-start.4
  41.0 8.1 %all_to_all.57 = bf16[8,16,640]{2,1,0:T(8,128)(2,1)S(1)} all-to-all(bf16[8,16,640]{2,1,0:T(8,128)(2,1)S(1)} %broadcast_in_dim.13), channel_id=1, replica_groups=mesh['ly'=2,'yl'=2,'zh'=4,'x'=4,'zl'=4,'core'=2] {'yl','x'}, dimensions={0} | all-to-all | bytes 327680 | tf_op jit(solution)/shard_map/all_to_all | solution.py:355
  49.2 0.0 copy-done
  49.2 0.0 copy-done.2
  49.2 0.0 copy-done.3
  49.2 0.0 copy-done.4
  49.2 2.9 %shard_map.145 = (bf16[128,640]{1,0:T(8,128)(2,1)S(1)}, f32[128,256]{1,0:T(8,128)S(1)}) custom-call(bf16[128,256]{1,0:T(8,128)(2,1)S(1)} %bitcast.16, bf16[128,256]{1,0:T(8,128)(2,1)S(1)} %bitcast.21, bf16[128,640]{1,0:T(8,128)(2,1)S(1)} %bitcast.12, bf16[512,256]{1,0:T(8,128)(2,1)S(1)} %copy-done, f32[24,256]{1,0:T(8,128)S(1)} %copy-done.4), custom_call_target="tpu_custom_call" | custom-call | tf_op jit(solution)/shard_map/pallas_call | solution.py:344
  52.1 8.0 %all_to_all.58 = bf16[8,16,640]{2,1,0:T(8,128)(2,1)S(1)} all-to-all(bf16[8,16,640]{2,1,0:T(8,128)(2,1)S(1)} %bitcast.24), channel_id=1, replica_groups=mesh['ly'=2,'yl'=2,'zh'=4,'x'=4,'zl'=4,'core'=2] {'yl','x'}, dimensions={0} | all-to-all | bytes 327680 | tf_op jit(solution)/shard_map/all_to_all | solution.py:355
  60.2 14.2 %all_to_all.59 = bf16[4,16,640]{2,1,0:T(8,128)(2,1)S(1)} all-to-all(bf16[4,16,640]{2,1,0:T(8,128)(2,1)S(1)} %broadcast_in_dim.14), channel_id=1, replica_groups=mesh['ly'=2,'yl'=2,'zh'=4,'x'=4,'zl'=4,'core'=2] {'zh'}, dimensions={0} | all-to-all | bytes 163840 | tf_op jit(solution)/shard_map/all_to_all | solution.py:355
  74.3 0.0 copy-start.1
  74.4 0.0 copy-start.5
  74.4 8.1 %all_to_all.60 = bf16[8,16,640]{2,1,0:T(8,128)(2,1)S(1)} all-to-all(bf16[8,16,640]{2,1,0:T(8,128)(2,1)S(1)} %broadcast_in_dim.15), channel_id=1, replica_groups=mesh['ly'=2,'yl'=2,'zh'=4,'x'=4,'zl'=4,'core'=2] {'yl','x'}, dimensions={0} | all-to-all | bytes 327680 | tf_op jit(solution)/shard_map/all_to_all | solution.py:355
  82.5 0.0 copy-done.1
  82.5 0.0 copy-done.5
  82.5 0.2 shard_map.146
  82.8 1.3 collective-permute-start
  84.1 0.9 shard_map.147
  84.9 4.8 %collective-permute-done.above_ref = bf16[128,256]{1,0:T(8,128)(2,1)S(1)} collective-permute-done((bf16[128,256]{1,0:T(8,128)(2,1)S(1)}, bf16[128,256]{1,0:T(8,128)(2,1)S(1)}, u32[]{:S(2)}, u32[]{:S(2)}) %collective-permute-start) | collective-permute-done | bytes 65568 | tf_op jit(solution)/shard_map/ppermute | solution.py:407
  89.7 2.9 %shard_map.148 = (bf16[128,640]{1,0:T(8,128)(2,1)S(1)}, f32[128,256]{1,0:T(8,128)S(1)}, bf16[128,256]{1,0:T(8,128)(2,1)S(1)}, f32[16,8,128]{2,1,0:T(8,128)S(1)}, f32[2,8,128]{2,1,0:T(8,128)S(1)}) custom-call(bf16[512,256]{1,0:T(8,128)(2,1)S(1)} %copy-done, bf16[128,256]{1,0:T(8,128)(2,1)S(1)} %collective-permute-done.above_ref, ...), custom_call_target="tpu_custom_call" | custom-call | tf_op jit(solution)/shard_map/pallas_call | solution.py:344
  92.6 8.0 %all_to_all.61 = bf16[8,16,640]{2,1,0:T(8,128)(2,1)S(1)} all-to-all(bf16[8,16,640]{2,1,0:T(8,128)(2,1)S(1)} %bitcast.23), channel_id=1, replica_groups=mesh['ly'=2,'yl'=2,'zh'=4,'x'=4,'zl'=4,'core'=2] {'yl','x'}, dimensions={0} | all-to-all | bytes 327680 | tf_op jit(solution)/shard_map/all_to_all | solution.py:355
  100.7 14.2 %all_to_all.62 = bf16[4,16,640]{2,1,0:T(8,128)(2,1)S(1)} all-to-all(bf16[4,16,640]{2,1,0:T(8,128)(2,1)S(1)} %broadcast_in_dim.16), channel_id=1, replica_groups=mesh['ly'=2,'yl'=2,'zh'=4,'x'=4,'zl'=4,'core'=2] {'zh'}, dimensions={0} | all-to-all | bytes 163840 | tf_op jit(solution)/shard_map/all_to_all | solution.py:355
  114.9 8.0 %all_to_all.63 = bf16[8,16,640]{2,1,0:T(8,128)(2,1)S(1)} all-to-all(bf16[8,16,640]{2,1,0:T(8,128)(2,1)S(1)} %broadcast_in_dim.17), channel_id=1, replica_groups=mesh['ly'=2,'yl'=2,'zh'=4,'x'=4,'zl'=4,'core'=2] {'yl','x'}, dimensions={0} | all-to-all | bytes 327680 | tf_op jit(solution)/shard_map/all_to_all | solution.py:355
  122.9 1.0 shard_map.149
  123.9 18.2 %all_to_all.64 = bf16[2,4,16,2176]{3,2,1,0:T(8,128)(2,1)S(1)} all-to-all(bf16[2,4,16,2176]{3,2,1,0:T(8,128)(2,1)S(1)} %get-tuple-element.50), channel_id=1, replica_groups=mesh['ly'=2,'yl'=2,'zh'=4,'x'=4,'zl'=4,'core'=2] {'core'}, dimensions={0} | all-to-all | bytes 1114112 | tf_op jit(solution)/shard_map/all_to_all | solution.py:355
  142.1 0.2 reduce_sum.87
  142.3 10.9 %all_to_all.65.got_ref = bf16[4,16,2176]{2,1,0:T(8,128)(2,1)S(1)} all-to-all(bf16[4,16,2176]{2,1,0:T(8,128)(2,1)S(1)} %reduce_sum.87), channel_id=1, replica_groups=mesh['ly'=2,'yl'=2,'zh'=4,'x'=4,'zl'=4,'core'=2] {'zl'}, dimensions={0} | all-to-all | bytes 557056 | tf_op jit(solution)/shard_map/all_to_all | solution.py:355
  153.2 0.7 shard_map.150
  (15 shorter events, 0.2 us)
Async XLA Ops:
  41.0 8.2 %copy-start = (bf16[512,256]{1,0:T(8,128)(2,1)S(1)}, bf16[512,256]{1,0:T(8,128)(2,1)}, u32[]{:S(2)}) copy-start(bf16[512,256]{1,0:T(8,128)(2,1)} %wd_any.3) | copy-start | bytes 786436
  41.0 8.2 %copy-start.2 = (bf16[4,32,256]{2,1,0:T(8,128)(2,1)S(1)}, bf16[4,32,256]{2,1,0:T(8,128)(2,1)}, u32[]{:S(2)}) copy-start(bf16[4,32,256]{2,1,0:T(8,128)(2,1)} %param.9) | copy-start | bytes 196612
  41.0 8.2 %copy-start.3 = (bf16[4,32,256]{2,1,0:T(8,128)(2,1)S(1)}, bf16[4,32,256]{2,1,0:T(8,128)(2,1)}, u32[]{:S(2)}) copy-start(bf16[4,32,256]{2,1,0:T(8,128)(2,1)} %param.10) | copy-start | bytes 196612
  41.0 8.2 %copy-start.4 = (f32[24,256]{1,0:T(8,128)S(1)}, f32[24,256]{1,0:T(8,128)}, u32[]{:S(2)}) copy-start(f32[24,256]{1,0:T(8,128)} %get-tuple-element.32.const_ref.const_any) | copy-start | bytes 73732
  74.3 8.2 %copy-start.1 = (bf16[256,512]{1,0:T(8,128)(2,1)S(1)}, bf16[256,512]{1,0:T(8,128)(2,1)}, u32[]{:S(2)}) copy-start(bf16[256,512]{1,0:T(8,128)(2,1)} %wl_ref.3) | copy-start | bytes 786436
  74.4 8.2 %copy-start.5 = (bf16[32,256]{1,0:T(8,128)(2,1)S(1)}, bf16[32,256]{1,0:T(8,128)(2,1)}, u32[]{:S(2)}) copy-start(bf16[32,256]{1,0:T(8,128)(2,1)} %ws_ref.3) | copy-start | bytes 49156
  82.8 6.9 %collective-permute-start = (bf16[128,256]{1,0:T(8,128)(2,1)S(1)}, bf16[128,256]{1,0:T(8,128)(2,1)S(1)}, u32[]{:S(2)}, u32[]{:S(2)}) collective-permute-start(bf16[128,256]{1,0:T(8,128)(2,1)S(1)} %shard_map.146), channel_id=1, source_target_pairs={{256,0},{257,1},{258,2},{259,3},{260,4},{261,5},{262,6},{263,7},{2... | collective-permute-start | bytes 196616 | tf_op jit(solution)/shard_map/ppermute | solution.py:407

commit v6 on v5

--- a/solution.py
+++ b/solution.py
@@ -261,11 +261,11 @@
     grad_ref[...] = layer_grad(cat_ref, wl_ref, ws_ref, core_ref)
 
 
-def part_kernel(micro, const_ref, cat_ref, down_ref, x_ref, wl_ref, ws_ref, core_ref, dpre_ref, rate_ref, ends_ref,
-                send_ref, grad_ref, small):
-    cores, groups, tile, _ = send_ref.shape
+def part_kernel(micro, cat_ref, down_ref, x_ref, dpre_ref, rate_ref, ends_ref, keep_ref, give_ref, small):
+    groups, tile, _ = keep_ref.shape
+    cores = small.shape[0] // groups
     replicas, states = cores * groups, rate_ref.shape[0]
-    channels, rank = wl_ref.shape
+    channels, rank = x_ref.shape[1], cat_ref.shape[1] // 128 * 128 - 128
     own, deep, doubled = channels // replicas, rank // replicas, 2 * states
     share, rate_share = doubled // replicas, states // replicas
     x, down = x_ref[...], down_ref[...]
@@ -291,15 +291,28 @@
         row = row_of(ends_ref[k])
         for r in range(replicas):
             small[r, at + k:at + k + 1, :own] = row[:, r * own:(r + 1) * own]
-    for r in range(replicas):
-        to = (r % cores, r // cores)
-        for i in range(own // tile):
-            send_ref[*to, :, i * rank:(i + 1) * rank] = low[r * own + i * tile:r * own + (i + 1) * tile]
-        first = own // tile * rank
-        for i in range(deep // tile):
-            lanes = slice(first + i * channels, first + (i + 1) * channels)
-            send_ref[*to, :, lanes] = delta[r * deep + i * tile:r * deep + (i + 1) * tile]
-        send_ref[*to, :, first + deep // tile * channels:] = small[r].astype(BF16)
+    first = own // tile * rank
+
+    def fill(ref, core):
+        for z in range(groups):
+            r = z * cores + core
+            for i in range(own // tile):
+                ref[z, :, i * rank:(i + 1) * rank] = low[r * own + i * tile:r * own + (i + 1) * tile]
+            for i in range(deep // tile):
+                lanes = slice(first + i * channels, first + (i + 1) * channels)
+                ref[z, :, lanes] = delta[r * deep + i * tile:r * deep + (i + 1) * tile]
+            ref[z, :, first + deep // tile * channels:] = small[r].astype(BF16)
+
+    mine = lax.axis_index("core")
+    for core in range(cores):
+        @pl.when(mine == core)
+        def _():
+            fill(keep_ref, core)
+            fill(give_ref, 1 - core)
+
+
+def order_kernel(states, const_ref, down_ref, wl_ref, ws_ref, core_ref, grad_ref):
+    micro = grad_ref.shape[0]
     grad = layer_grad(down_ref, wl_ref, ws_ref, core_ref).astype(F32).reshape(grad_ref.shape)
     for j in range(micro):
         which = const_ref[states + 2 + j:states + 3 + j, :]
@@ -420,12 +433,18 @@
 
     own, deep = channels // replicas, rank // replicas
     lanes = own // TILE * rank + deep // TILE * channels + 128
-    groups, cores = (lax.axis_size(axis) for axis in REPLICAS)
-    partials, grad = call(
-        functools.partial(part_kernel, micro),
-        [((cores, groups, TILE, lanes), BF16), ((micro, length, channels), BF16)], [(replicas, TILE, 128)],
-        const, cat, down_cat, x, w_low, w_select, core, dpre, rate_sum, end_sums)
-    pairs = total(exchange(partials, "core")).astype(BF16)
+    groups = lax.axis_size("zl")
+    share_out = ((groups, TILE, lanes), BF16)
+    keep, give = call(
+        functools.partial(part_kernel, micro), [share_out, share_out], [(replicas, TILE, 128)],
+        cat, down_cat, x, dpre, rate_sum, end_sums)
+    other = lax.ppermute(give, "core", [(0, 1), (1, 0)])
+    held_cat, _ = lax.optimization_barrier((down_cat, give))
+    grad, = call(
+        functools.partial(order_kernel, states), [((micro, length, channels), BF16)], [],
+        const, held_cat, w_low, w_select, core)
+    other, grad = lax.optimization_barrier((other, grad))
+    pairs = (keep.astype(F32) + other.astype(F32)).astype(BF16)
     got = exchange(pairs, "zl")
     sums = call(
         total_kernel,

time: 155 us -> 153 us (0.987)
  blocking collectives: 136 us -> 118 us
  starting transfers between devices: 1.29 us -> 17.6 us
    all_to_all x11 -> x10, blocking collectives: 136 us -> 118 us  [exchange(): return lax.all_to_all(blocks, axes, 0, 0)]
    ppermute x0 -> x1, starting transfers between devices: none -> 16.3 us  [per_device(): other = lax.ppermute(give, 'core', [(0, 1), (1, 0)])]
    pallas_call x7 -> x8, Pallas kernels: 10.6 us -> 10.8 us  [call(): pl.pallas_call(kernel, out_shape=[jax.ShapeDtypeStruct(*out) for out in o...]
  transfers between devices with their start and end apart: 1 -> 2, of which waited for: 1 -> 2; matrix products, arithmetic and copies ran while one was open for 0% -> 0% of each run, Pallas kernels for 1% -> 1%
where the time goes in v6:
time: 153 us; the launch traced here: 152 us
  blocking collectives  118 us (77%)
  starting transfers between devices  17.6 us (12%)
  Pallas kernels  10.8 us (7%)
  waiting for transfers between devices  5.04 us (3%)
    all_to_all x10, blocking collectives, exchange(): return lax.all_to_all(blocks, axes, 0, 0)  118 us
    ppermute x1, starting transfers between devices, per_device(): other = lax.ppermute(give, 'core', [(0, 1), (1, 0)])  16.3 us
    pallas_call x8, Pallas kernels, call(): pl.pallas_call(kernel, out_shape=[jax.ShapeDtypeStruct(*out) for out in o...  10.8 us
    ppermute x1, waiting for transfers between devices, per_device(): above = lax.ppermute(handed, 'ly', [(1, 0)])  4.78 us
  transfers between devices with their start and end apart: 2, of which 2 were waited for; matrix products, arithmetic and copies ran while one was open for 0% of the time, Pallas kernels for 1%

profile of v6, /device:TPU:1, one launch (start us, length us, event | category | flops | bytes accessed | tf_op | source)
XLA Modules:
  0.0 152.4 jit_solution(5163022879286910344)
XLA Ops:
  0.6 1.9 %shard_map.144 = (bf16[128,640]{1,0:T(8,128)(2,1)}, f32[24,256]{1,0:T(8,128)}) custom-call(bf16[128,256]{1,0:T(8,128)(2,1)} %bitcast.17, bf16[32,256]{1,0:T(8,128)(2,1)} %ws_ref.3, bf16[256,512]{1,0:T(8,128)(2,1)} %wl_ref.3, f32[16,256]{1,0:T(8,128)} %rate_hbm.1, f32[1,256]{1,0:T(1,128)} %bitcast.27, f32[1,256]{1,0:T(1,128)} %bitcast.28, s32[4]{0:T(128)} %plan_hbm.1), custom_call_target="tpu_custom_call" | custom-call | tf_op jit(solution)/shard_map/pallas_call | solution.py:357
  2.6 11.5 %all_to_all.50 = bf16[8,16,640]{2,1,0:T(8,128)(2,1)S(1)} all-to-all(bf16[8,16,640]{2,1,0:T(8,128)(2,1)} %bitcast.26), channel_id=1, replica_groups=mesh['ly'=2,'yl'=2,'zh'=4,'x'=4,'zl'=4,'core'=2] {'yl','x'}, dimensions={0} | all-to-all | bytes 327680 | tf_op jit(solution)/shard_map/all_to_all | solution.py:368
  14.1 26.7 %all_to_all.51 = bf16[4,16,640]{2,1,0:T(8,128)(2,1)S(1)} all-to-all(bf16[4,16,640]{2,1,0:T(8,128)(2,1)S(1)} %broadcast_in_dim.12), channel_id=1, replica_groups=mesh['ly'=2,'yl'=2,'zh'=4,'x'=4,'zl'=4,'core'=2] {'zh'}, dimensions={0} | all-to-all | bytes 163840 | tf_op jit(solution)/shard_map/all_to_all | solution.py:368
  40.8 0.1 slice.16
  40.9 0.1 pad_maximum_fusion
  41.0 0.0 copy-start
  41.0 0.0 copy-start.2
  41.0 0.0 copy-start.3
  41.0 0.0 copy-start.4
  41.0 8.1 %all_to_all.52 = bf16[8,16,640]{2,1,0:T(8,128)(2,1)S(1)} all-to-all(bf16[8,16,640]{2,1,0:T(8,128)(2,1)S(1)} %broadcast_in_dim.13), channel_id=1, replica_groups=mesh['ly'=2,'yl'=2,'zh'=4,'x'=4,'zl'=4,'core'=2] {'yl','x'}, dimensions={0} | all-to-all | bytes 327680 | tf_op jit(solution)/shard_map/all_to_all | solution.py:368
  49.2 0.0 copy-done
  49.2 0.0 copy-done.2
  49.2 0.0 copy-done.3
  49.2 0.0 copy-done.4
  49.2 2.9 %shard_map.145 = (bf16[128,640]{1,0:T(8,128)(2,1)S(1)}, f32[128,256]{1,0:T(8,128)S(1)}) custom-call(bf16[128,256]{1,0:T(8,128)(2,1)S(1)} %bitcast.18, bf16[128,256]{1,0:T(8,128)(2,1)S(1)} %bitcast.22, bf16[128,640]{1,0:T(8,128)(2,1)S(1)} %bitcast.12, bf16[512,256]{1,0:T(8,128)(2,1)S(1)} %copy-done, f32[24,256]{1,0:T(8,128)S(1)} %copy-done.4), custom_call_target="tpu_custom_call" | custom-call | tf_op jit(solution)/shard_map/pallas_call | solution.py:357
  52.1 8.0 %all_to_all.53 = bf16[8,16,640]{2,1,0:T(8,128)(2,1)S(1)} all-to-all(bf16[8,16,640]{2,1,0:T(8,128)(2,1)S(1)} %bitcast.25), channel_id=1, replica_groups=mesh['ly'=2,'yl'=2,'zh'=4,'x'=4,'zl'=4,'core'=2] {'yl','x'}, dimensions={0} | all-to-all | bytes 327680 | tf_op jit(solution)/shard_map/all_to_all | solution.py:368
  60.2 14.2 %all_to_all.54 = bf16[4,16,640]{2,1,0:T(8,128)(2,1)S(1)} all-to-all(bf16[4,16,640]{2,1,0:T(8,128)(2,1)S(1)} %broadcast_in_dim.14), channel_id=1, replica_groups=mesh['ly'=2,'yl'=2,'zh'=4,'x'=4,'zl'=4,'core'=2] {'zh'}, dimensions={0} | all-to-all | bytes 163840 | tf_op jit(solution)/shard_map/all_to_all | solution.py:368
  74.3 0.0 copy-start.1
  74.4 0.0 copy-start.5
  74.4 8.1 %all_to_all.55 = bf16[8,16,640]{2,1,0:T(8,128)(2,1)S(1)} all-to-all(bf16[8,16,640]{2,1,0:T(8,128)(2,1)S(1)} %broadcast_in_dim.15), channel_id=1, replica_groups=mesh['ly'=2,'yl'=2,'zh'=4,'x'=4,'zl'=4,'core'=2] {'yl','x'}, dimensions={0} | all-to-all | bytes 327680 | tf_op jit(solution)/shard_map/all_to_all | solution.py:368
  82.5 0.0 copy-done.1
  82.5 0.0 copy-done.5
  82.5 0.2 shard_map.146
  82.8 1.3 collective-permute-start
  84.1 0.9 shard_map.147
  84.9 4.8 %collective-permute-done.above_ref = bf16[128,256]{1,0:T(8,128)(2,1)S(1)} collective-permute-done((bf16[128,256]{1,0:T(8,128)(2,1)S(1)}, bf16[128,256]{1,0:T(8,128)(2,1)S(1)}, u32[]{:S(2)}, u32[]{:S(2)}) %collective-permute-start) | collective-permute-done | bytes 65568 | tf_op jit(solution)/shard_map/ppermute | solution.py:420
  89.7 2.9 %shard_map.148 = (bf16[128,640]{1,0:T(8,128)(2,1)S(1)}, f32[128,256]{1,0:T(8,128)S(1)}, bf16[128,256]{1,0:T(8,128)(2,1)S(1)}, f32[16,8,128]{2,1,0:T(8,128)S(1)}, f32[2,8,128]{2,1,0:T(8,128)S(1)}) custom-call(bf16[512,256]{1,0:T(8,128)(2,1)S(1)} %copy-done, bf16[128,256]{1,0:T(8,128)(2,1)S(1)} %collective-permute-done.above_ref, ...), custom_call_target="tpu_custom_call" | custom-call | tf_op jit(solution)/shard_map/pallas_call | solution.py:357
  92.6 8.0 %all_to_all.56 = bf16[8,16,640]{2,1,0:T(8,128)(2,1)S(1)} all-to-all(bf16[8,16,640]{2,1,0:T(8,128)(2,1)S(1)} %bitcast.24), channel_id=1, replica_groups=mesh['ly'=2,'yl'=2,'zh'=4,'x'=4,'zl'=4,'core'=2] {'yl','x'}, dimensions={0} | all-to-all | bytes 327680 | tf_op jit(solution)/shard_map/all_to_all | solution.py:368
  100.7 14.2 %all_to_all.57 = bf16[4,16,640]{2,1,0:T(8,128)(2,1)S(1)} all-to-all(bf16[4,16,640]{2,1,0:T(8,128)(2,1)S(1)} %broadcast_in_dim.16), channel_id=1, replica_groups=mesh['ly'=2,'yl'=2,'zh'=4,'x'=4,'zl'=4,'core'=2] {'zh'}, dimensions={0} | all-to-all | bytes 163840 | tf_op jit(solution)/shard_map/all_to_all | solution.py:368
  114.9 8.0 %all_to_all.58 = bf16[8,16,640]{2,1,0:T(8,128)(2,1)S(1)} all-to-all(bf16[8,16,640]{2,1,0:T(8,128)(2,1)S(1)} %broadcast_in_dim.17), channel_id=1, replica_groups=mesh['ly'=2,'yl'=2,'zh'=4,'x'=4,'zl'=4,'core'=2] {'yl','x'}, dimensions={0} | all-to-all | bytes 327680 | tf_op jit(solution)/shard_map/all_to_all | solution.py:368
  122.9 0.4 shard_map.149
  123.3 16.3 %collective-permute-start.1 = (bf16[4,16,2176]{2,1,0:T(8,128)(2,1)S(1)}, bf16[4,16,2176]{2,1,0:T(8,128)(2,1)S(1)}, u32[]{:S(2)}, u32[]{:S(2)}) collective-permute-start(bf16[4,16,2176]{2,1,0:T(8,128)(2,1)S(1)} %get-tuple-element.51), channel_id=1, source_target_pairs={{0,1},{1,0},{2,3},{3,2},{4,5},{5,4},{6,7},{7,6},{8,9},{9,8},{10,11... | collective-permute-start | bytes 835592 | tf_op jit(solution)/shard_map/ppermute | solution.py:441
  139.6 0.9 shard_map.150
  140.5 0.3 collective-permute-done.1
  140.8 0.1 add_convert_fusion
  140.8 10.9 %all_to_all.59.got_ref = bf16[4,16,2176]{2,1,0:T(8,128)(2,1)S(1)} all-to-all(bf16[4,16,2176]{2,1,0:T(8,128)(2,1)S(1)} %add_convert_fusion), channel_id=1, replica_groups=mesh['ly'=2,'yl'=2,'zh'=4,'x'=4,'zl'=4,'core'=2] {'zl'}, dimensions={0} | all-to-all | bytes 557056 | tf_op jit(solution)/shard_map/all_to_all | solution.py:368
  151.7 0.7 shard_map.151
  (15 shorter events, 0.2 us)
Async XLA Ops:
  41.0 8.2 %copy-start = (bf16[512,256]{1,0:T(8,128)(2,1)S(1)}, bf16[512,256]{1,0:T(8,128)(2,1)}, u32[]{:S(2)}) copy-start(bf16[512,256]{1,0:T(8,128)(2,1)} %wd_any.3) | copy-start | bytes 786436
  41.0 8.2 %copy-start.2 = (bf16[4,32,256]{2,1,0:T(8,128)(2,1)S(1)}, bf16[4,32,256]{2,1,0:T(8,128)(2,1)}, u32[]{:S(2)}) copy-start(bf16[4,32,256]{2,1,0:T(8,128)(2,1)} %param.9) | copy-start | bytes 196612
  41.0 8.2 %copy-start.3 = (bf16[4,32,256]{2,1,0:T(8,128)(2,1)S(1)}, bf16[4,32,256]{2,1,0:T(8,128)(2,1)}, u32[]{:S(2)}) copy-start(bf16[4,32,256]{2,1,0:T(8,128)(2,1)} %param.10) | copy-start | bytes 196612
  41.0 8.2 %copy-start.4 = (f32[24,256]{1,0:T(8,128)S(1)}, f32[24,256]{1,0:T(8,128)}, u32[]{:S(2)}) copy-start(f32[24,256]{1,0:T(8,128)} %get-tuple-element.36.const_ref.const_any) | copy-start | bytes 73732
  74.3 8.2 %copy-start.1 = (bf16[256,512]{1,0:T(8,128)(2,1)S(1)}, bf16[256,512]{1,0:T(8,128)(2,1)}, u32[]{:S(2)}) copy-start(bf16[256,512]{1,0:T(8,128)(2,1)} %wl_ref.3) | copy-start | bytes 786436
  74.4 8.2 %copy-start.5 = (bf16[32,256]{1,0:T(8,128)(2,1)S(1)}, bf16[32,256]{1,0:T(8,128)(2,1)}, u32[]{:S(2)}) copy-start(bf16[32,256]{1,0:T(8,128)(2,1)} %ws_ref.3) | copy-start | bytes 49156
  82.8 6.9 %collective-permute-start = (bf16[128,256]{1,0:T(8,128)(2,1)S(1)}, bf16[128,256]{1,0:T(8,128)(2,1)S(1)}, u32[]{:S(2)}, u32[]{:S(2)}) collective-permute-start(bf16[128,256]{1,0:T(8,128)(2,1)S(1)} %shard_map.146), channel_id=1, source_target_pairs={{256,0},{257,1},{258,2},{259,3},{260,4},{261,5},{262,6},{263,7},{2... | collective-permute-start | bytes 196616 | tf_op jit(solution)/shard_map/ppermute | solution.py:420
  123.3 17.5 %collective-permute-start.1 = (bf16[4,16,2176]{2,1,0:T(8,128)(2,1)S(1)}, bf16[4,16,2176]{2,1,0:T(8,128)(2,1)S(1)}, u32[]{:S(2)}, u32[]{:S(2)}) collective-permute-start(bf16[4,16,2176]{2,1,0:T(8,128)(2,1)S(1)} %get-tuple-element.51), channel_id=1, source_target_pairs={{0,1},{1,0},{2,3},{3,2},{4,5},{5,4},{6,7},{7,6},{8,9},{9,8},{10,11... | collective-permute-start | bytes 835592 | tf_op jit(solution)/shard_map/ppermute | solution.py:441

commit v7 on v6

--- a/solution.py
+++ b/solution.py
@@ -110,7 +110,7 @@
 
 
 def get_rows(ref, micro):
-    length = ref.shape[0] // (2 * micro)
+    length = ref.shape[0] // (2 * micro) - 1
     return jnp.concatenate([jnp.concatenate(
         [ref[pl.ds(k * micro + m, length, stride=2 * micro), :] for m in range(micro)], axis=0)
         for k in range(2)], axis=1)
@@ -127,7 +127,7 @@
     x8 = pick_half(half, dot(T, x)).reshape(slabs)
     Q[...] = cat8
     put_rows(DP, micro, dot(cat[:, :rank], wd))
-    pre8 = DP[...].reshape(slabs)
+    pre8 = DP[:2 * micro * length, :].reshape(slabs)
     pre8 = pre8 + pick_half(lower, const_ref[states:states + 1, :])[None]
     step8 = jax.nn.softplus(pre8)
     X[...] = x8
@@ -406,7 +406,7 @@
     cat = to_all(packed, NEAR).reshape(tokens, WIDTH)
 
     dims = (micro, length, states, rank)
-    slab, rows_all = (length, 2 * micro, 128), (2 * tokens, 128)
+    slab, rows_all = (length, 2 * micro, 128), (2 * tokens + 2 * micro, 128)
     send_out, grad_out = ((tokens, WIDTH), BF16), (tokens, channels)
     scratch = [slab, pltpu.VMEM((length // 2, 4 * micro, doubled * 128), BF16), rows_all, rows_all]
     state = [(length, states, 2 * micro, 128), (length + 1, states, 2 * micro, 128),

time: 153 us -> 153 us (level)
  no operation moved by 1% of the time
where the time goes in v7:
time: 153 us; the launch traced here: 152 us
  blocking collectives  118 us (77%)
  starting transfers between devices  17.6 us (12%)
  Pallas kernels  10.8 us (7%)
  waiting for transfers between devices  5.04 us (3%)
    all_to_all x10, blocking collectives, exchange(): return lax.all_to_all(blocks, axes, 0, 0)  118 us
    ppermute x1, starting transfers between devices, per_device(): other = lax.ppermute(give, 'core', [(0, 1), (1, 0)])  16.3 us
    pallas_call x8, Pallas kernels, call(): pl.pallas_call(kernel, out_shape=[jax.ShapeDtypeStruct(*out) for out in o...  10.8 us
    ppermute x1, waiting for transfers between devices, per_device(): above = lax.ppermute(handed, 'ly', [(1, 0)])  4.78 us
  transfers between devices with their start and end apart: 2, of which 2 were waited for; matrix products, arithmetic and copies ran while one was open for 0% of the time, Pallas kernels for 1%

profile of v7, /device:TPU:1, one launch (start us, length us, event | category | flops | bytes accessed | tf_op | source)
XLA Modules:
  0.0 152.4 jit_solution(17550183923038495874)
XLA Ops:
  0.6 1.9 %shard_map.144 = (bf16[128,640]{1,0:T(8,128)(2,1)}, f32[24,256]{1,0:T(8,128)}) custom-call(bf16[128,256]{1,0:T(8,128)(2,1)} %bitcast.17, bf16[32,256]{1,0:T(8,128)(2,1)} %ws_ref.3, bf16[256,512]{1,0:T(8,128)(2,1)} %wl_ref.3, f32[16,256]{1,0:T(8,128)} %rate_hbm.1, f32[1,256]{1,0:T(1,128)} %bitcast.27, f32[1,256]{1,0:T(1,128)} %bitcast.28, s32[4]{0:T(128)} %plan_hbm.1), custom_call_target="tpu_custom_call" | custom-call | tf_op jit(solution)/shard_map/pallas_call | solution.py:357
  2.6 11.5 %all_to_all.50 = bf16[8,16,640]{2,1,0:T(8,128)(2,1)S(1)} all-to-all(bf16[8,16,640]{2,1,0:T(8,128)(2,1)} %bitcast.26), channel_id=1, replica_groups=mesh['ly'=2,'yl'=2,'zh'=4,'x'=4,'zl'=4,'core'=2] {'yl','x'}, dimensions={0} | all-to-all | bytes 327680 | tf_op jit(solution)/shard_map/all_to_all | solution.py:368
  14.1 26.7 %all_to_all.51 = bf16[4,16,640]{2,1,0:T(8,128)(2,1)S(1)} all-to-all(bf16[4,16,640]{2,1,0:T(8,128)(2,1)S(1)} %broadcast_in_dim.12), channel_id=1, replica_groups=mesh['ly'=2,'yl'=2,'zh'=4,'x'=4,'zl'=4,'core'=2] {'zh'}, dimensions={0} | all-to-all | bytes 163840 | tf_op jit(solution)/shard_map/all_to_all | solution.py:368
  40.8 0.1 slice.16
  40.9 0.1 pad_maximum_fusion
  41.0 0.0 copy-start
  41.0 0.0 copy-start.2
  41.0 0.0 copy-start.3
  41.0 0.0 copy-start.4
  41.0 8.1 %all_to_all.52 = bf16[8,16,640]{2,1,0:T(8,128)(2,1)S(1)} all-to-all(bf16[8,16,640]{2,1,0:T(8,128)(2,1)S(1)} %broadcast_in_dim.13), channel_id=1, replica_groups=mesh['ly'=2,'yl'=2,'zh'=4,'x'=4,'zl'=4,'core'=2] {'yl','x'}, dimensions={0} | all-to-all | bytes 327680 | tf_op jit(solution)/shard_map/all_to_all | solution.py:368
  49.2 0.0 copy-done
  49.2 0.0 copy-done.2
  49.2 0.0 copy-done.3
  49.2 0.0 copy-done.4
  49.2 2.9 %shard_map.145 = (bf16[128,640]{1,0:T(8,128)(2,1)S(1)}, f32[128,256]{1,0:T(8,128)S(1)}) custom-call(bf16[128,256]{1,0:T(8,128)(2,1)S(1)} %bitcast.18, bf16[128,256]{1,0:T(8,128)(2,1)S(1)} %bitcast.22, bf16[128,640]{1,0:T(8,128)(2,1)S(1)} %bitcast.12, bf16[512,256]{1,0:T(8,128)(2,1)S(1)} %copy-done, f32[24,256]{1,0:T(8,128)S(1)} %copy-done.4), custom_call_target="tpu_custom_call" | custom-call | tf_op jit(solution)/shard_map/pallas_call | solution.py:357
  52.1 8.0 %all_to_all.53 = bf16[8,16,640]{2,1,0:T(8,128)(2,1)S(1)} all-to-all(bf16[8,16,640]{2,1,0:T(8,128)(2,1)S(1)} %bitcast.25), channel_id=1, replica_groups=mesh['ly'=2,'yl'=2,'zh'=4,'x'=4,'zl'=4,'core'=2] {'yl','x'}, dimensions={0} | all-to-all | bytes 327680 | tf_op jit(solution)/shard_map/all_to_all | solution.py:368
  60.2 14.2 %all_to_all.54 = bf16[4,16,640]{2,1,0:T(8,128)(2,1)S(1)} all-to-all(bf16[4,16,640]{2,1,0:T(8,128)(2,1)S(1)} %broadcast_in_dim.14), channel_id=1, replica_groups=mesh['ly'=2,'yl'=2,'zh'=4,'x'=4,'zl'=4,'core'=2] {'zh'}, dimensions={0} | all-to-all | bytes 163840 | tf_op jit(solution)/shard_map/all_to_all | solution.py:368
  74.3 0.0 copy-start.1
  74.4 0.0 copy-start.5
  74.4 8.1 %all_to_all.55 = bf16[8,16,640]{2,1,0:T(8,128)(2,1)S(1)} all-to-all(bf16[8,16,640]{2,1,0:T(8,128)(2,1)S(1)} %broadcast_in_dim.15), channel_id=1, replica_groups=mesh['ly'=2,'yl'=2,'zh'=4,'x'=4,'zl'=4,'core'=2] {'yl','x'}, dimensions={0} | all-to-all | bytes 327680 | tf_op jit(solution)/shard_map/all_to_all | solution.py:368
  82.5 0.0 copy-done.1
  82.5 0.0 copy-done.5
  82.5 0.2 shard_map.146
  82.8 1.3 collective-permute-start
  84.1 0.9 shard_map.147
  84.9 4.8 %collective-permute-done.above_ref = bf16[128,256]{1,0:T(8,128)(2,1)S(1)} collective-permute-done((bf16[128,256]{1,0:T(8,128)(2,1)S(1)}, bf16[128,256]{1,0:T(8,128)(2,1)S(1)}, u32[]{:S(2)}, u32[]{:S(2)}) %collective-permute-start) | collective-permute-done | bytes 65568 | tf_op jit(solution)/shard_map/ppermute | solution.py:420
  89.7 2.9 %shard_map.148 = (bf16[128,640]{1,0:T(8,128)(2,1)S(1)}, f32[128,256]{1,0:T(8,128)S(1)}, bf16[128,256]{1,0:T(8,128)(2,1)S(1)}, f32[16,8,128]{2,1,0:T(8,128)S(1)}, f32[2,8,128]{2,1,0:T(8,128)S(1)}) custom-call(bf16[512,256]{1,0:T(8,128)(2,1)S(1)} %copy-done, bf16[128,256]{1,0:T(8,128)(2,1)S(1)} %collective-permute-done.above_ref, ...), custom_call_target="tpu_custom_call" | custom-call | tf_op jit(solution)/shard_map/pallas_call | solution.py:357
  92.7 8.0 %all_to_all.56 = bf16[8,16,640]{2,1,0:T(8,128)(2,1)S(1)} all-to-all(bf16[8,16,640]{2,1,0:T(8,128)(2,1)S(1)} %bitcast.24), channel_id=1, replica_groups=mesh['ly'=2,'yl'=2,'zh'=4,'x'=4,'zl'=4,'core'=2] {'yl','x'}, dimensions={0} | all-to-all | bytes 327680 | tf_op jit(solution)/shard_map/all_to_all | solution.py:368
  100.7 14.2 %all_to_all.57 = bf16[4,16,640]{2,1,0:T(8,128)(2,1)S(1)} all-to-all(bf16[4,16,640]{2,1,0:T(8,128)(2,1)S(1)} %broadcast_in_dim.16), channel_id=1, replica_groups=mesh['ly'=2,'yl'=2,'zh'=4,'x'=4,'zl'=4,'core'=2] {'zh'}, dimensions={0} | all-to-all | bytes 163840 | tf_op jit(solution)/shard_map/all_to_all | solution.py:368
  114.9 8.0 %all_to_all.58 = bf16[8,16,640]{2,1,0:T(8,128)(2,1)S(1)} all-to-all(bf16[8,16,640]{2,1,0:T(8,128)(2,1)S(1)} %broadcast_in_dim.17), channel_id=1, replica_groups=mesh['ly'=2,'yl'=2,'zh'=4,'x'=4,'zl'=4,'core'=2] {'yl','x'}, dimensions={0} | all-to-all | bytes 327680 | tf_op jit(solution)/shard_map/all_to_all | solution.py:368
  122.9 0.4 shard_map.149
  123.3 16.3 %collective-permute-start.1 = (bf16[4,16,2176]{2,1,0:T(8,128)(2,1)S(1)}, bf16[4,16,2176]{2,1,0:T(8,128)(2,1)S(1)}, u32[]{:S(2)}, u32[]{:S(2)}) collective-permute-start(bf16[4,16,2176]{2,1,0:T(8,128)(2,1)S(1)} %get-tuple-element.51), channel_id=1, source_target_pairs={{0,1},{1,0},{2,3},{3,2},{4,5},{5,4},{6,7},{7,6},{8,9},{9,8},{10,11... | collective-permute-start | bytes 835592 | tf_op jit(solution)/shard_map/ppermute | solution.py:441
  139.6 0.9 shard_map.150
  140.5 0.3 collective-permute-done.1
  140.8 0.1 add_convert_fusion
  140.8 10.9 %all_to_all.59.got_ref = bf16[4,16,2176]{2,1,0:T(8,128)(2,1)S(1)} all-to-all(bf16[4,16,2176]{2,1,0:T(8,128)(2,1)S(1)} %add_convert_fusion), channel_id=1, replica_groups=mesh['ly'=2,'yl'=2,'zh'=4,'x'=4,'zl'=4,'core'=2] {'zl'}, dimensions={0} | all-to-all | bytes 557056 | tf_op jit(solution)/shard_map/all_to_all | solution.py:368
  151.8 0.7 shard_map.151
  (15 shorter events, 0.2 us)
Async XLA Ops:
  41.0 8.2 %copy-start = (bf16[512,256]{1,0:T(8,128)(2,1)S(1)}, bf16[512,256]{1,0:T(8,128)(2,1)}, u32[]{:S(2)}) copy-start(bf16[512,256]{1,0:T(8,128)(2,1)} %wd_any.3) | copy-start | bytes 786436
  41.0 8.2 %copy-start.2 = (bf16[4,32,256]{2,1,0:T(8,128)(2,1)S(1)}, bf16[4,32,256]{2,1,0:T(8,128)(2,1)}, u32[]{:S(2)}) copy-start(bf16[4,32,256]{2,1,0:T(8,128)(2,1)} %param.9) | copy-start | bytes 196612
  41.0 8.2 %copy-start.3 = (bf16[4,32,256]{2,1,0:T(8,128)(2,1)S(1)}, bf16[4,32,256]{2,1,0:T(8,128)(2,1)}, u32[]{:S(2)}) copy-start(bf16[4,32,256]{2,1,0:T(8,128)(2,1)} %param.10) | copy-start | bytes 196612
  41.0 8.2 %copy-start.4 = (f32[24,256]{1,0:T(8,128)S(1)}, f32[24,256]{1,0:T(8,128)}, u32[]{:S(2)}) copy-start(f32[24,256]{1,0:T(8,128)} %get-tuple-element.36.const_ref.const_any) | copy-start | bytes 73732
  74.3 8.2 %copy-start.1 = (bf16[256,512]{1,0:T(8,128)(2,1)S(1)}, bf16[256,512]{1,0:T(8,128)(2,1)}, u32[]{:S(2)}) copy-start(bf16[256,512]{1,0:T(8,128)(2,1)} %wl_ref.3) | copy-start | bytes 786436
  74.4 8.2 %copy-start.5 = (bf16[32,256]{1,0:T(8,128)(2,1)S(1)}, bf16[32,256]{1,0:T(8,128)(2,1)}, u32[]{:S(2)}) copy-start(bf16[32,256]{1,0:T(8,128)(2,1)} %ws_ref.3) | copy-start | bytes 49156
  82.8 6.9 %collective-permute-start = (bf16[128,256]{1,0:T(8,128)(2,1)S(1)}, bf16[128,256]{1,0:T(8,128)(2,1)S(1)}, u32[]{:S(2)}, u32[]{:S(2)}) collective-permute-start(bf16[128,256]{1,0:T(8,128)(2,1)S(1)} %shard_map.146), channel_id=1, source_target_pairs={{256,0},{257,1},{258,2},{259,3},{260,4},{261,5},{262,6},{263,7},{2... | collective-permute-start | bytes 196616 | tf_op jit(solution)/shard_map/ppermute | solution.py:420
  123.3 17.5 %collective-permute-start.1 = (bf16[4,16,2176]{2,1,0:T(8,128)(2,1)S(1)}, bf16[4,16,2176]{2,1,0:T(8,128)(2,1)S(1)}, u32[]{:S(2)}, u32[]{:S(2)}) collective-permute-start(bf16[4,16,2176]{2,1,0:T(8,128)(2,1)S(1)} %get-tuple-element.51), channel_id=1, source_target_pairs={{0,1},{1,0},{2,3},{3,2},{4,5},{5,4},{6,7},{7,6},{8,9},{9,8},{10,11... | collective-permute-start | bytes 835592 | tf_op jit(solution)/shard_map/ppermute | solution.py:441

commit v8 on v7

--- a/solution.py
+++ b/solution.py
@@ -261,8 +261,8 @@
     grad_ref[...] = layer_grad(cat_ref, wl_ref, ws_ref, core_ref)
 
 
-def part_kernel(micro, cat_ref, down_ref, x_ref, dpre_ref, rate_ref, ends_ref, keep_ref, give_ref, small):
-    groups, tile, _ = keep_ref.shape
+def part_kernel(micro, away, cat_ref, down_ref, x_ref, dpre_ref, rate_ref, ends_ref, out_ref, small):
+    groups, tile, _ = out_ref.shape
     cores = small.shape[0] // groups
     replicas, states = cores * groups, rate_ref.shape[0]
     channels, rank = x_ref.shape[1], cat_ref.shape[1] // 128 * 128 - 128
@@ -307,8 +307,7 @@
     for core in range(cores):
         @pl.when(mine == core)
         def _():
-            fill(keep_ref, core)
-            fill(give_ref, 1 - core)
+            fill(out_ref, 1 - core if away else core)
 
 
 def order_kernel(states, const_ref, down_ref, wl_ref, ws_ref, core_ref, grad_ref):
@@ -435,15 +434,18 @@
     lanes = own // TILE * rank + deep // TILE * channels + 128
     groups = lax.axis_size("zl")
     share_out = ((groups, TILE, lanes), BF16)
-    keep, give = call(
-        functools.partial(part_kernel, micro), [share_out, share_out], [(replicas, TILE, 128)],
+    give, = call(
+        functools.partial(part_kernel, micro, True), [share_out], [(replicas, TILE, 128)],
         cat, down_cat, x, dpre, rate_sum, end_sums)
     other = lax.ppermute(give, "core", [(0, 1), (1, 0)])
     held_cat, _ = lax.optimization_barrier((down_cat, give))
     grad, = call(
         functools.partial(order_kernel, states), [((micro, length, channels), BF16)], [],
         const, held_cat, w_low, w_select, core)
-    other, grad = lax.optimization_barrier((other, grad))
+    keep, = call(
+        functools.partial(part_kernel, micro, False), [share_out], [(replicas, TILE, 128)],
+        cat, held_cat, x, dpre, rate_sum, end_sums)
+    other, grad, keep = lax.optimization_barrier((other, grad, keep))
     pairs = (keep.astype(F32) + other.astype(F32)).astype(BF16)
     got = exchange(pairs, "zl")
     sums = call(

time: 153 us -> 153 us (level)
    pallas_call x8 -> x9, Pallas kernels: 10.8 us -> 11.1 us  [call(): pl.pallas_call(kernel, out_shape=[jax.ShapeDtypeStruct(*out) for out in o...]
  transfers between devices with their start and end apart: 2 -> 2, of which waited for: 2 -> 1; matrix products, arithmetic and copies ran while one was open for 0% -> 0% of each run, Pallas kernels for 1% -> 1%
where the time goes in v8:
time: 153 us
  blocking collectives  118 us (77%)
  starting transfers between devices  17.6 us (12%)
  Pallas kernels  11.1 us (7%)
  waiting for transfers between devices  4.78 us (3%)
    all_to_all x10, blocking collectives, exchange(): return lax.all_to_all(blocks, axes, 0, 0)  118 us
    ppermute x1, starting transfers between devices, per_device(): other = lax.ppermute(give, 'core', [(0, 1), (1, 0)])  16.3 us
    pallas_call x9, Pallas kernels, call(): pl.pallas_call(kernel, out_shape=[jax.ShapeDtypeStruct(*out) for out in o...  11.1 us
    ppermute x1, waiting for transfers between devices, per_device(): above = lax.ppermute(handed, 'ly', [(1, 0)])  4.78 us
  transfers between devices with their start and end apart: 2, of which 1 were waited for; matrix products, arithmetic and copies ran while one was open for 0% of the time, Pallas kernels for 1%

profile of v8, /device:TPU:1, one launch (start us, length us, event | category | flops | bytes accessed | tf_op | source)
XLA Modules:
  0.0 152.8 jit_solution(327325012617754471)
XLA Ops:
  0.6 1.9 %shard_map.144 = (bf16[128,640]{1,0:T(8,128)(2,1)}, f32[24,256]{1,0:T(8,128)}) custom-call(bf16[128,256]{1,0:T(8,128)(2,1)} %bitcast.19, bf16[32,256]{1,0:T(8,128)(2,1)} %ws_ref.3, bf16[256,512]{1,0:T(8,128)(2,1)} %wl_ref.3, f32[16,256]{1,0:T(8,128)} %rate_hbm.1, f32[1,256]{1,0:T(1,128)} %bitcast.30, f32[1,256]{1,0:T(1,128)} %bitcast.31, s32[4]{0:T(128)} %plan_hbm.1), custom_call_target="tpu_custom_call" | custom-call | tf_op jit(solution)/shard_map/pallas_call | solution.py:356
  2.6 11.5 %all_to_all.50 = bf16[8,16,640]{2,1,0:T(8,128)(2,1)S(1)} all-to-all(bf16[8,16,640]{2,1,0:T(8,128)(2,1)} %bitcast.29), channel_id=1, replica_groups=mesh['ly'=2,'yl'=2,'zh'=4,'x'=4,'zl'=4,'core'=2] {'yl','x'}, dimensions={0} | all-to-all | bytes 327680 | tf_op jit(solution)/shard_map/all_to_all | solution.py:367
  14.1 26.7 %all_to_all.51 = bf16[4,16,640]{2,1,0:T(8,128)(2,1)S(1)} all-to-all(bf16[4,16,640]{2,1,0:T(8,128)(2,1)S(1)} %broadcast_in_dim.12), channel_id=1, replica_groups=mesh['ly'=2,'yl'=2,'zh'=4,'x'=4,'zl'=4,'core'=2] {'zh'}, dimensions={0} | all-to-all | bytes 163840 | tf_op jit(solution)/shard_map/all_to_all | solution.py:367
  40.8 0.1 slice.16
  40.9 0.1 pad_maximum_fusion
  41.0 0.0 copy-start
  41.0 0.0 copy-start.2
  41.0 0.0 copy-start.3
  41.0 0.0 copy-start.4
  41.0 8.1 %all_to_all.52 = bf16[8,16,640]{2,1,0:T(8,128)(2,1)S(1)} all-to-all(bf16[8,16,640]{2,1,0:T(8,128)(2,1)S(1)} %broadcast_in_dim.13), channel_id=1, replica_groups=mesh['ly'=2,'yl'=2,'zh'=4,'x'=4,'zl'=4,'core'=2] {'yl','x'}, dimensions={0} | all-to-all | bytes 327680 | tf_op jit(solution)/shard_map/all_to_all | solution.py:367
  49.2 0.0 copy-done
  49.2 0.0 copy-done.2
  49.2 0.0 copy-done.3
  49.2 0.0 copy-done.4
  49.2 2.9 %shard_map.145 = (bf16[128,640]{1,0:T(8,128)(2,1)S(1)}, f32[128,256]{1,0:T(8,128)S(1)}) custom-call(bf16[128,256]{1,0:T(8,128)(2,1)S(1)} %bitcast.20, bf16[128,256]{1,0:T(8,128)(2,1)S(1)} %bitcast.25, bf16[128,640]{1,0:T(8,128)(2,1)S(1)} %bitcast.12, bf16[512,256]{1,0:T(8,128)(2,1)S(1)} %copy-done, f32[24,256]{1,0:T(8,128)S(1)} %copy-done.4), custom_call_target="tpu_custom_call" | custom-call | tf_op jit(solution)/shard_map/pallas_call | solution.py:356
  52.1 8.0 %all_to_all.53 = bf16[8,16,640]{2,1,0:T(8,128)(2,1)S(1)} all-to-all(bf16[8,16,640]{2,1,0:T(8,128)(2,1)S(1)} %bitcast.28), channel_id=1, replica_groups=mesh['ly'=2,'yl'=2,'zh'=4,'x'=4,'zl'=4,'core'=2] {'yl','x'}, dimensions={0} | all-to-all | bytes 327680 | tf_op jit(solution)/shard_map/all_to_all | solution.py:367
  60.2 14.2 %all_to_all.54 = bf16[4,16,640]{2,1,0:T(8,128)(2,1)S(1)} all-to-all(bf16[4,16,640]{2,1,0:T(8,128)(2,1)S(1)} %broadcast_in_dim.14), channel_id=1, replica_groups=mesh['ly'=2,'yl'=2,'zh'=4,'x'=4,'zl'=4,'core'=2] {'zh'}, dimensions={0} | all-to-all | bytes 163840 | tf_op jit(solution)/shard_map/all_to_all | solution.py:367
  74.3 0.0 copy-start.1
  74.4 0.0 copy-start.5
  74.4 8.1 %all_to_all.55 = bf16[8,16,640]{2,1,0:T(8,128)(2,1)S(1)} all-to-all(bf16[8,16,640]{2,1,0:T(8,128)(2,1)S(1)} %broadcast_in_dim.15), channel_id=1, replica_groups=mesh['ly'=2,'yl'=2,'zh'=4,'x'=4,'zl'=4,'core'=2] {'yl','x'}, dimensions={0} | all-to-all | bytes 327680 | tf_op jit(solution)/shard_map/all_to_all | solution.py:367
  82.5 0.0 copy-done.1
  82.5 0.0 copy-done.5
  82.5 0.2 shard_map.146
  82.8 1.3 collective-permute-start
  84.1 0.9 shard_map.147
  84.9 4.8 %collective-permute-done.above_ref = bf16[128,256]{1,0:T(8,128)(2,1)S(1)} collective-permute-done((bf16[128,256]{1,0:T(8,128)(2,1)S(1)}, bf16[128,256]{1,0:T(8,128)(2,1)S(1)}, u32[]{:S(2)}, u32[]{:S(2)}) %collective-permute-start) | collective-permute-done | bytes 65568 | tf_op jit(solution)/shard_map/ppermute | solution.py:419
  89.7 2.9 %shard_map.148 = (bf16[128,640]{1,0:T(8,128)(2,1)S(1)}, f32[128,256]{1,0:T(8,128)S(1)}, bf16[128,256]{1,0:T(8,128)(2,1)S(1)}, f32[16,8,128]{2,1,0:T(8,128)S(1)}, f32[2,8,128]{2,1,0:T(8,128)S(1)}) custom-call(bf16[512,256]{1,0:T(8,128)(2,1)S(1)} %copy-done, bf16[128,256]{1,0:T(8,128)(2,1)S(1)} %collective-permute-done.above_ref, ...), custom_call_target="tpu_custom_call" | custom-call | tf_op jit(solution)/shard_map/pallas_call | solution.py:356
  92.7 8.0 %all_to_all.56 = bf16[8,16,640]{2,1,0:T(8,128)(2,1)S(1)} all-to-all(bf16[8,16,640]{2,1,0:T(8,128)(2,1)S(1)} %bitcast.27), channel_id=1, replica_groups=mesh['ly'=2,'yl'=2,'zh'=4,'x'=4,'zl'=4,'core'=2] {'yl','x'}, dimensions={0} | all-to-all | bytes 327680 | tf_op jit(solution)/shard_map/all_to_all | solution.py:367
  100.7 14.2 %all_to_all.57 = bf16[4,16,640]{2,1,0:T(8,128)(2,1)S(1)} all-to-all(bf16[4,16,640]{2,1,0:T(8,128)(2,1)S(1)} %broadcast_in_dim.16), channel_id=1, replica_groups=mesh['ly'=2,'yl'=2,'zh'=4,'x'=4,'zl'=4,'core'=2] {'zh'}, dimensions={0} | all-to-all | bytes 163840 | tf_op jit(solution)/shard_map/all_to_all | solution.py:367
  114.9 8.0 %all_to_all.58 = bf16[8,16,640]{2,1,0:T(8,128)(2,1)S(1)} all-to-all(bf16[8,16,640]{2,1,0:T(8,128)(2,1)S(1)} %broadcast_in_dim.17), channel_id=1, replica_groups=mesh['ly'=2,'yl'=2,'zh'=4,'x'=4,'zl'=4,'core'=2] {'yl','x'}, dimensions={0} | all-to-all | bytes 327680 | tf_op jit(solution)/shard_map/all_to_all | solution.py:367
  122.9 0.3 shard_map.149
  123.3 16.3 %collective-permute-start.1 = (bf16[4,16,2176]{2,1,0:T(8,128)(2,1)S(1)}, bf16[4,16,2176]{2,1,0:T(8,128)(2,1)S(1)}, u32[]{:S(2)}, u32[]{:S(2)}) collective-permute-start(bf16[4,16,2176]{2,1,0:T(8,128)(2,1)S(1)} %shard_map.149), channel_id=1, source_target_pairs={{0,1},{1,0},{2,3},{3,2},{4,5},{5,4},{6,7},{7,6},{8,9},{9,8},{10,11... | collective-permute-start | bytes 835592 | tf_op jit(solution)/shard_map/ppermute | solution.py:440
  139.6 0.4 shard_map.151
  139.9 0.9 shard_map.150
  140.8 0.0 collective-permute-done.1
  140.8 0.1 add_convert_fusion
  140.9 11.2 %all_to_all.59.got_ref = bf16[4,16,2176]{2,1,0:T(8,128)(2,1)S(1)} all-to-all(bf16[4,16,2176]{2,1,0:T(8,128)(2,1)S(1)} %add_convert_fusion), channel_id=1, replica_groups=mesh['ly'=2,'yl'=2,'zh'=4,'x'=4,'zl'=4,'core'=2] {'zl'}, dimensions={0} | all-to-all | bytes 557056 | tf_op jit(solution)/shard_map/all_to_all | solution.py:367
  152.1 0.7 shard_map.152
  (15 shorter events, 0.2 us)
Async XLA Ops:
  41.0 8.2 %copy-start = (bf16[512,256]{1,0:T(8,128)(2,1)S(1)}, bf16[512,256]{1,0:T(8,128)(2,1)}, u32[]{:S(2)}) copy-start(bf16[512,256]{1,0:T(8,128)(2,1)} %wd_any.3) | copy-start | bytes 786436
  41.0 8.2 %copy-start.2 = (bf16[4,32,256]{2,1,0:T(8,128)(2,1)S(1)}, bf16[4,32,256]{2,1,0:T(8,128)(2,1)}, u32[]{:S(2)}) copy-start(bf16[4,32,256]{2,1,0:T(8,128)(2,1)} %param.9) | copy-start | bytes 196612
  41.0 8.2 %copy-start.3 = (bf16[4,32,256]{2,1,0:T(8,128)(2,1)S(1)}, bf16[4,32,256]{2,1,0:T(8,128)(2,1)}, u32[]{:S(2)}) copy-start(bf16[4,32,256]{2,1,0:T(8,128)(2,1)} %param.10) | copy-start | bytes 196612
  41.0 8.2 %copy-start.4 = (f32[24,256]{1,0:T(8,128)S(1)}, f32[24,256]{1,0:T(8,128)}, u32[]{:S(2)}) copy-start(f32[24,256]{1,0:T(8,128)} %get-tuple-element.35.const_ref.const_any) | copy-start | bytes 73732
  74.3 8.2 %copy-start.1 = (bf16[256,512]{1,0:T(8,128)(2,1)S(1)}, bf16[256,512]{1,0:T(8,128)(2,1)}, u32[]{:S(2)}) copy-start(bf16[256,512]{1,0:T(8,128)(2,1)} %wl_ref.3) | copy-start | bytes 786436
  74.4 8.2 %copy-start.5 = (bf16[32,256]{1,0:T(8,128)(2,1)S(1)}, bf16[32,256]{1,0:T(8,128)(2,1)}, u32[]{:S(2)}) copy-start(bf16[32,256]{1,0:T(8,128)(2,1)} %ws_ref.3) | copy-start | bytes 49156
  82.8 6.9 %collective-permute-start = (bf16[128,256]{1,0:T(8,128)(2,1)S(1)}, bf16[128,256]{1,0:T(8,128)(2,1)S(1)}, u32[]{:S(2)}, u32[]{:S(2)}) collective-permute-start(bf16[128,256]{1,0:T(8,128)(2,1)S(1)} %shard_map.146), channel_id=1, source_target_pairs={{256,0},{257,1},{258,2},{259,3},{260,4},{261,5},{262,6},{263,7},{2... | collective-permute-start | bytes 196616 | tf_op jit(solution)/shard_map/ppermute | solution.py:419
  123.3 17.6 %collective-permute-start.1 = (bf16[4,16,2176]{2,1,0:T(8,128)(2,1)S(1)}, bf16[4,16,2176]{2,1,0:T(8,128)(2,1)S(1)}, u32[]{:S(2)}, u32[]{:S(2)}) collective-permute-start(bf16[4,16,2176]{2,1,0:T(8,128)(2,1)S(1)} %shard_map.149), channel_id=1, source_target_pairs={{0,1},{1,0},{2,3},{3,2},{4,5},{5,4},{6,7},{7,6},{8,9},{9,8},{10,11... | collective-permute-start | bytes 835592 | tf_op jit(solution)/shard_map/ppermute | solution.py:440
